TPU v7x, 512 devices: a whole 4x4x16 slice. The times are simulated.
512 devices in a mesh: gx: 8 (over z_hi, core), gy: 16 (over x, z_lo), dev: 4 (over y).
Axes of the slice: x: 4, y: 4, z: 16 (z_hi: 4, z_lo: 4; z = z_hi * 4 + z_lo), core: 2. Of those that a mesh axis runs over, the one named last changes fastest.
Arguments:
- volume: bfloat16 [16, 16, 128, 4096], P(None, None, ('gx', 'dev'), 'gy'), may hold values from -6 to 6
- w_first: bfloat16 [16, 16, 3, 3, 3], replicated, may hold values from -0.4375 to 0.4375
- w_second: bfloat16 [16, 16, 3, 3, 3], replicated, may hold values from -0.4375 to 0.4375
- w_third: bfloat16 [32, 16, 3, 3, 3], replicated, may hold values from -0.4375 to 0.4375
- w_fourth: bfloat16 [32, 32, 3, 3, 3], replicated, may hold values from -0.3125 to 0.3125
Outputs:
- features: bfloat16 [32, 8, 64, 2048], P(None, 'dev', 'gx', 'gy')
All inputs are finite; a program needn't handle non-finite values.
Results may differ from a plain program's by a relative error of at most 0.0066.
Values may be sent and summed in bfloat16 or wider, within the bound.
No kernel may reach another device: no remote copies, remote signals or barrier semaphores. Data moves between devices by JAX's collectives and lax.ppermute only.
A program may use at most 64 MiB of HBM per device.

v0:
```python
import jax
import jax.numpy as jnp
from jax import lax
from jax.experimental import pallas as pl
from jax.experimental.pallas import tpu as pltpu
from jax.sharding import PartitionSpec as P

F32 = jnp.float32
BF16 = jnp.bfloat16
HALO = 16
COLS = 256
WIDE = COLS + 2 * HALO
HALF = WIDE // 2
VMEM_LIMIT = 48 * 1024 * 1024


def call(kernel, outs, scratch, flops, moved):
    return pl.pallas_call(
        kernel,
        out_shape=outs,
        scratch_shapes=scratch,
        compiler_params=pltpu.CompilerParams(vmem_limit_bytes=VMEM_LIMIT),
        cost_estimate=pl.CostEstimate(flops=flops, bytes_accessed=moved, transcendentals=0),
    )


def pack_kernel(x_ref, top, bottom, left, right, left_top, left_bottom, right_top, right_bottom, wide):
    wide[...] = x_ref[...].astype(F32)
    for r in range(4):
        image = wide[:, r, :].reshape(16, 16, COLS)
        image = jnp.transpose(image, (1, 0, 2)).reshape(256, COLS)
        image = jnp.transpose(image, (1, 0)).astype(BF16)
        first, last = image[:HALO], image[COLS - HALO :]
        left[r] = first
        right[r] = last
        half = r % 2
        if r < 2:
            top[half] = image
            left_top[half] = first
            right_top[half] = last
        else:
            bottom[half] = image
            left_bottom[half] = first
            right_bottom[half] = last


def one_hot(rows, lanes, of_lane):
    row = lax.broadcasted_iota(jnp.int32, (rows, lanes), 0)
    lane = lax.broadcasted_iota(jnp.int32, (rows, lanes), 1)
    return jnp.where(of_lane(lane) == row, 1.0, 0.0).astype(BF16)


def band(w_ref, out_ref, ins, outs, depths, lanes, o_of, z_of, tap_of):
    spread = jnp.dot(w_ref[...], one_hot(outs, lanes, o_of), preferred_element_type=F32)
    lane = lax.broadcasted_iota(jnp.int32, (ins, lanes), 1)
    z = z_of(lane)
    for zin in range(depths):
        tap = tap_of(zin, z)
        masks = [tap == a for a in range(3)]
        for b in range(3):
            for c in range(3):
                block = jnp.zeros((ins, lanes), F32)
                for a in range(3):
                    at = ((a * 3 + b) * 3 + c) * ins
                    block = jnp.where(masks[a], spread[at : at + ins], block)
                row = (b * depths + zin) * ins
                out_ref[row : row + ins, c * lanes : (c + 1) * lanes] = block.astype(BF16)


def weights_kernel(w1, w2, w3, w4, b1, b2, b3, b4):
    dev = lax.axis_index("dev")

    def same(zin, z):
        return zin - z + 1

    band(w1, b1, 16, 16, 16, 256, lambda n: n % 16, lambda n: n // 16, same)
    band(w2, b2, 16, 16, 16, 256, lambda n: n % 16, lambda n: 2 * ((n // 16) % 8) + n // 128, same)

    def shifted(zin, z):
        at = 2 * dev - 1 + z
        return jnp.where((at >= 0) & (at < 8), zin - at + 1, -1)

    band(w3, b3, 16, 32, 8, 128, lambda n: n % 32, lambda n: n // 32, shifted)
    band(w4, b4, 32, 32, 4, 128, lambda n: n // 2, lambda n: n % 2, lambda zin, z: zin - z)


def taps(rows, band_ref):
    lanes = rows[0].shape[1]
    lanes = band_ref.shape[1] // 3
    size = rows[0].shape[0]
    acc = jnp.dot(jnp.concatenate(rows, axis=1), band_ref[...], preferred_element_type=F32)
    total = pltpu.roll(acc[:, :lanes], 1, 0) + acc[:, lanes : 2 * lanes] + pltpu.roll(acc[:, 2 * lanes :], size - 1, 0)
    return jnp.maximum(total, 0.0)


def fine_kernel(top, bottom, up, down, left, right, up_left, up_right, down_left, down_right, b1, b2, pooled, x, level, wide):
    gx, dev, gy = lax.axis_index("gx"), lax.axis_index("dev"), lax.axis_index("gy")
    tile = gx * 4 + dev
    last_tile = 4 * lax.axis_size("gx") - 1
    last_gy = lax.axis_size("gy") - 1
    for r in range(2):
        for at, main, near, far in (
            (0, up[r], up_left[r], up_right[r]),
            (2, top[r], left[r], right[r]),
            (4, bottom[r], left[2 + r], right[2 + r]),
            (6, down[r], down_left[r], down_right[r]),
        ):
            x[at + r, :HALO] = near
            x[at + r, HALO : HALO + COLS] = main
            x[at + r, HALO + COLS :] = far
    for q in range(6):
        level[q] = taps([x[q], x[q + 1], x[q + 2]], b1).astype(BF16)

    @pl.when(gy == 0)
    def _():
        level[:, :HALO] = jnp.zeros((6, HALO, 256), BF16)

    @pl.when(gy == last_gy)
    def _():
        level[:, HALO + COLS :] = jnp.zeros((6, HALO, 256), BF16)

    @pl.when(tile == 0)
    def _():
        level[0] = jnp.zeros((WIDE, 256), BF16)

    @pl.when(tile == last_tile)
    def _():
        level[5] = jnp.zeros((WIDE, 256), BF16)

    col = lax.broadcasted_iota(jnp.int32, (HALF, 128), 0)
    inside = ((col >= HALO // 2) | (gy > 0)) & ((col < HALF - HALO // 2) | (gy < last_gy))
    for pair in range(2):
        two = [taps([level[q], level[q + 1], level[q + 2]], b2) for q in (2 * pair, 2 * pair + 1)]
        both = jnp.maximum(two[0], two[1])
        wide[...] = jnp.maximum(both[:, :128], both[:, 128:])
        most = jnp.maximum(wide[pl.ds(0, HALF, stride=2), :], wide[pl.ds(1, HALF, stride=2), :])
        pooled[pair] = jnp.where(inside, most, 0.0).astype(BF16)


def coarse_kernel(own, r1, r2, r3, q0, q1, q2, q3, b3, b4, out, x, level, wide):
    gx, dev, gy = lax.axis_index("gx"), lax.axis_index("dev"), lax.axis_index("gy")
    last_gx = lax.axis_size("gx") - 1
    last_gy = lax.axis_size("gy") - 1
    for k, part in enumerate((own, r1, r2, r3)):
        x[pl.ds(2 + 2 * ((dev + 4 - k) % 4), 2)] = part[...]
    for m, part in enumerate((q0, q1, q2, q3)):

        @pl.when(dev == m)
        def _():
            x[0:2] = part[...]

        @pl.when(dev == 3 - m)
        def _():
            x[10:12] = part[...]

    col = lax.broadcasted_iota(jnp.int32, (HALF, 128), 0)
    inside = ((col >= HALO // 2) | (gy > 0)) & ((col < HALF - HALO // 2) | (gy < last_gy))
    for q in range(10):
        keep = inside
        if q == 0:
            keep = keep & (gx > 0)
        if q == 9:
            keep = keep & (gx < last_gx)
        level[q] = jnp.where(keep, taps([x[q], x[q + 1], x[q + 2]], b3), 0.0).astype(BF16)
    for q in range(8):
        features = taps([level[q], level[q + 1], level[q + 2]], b4)
        turned = jnp.transpose(features[HALO // 2 : HALO // 2 + 128], (1, 0))
        wide[pl.ds(q, 64, stride=8), :] = turned[:64]
    out[...] = wide[...].astype(BF16)


def shift(cells, row_step, col_step):
    groups, col_tiles, devs = (lax.axis_size(axis) for axis in ("gx", "gy", "dev"))
    pairs = []
    for g in range(groups):
        for t in range(col_tiles):
            for d in range(devs):
                tile, col_tile = g * devs + d + row_step, t + col_step
                if 0 <= tile < groups * devs and 0 <= col_tile < col_tiles:
                    target = ((tile // devs) * col_tiles + col_tile) * devs + tile % devs
                    pairs.append(((g * col_tiles + t) * devs + d, target))
    return lax.ppermute(cells, ("gx", "gy", "dev"), pairs)


def body(volume, w_first, w_second, w_third, w_fourth):
    groups, devs = lax.axis_size("gx"), lax.axis_size("dev")
    sds = jax.ShapeDtypeStruct
    x = volume.reshape(256, 4, COLS)
    ends = sds((4, HALO, 256), BF16)
    corner = sds((2, HALO, 256), BF16)
    main = sds((2, COLS, 256), BF16)
    top, bottom, left, right, left_top, left_bottom, right_top, right_bottom = call(
        pack_kernel, [main, main, ends, ends, corner, corner, corner, corner], [pltpu.VMEM((256, 4, COLS), F32)], 0, 1 << 20
    )(x)

    rows = ("gx", "dev")
    up = shift(bottom, 1, 0)
    down = shift(top, -1, 0)
    from_left = shift(right, 0, 1)
    from_right = shift(left, 0, -1)
    up_left = shift(right_bottom, 1, 1)
    up_right = shift(left_bottom, 1, -1)
    down_left = shift(right_top, -1, 1)
    down_right = shift(left_top, -1, -1)

    def by_tap(weight):
        return jnp.transpose(weight, (2, 3, 4, 1, 0)).reshape(27 * weight.shape[1], weight.shape[0])

    b1, b2, b3, b4 = call(
        weights_kernel,
        [sds((768, 768), BF16), sds((768, 768), BF16), sds((384, 384), BF16), sds((384, 384), BF16)],
        [],
        0,
        3 << 20,
    )(by_tap(w_first), by_tap(w_second), by_tap(w_third), by_tap(w_fourth))

    pooled = call(
        fine_kernel,
        sds((2, HALF, 128), BF16),
        [pltpu.VMEM((8, WIDE, 256), BF16), pltpu.VMEM((6, WIDE, 256), BF16), pltpu.VMEM((WIDE, 128), F32)],
        2 * 10 * WIDE * 768 * 768,
        5 << 20,
    )(top, bottom, up, down, from_left, from_right, up_left, up_right, down_left, down_right, b1, b2)

    spread = [lax.ppermute(pooled, "dev", [(i, (i + k) % devs) for i in range(devs)]) for k in (1, 2, 3)]
    edge = []
    for m in range(4):
        pairs = [(g * devs + 3, (g + 1) * devs + m) for g in range(groups - 1)]
        pairs += [(g * devs, (g - 1) * devs + 3 - m) for g in range(1, groups)]
        edge.append(lax.ppermute(pooled, rows, pairs))

    out = call(
        coarse_kernel,
        sds((512, 128), BF16),
        [pltpu.VMEM((12, HALF, 128), BF16), pltpu.VMEM((10, HALF, 128), BF16), pltpu.VMEM((512, 128), F32)],
        2 * 18 * HALF * 384 * 384,
        2 << 20,
    )(pooled, *spread, *edge, b3, b4)
    return out.reshape(32, 2, 8, 128)


def solution(mesh):
    return jax.shard_map(
        body,
        mesh=mesh,
        in_specs=(P(None, None, ("gx", "dev"), "gy"), P(), P(), P(), P()),
        out_specs=P(None, "dev", "gx", "gy"),
        check_vma=False,
    )
```

profile of v0, /device:TPU:450, one launch (start us, length us, event | category | flops | bytes accessed | tf_op | source)
XLA Modules:
  0.0 80.2 jit_solution(4930114643217571418)
XLA Ops:
  0.0 1.0 %copy-done = bf16[16,16,4,256]{3,2,1,0:T(4,128)(2,1)S(1)} copy-done((bf16[16,16,4,256]{3,2,1,0:T(4,128)(2,1)S(1)}, bf16[16,16,4,256]{3,2,1,0:T(4,128)(2,1)}, u32[]{:S(2)}) %copy-start) | copy-done | bytes 524312
  1.6 7.3 %collective-permute-start.1 = (bf16[2,256,256]{2,1,0:T(8,128)(2,1)S(1)}, bf16[2,256,256]{2,1,0:T(8,128)(2,1)S(1)}, u32[]{:S(2)}, u32[]{:S(2)}) collective-permute-start(bf16[2,256,256]{2,1,0:T(8,128)(2,1)S(1)} %get-tuple-element.17.top), channel_id=1, source_target_pairs={{1,0},{2,1},{3,2},{5,4},{6,5},{7,6},{9,8},{10,9},{11,10},{13,12},{... | collective-permute-start | bytes 786440 | tf_op jit(solution)/shard_map/ppermute | solution.py:182
  9.0 1.9 %collective-permute-start = (bf16[2,256,256]{2,1,0:T(8,128)(2,1)S(1)}, bf16[2,256,256]{2,1,0:T(8,128)(2,1)S(1)}, u32[]{:S(2)}, u32[]{:S(2)}) collective-permute-start(bf16[2,256,256]{2,1,0:T(8,128)(2,1)S(1)} %get-tuple-element.18.bottom), channel_id=1, source_target_pairs={{0,1},{1,2},{2,3},{3,64},{4,5},{5,6},{6,7},{7,68},{8,9},{9,10},{10... | collective-permute-start | bytes 786440 | tf_op jit(solution)/shard_map/ppermute | solution.py:182
  10.9 1.9 %collective-permute-start.4 = (bf16[2,16,256]{2,1,0:T(8,128)(2,1)S(1)}, bf16[2,16,256]{2,1,0:T(8,128)(2,1)S(1)}, u32[]{:S(2)}, u32[]{:S(2)}) collective-permute-start(bf16[2,16,256]{2,1,0:T(8,128)(2,1)S(1)} %get-tuple-element.21), channel_id=1, source_target_pairs={{0,5},{1,6},{2,7},{3,68},{4,9},{5,10},{6,11},{7,72},{8,13},{9,14},... | collective-permute-start | bytes 49160 | tf_op jit(solution)/shard_map/ppermute | solution.py:182
  12.8 2.5 %collective-permute-start.5 = (bf16[2,16,256]{2,1,0:T(8,128)(2,1)S(1)}, bf16[2,16,256]{2,1,0:T(8,128)(2,1)S(1)}, u32[]{:S(2)}, u32[]{:S(2)}) collective-permute-start(bf16[2,16,256]{2,1,0:T(8,128)(2,1)S(1)} %get-tuple-element.22), channel_id=1, source_target_pairs={{4,1},{5,2},{6,3},{7,64},{8,5},{9,6},{10,7},{11,68},{12,9},{13,10}... | collective-permute-start | bytes 49160 | tf_op jit(solution)/shard_map/ppermute | solution.py:182
  15.4 8.6 %collective-permute-start.6 = (bf16[2,16,256]{2,1,0:T(8,128)(2,1)S(1)}, bf16[2,16,256]{2,1,0:T(8,128)(2,1)S(1)}, u32[]{:S(2)}, u32[]{:S(2)}) collective-permute-start(bf16[2,16,256]{2,1,0:T(8,128)(2,1)S(1)} %get-tuple-element.23), channel_id=1, source_target_pairs={{1,4},{2,5},{3,6},{5,8},{6,9},{7,10},{9,12},{10,13},{11,14},{13,16... | collective-permute-start | bytes 49160 | tf_op jit(solution)/shard_map/ppermute | solution.py:182
  24.0 6.0 %collective-permute-done.4.up_left = bf16[2,16,256]{2,1,0:T(8,128)(2,1)S(1)} collective-permute-done((bf16[2,16,256]{2,1,0:T(8,128)(2,1)S(1)}, bf16[2,16,256]{2,1,0:T(8,128)(2,1)S(1)}, u32[]{:S(2)}, u32[]{:S(2)}) %collective-permute-start.4) | collective-permute-done | bytes 16416 | tf_op jit(solution)/shard_map/ppermute | solution.py:182
  30.0 1.9 %collective-permute-start.2 = (bf16[4,16,256]{2,1,0:T(8,128)(2,1)S(1)}, bf16[4,16,256]{2,1,0:T(8,128)(2,1)S(1)}, u32[]{:S(2)}, u32[]{:S(2)}) collective-permute-start(bf16[4,16,256]{2,1,0:T(8,128)(2,1)S(1)} %get-tuple-element.19), channel_id=1, source_target_pairs={{0,4},{1,5},{2,6},{3,7},{4,8},{5,9},{6,10},{7,11},{8,12},{9,13},{1... | collective-permute-start | bytes 98312 | tf_op jit(solution)/shard_map/ppermute | solution.py:182
  31.9 6.3 %collective-permute-start.3 = (bf16[4,16,256]{2,1,0:T(8,128)(2,1)S(1)}, bf16[4,16,256]{2,1,0:T(8,128)(2,1)S(1)}, u32[]{:S(2)}, u32[]{:S(2)}) collective-permute-start(bf16[4,16,256]{2,1,0:T(8,128)(2,1)S(1)} %get-tuple-element.20), channel_id=1, source_target_pairs={{4,0},{5,1},{6,2},{7,3},{8,4},{9,5},{10,6},{11,7},{12,8},{13,9},{1... | collective-permute-start | bytes 98312 | tf_op jit(solution)/shard_map/ppermute | solution.py:182
  38.2 1.9 %collective-permute-start.7 = (bf16[2,16,256]{2,1,0:T(8,128)(2,1)S(1)}, bf16[2,16,256]{2,1,0:T(8,128)(2,1)S(1)}, u32[]{:S(2)}, u32[]{:S(2)}) collective-permute-start(bf16[2,16,256]{2,1,0:T(8,128)(2,1)S(1)} %get-tuple-element.24), channel_id=1, source_target_pairs={{5,0},{6,1},{7,2},{9,4},{10,5},{11,6},{13,8},{14,9},{15,10},{17,12... | collective-permute-start | bytes 49160 | tf_op jit(solution)/shard_map/ppermute | solution.py:182
  40.1 1.0 %copy.6 = bf16[3,3,3,16,16]{4,3,2,1,0:T(8,128)(2,1)S(1)} copy(bf16[3,3,3,16,16]{3,4,2,1,0:T(8,128)(2,1)} %bitcast.17) | data formatting | bytes 27648 | tf_op jit(solution)/shard_map/transpose | solution.py:207
  42.1 1.1 %copy.8 = bf16[3,3,3,32,32]{4,3,2,1,0:T(8,128)(2,1)S(1)} copy(bf16[3,3,3,32,32]{3,4,2,1,0:T(8,128)(2,1)} %bitcast.16) | data formatting | bytes 110592 | tf_op jit(solution)/shard_map/transpose | solution.py:207
  43.2 1.5 %shard_map.56 = (bf16[768,768]{1,0:T(8,128)(2,1)S(1)}, bf16[768,768]{1,0:T(8,128)(2,1)S(1)}, bf16[384,384]{1,0:T(8,128)(2,1)S(1)}, bf16[384,384]{1,0:T(8,128)(2,1)S(1)}) custom-call(bf16[432,16]{1,0:T(8,128)(2,1)S(1)} %bitcast.13, bf16[432,16]{1,0:T(8,128)(2,1)S(1)} %bitcast.14, bf16[432,32]{1,0:T(8,128)(2,1)S(1)} %bitcast.15, bf16[864,32]{1,0:T(8,128)(2,1)S(1)} %bitcast.11), custom_call_target="tpu_custom_call" | custom-call | bytes 3145728 | tf_op jit(solution)/shard_map/pallas_call | solution.py:209
  44.8 3.9 %shard_map.57.own = bf16[2,144,128]{2,1,0:T(8,128)(2,1)S(1)} custom-call(bf16[2,256,256]{2,1,0:T(8,128)(2,1)S(1)} %get-tuple-element.17.top, bf16[2,256,256]{2,1,0:T(8,128)(2,1)S(1)} %get-tuple-element.18.bottom, bf16[2,256,256]{2,1,0:T(8,128)(2,1)S(1)} %collective-permute-done.up, bf16[2,256,256]{2,1,0:T(8,128)(2,1)S(1)} %collective-permute-done.1.down, ...), custom_call_target="tpu_custom_call" | custom-call | flops 3397386240 | bytes 5242880 | tf_op jit(solution)/shard_map/pallas_call | solution.py:217
  48.7 1.9 %collective-permute-start.14 = (bf16[2,144,128]{2,1,0:T(8,128)(2,1)S(1)}, bf16[2,144,128]{2,1,0:T(8,128)(2,1)S(1)}, u32[]{:S(2)}, u32[]{:S(2)}) collective-permute-start(bf16[2,144,128]{2,1,0:T(8,128)(2,1)S(1)} %shard_map.57.own), channel_id=1, source_target_pairs={{3,67},{67,131},{131,195},{195,259},{259,323},{323,387},{387,451},... | collective-permute-start | bytes 221192 | tf_op jit(solution)/shard_map/ppermute | solution.py:230
  50.6 1.3 %collective-permute-start.13 = (bf16[2,144,128]{2,1,0:T(8,128)(2,1)S(1)}, bf16[2,144,128]{2,1,0:T(8,128)(2,1)S(1)}, u32[]{:S(2)}, u32[]{:S(2)}) collective-permute-start(bf16[2,144,128]{2,1,0:T(8,128)(2,1)S(1)} %shard_map.57.own), channel_id=1, source_target_pairs={{3,66},{67,130},{131,194},{195,258},{259,322},{323,386},{387,450},... | collective-permute-start | bytes 221192 | tf_op jit(solution)/shard_map/ppermute | solution.py:230
  51.9 1.3 %collective-permute-start.12 = (bf16[2,144,128]{2,1,0:T(8,128)(2,1)S(1)}, bf16[2,144,128]{2,1,0:T(8,128)(2,1)S(1)}, u32[]{:S(2)}, u32[]{:S(2)}) collective-permute-start(bf16[2,144,128]{2,1,0:T(8,128)(2,1)S(1)} %shard_map.57.own), channel_id=1, source_target_pairs={{3,65},{67,129},{131,193},{195,257},{259,321},{323,385},{387,449},... | collective-permute-start | bytes 221192 | tf_op jit(solution)/shard_map/ppermute | solution.py:230
  53.2 11.9 %collective-permute-start.11 = (bf16[2,144,128]{2,1,0:T(8,128)(2,1)S(1)}, bf16[2,144,128]{2,1,0:T(8,128)(2,1)S(1)}, u32[]{:S(2)}, u32[]{:S(2)}) collective-permute-start(bf16[2,144,128]{2,1,0:T(8,128)(2,1)S(1)} %shard_map.57.own), channel_id=1, source_target_pairs={{3,64},{67,128},{131,192},{195,256},{259,320},{323,384},{387,448},... | collective-permute-start | bytes 221192 | tf_op jit(solution)/shard_map/ppermute | solution.py:230
  65.1 1.9 %collective-permute-start.10 = (bf16[2,144,128]{2,1,0:T(8,128)(2,1)S(1)}, bf16[2,144,128]{2,1,0:T(8,128)(2,1)S(1)}, u32[]{:S(2)}, u32[]{:S(2)}) collective-permute-start(bf16[2,144,128]{2,1,0:T(8,128)(2,1)S(1)} %shard_map.57.own), channel_id=1, source_target_pairs={{0,3},{1,0},{2,1},{3,2},{4,7},{5,4},{6,5},{7,6},{8,11},{9,8},{10,9... | collective-permute-start | bytes 221192 | tf_op jit(solution)/shard_map/ppermute | solution.py:225
  67.1 1.9 %collective-permute-start.9 = (bf16[2,144,128]{2,1,0:T(8,128)(2,1)S(1)}, bf16[2,144,128]{2,1,0:T(8,128)(2,1)S(1)}, u32[]{:S(2)}, u32[]{:S(2)}) collective-permute-start(bf16[2,144,128]{2,1,0:T(8,128)(2,1)S(1)} %shard_map.57.own), channel_id=1, source_target_pairs={{0,2},{1,3},{2,0},{3,1},{4,6},{5,7},{6,4},{7,5},{8,10},{9,11},{10,... | collective-permute-start | bytes 221192 | tf_op jit(solution)/shard_map/ppermute | solution.py:225
  69.0 3.9 %collective-permute-start.8 = (bf16[2,144,128]{2,1,0:T(8,128)(2,1)S(1)}, bf16[2,144,128]{2,1,0:T(8,128)(2,1)S(1)}, u32[]{:S(2)}, u32[]{:S(2)}) collective-permute-start(bf16[2,144,128]{2,1,0:T(8,128)(2,1)S(1)} %shard_map.57.own), channel_id=1, source_target_pairs={{0,1},{1,2},{2,3},{3,0},{4,5},{5,6},{6,7},{7,4},{8,9},{9,10},{10,1... | collective-permute-start | bytes 221192 | tf_op jit(solution)/shard_map/ppermute | solution.py:225
  73.0 1.9 %collective-permute-done.9.r2 = bf16[2,144,128]{2,1,0:T(8,128)(2,1)S(1)} collective-permute-done((bf16[2,144,128]{2,1,0:T(8,128)(2,1)S(1)}, bf16[2,144,128]{2,1,0:T(8,128)(2,1)S(1)}, u32[]{:S(2)}, u32[]{:S(2)}) %collective-permute-start.9) | collective-permute-done | bytes 73760 | tf_op jit(solution)/shard_map/ppermute | solution.py:225
  74.8 3.1 %collective-permute-done.8.r1 = bf16[2,144,128]{2,1,0:T(8,128)(2,1)S(1)} collective-permute-done((bf16[2,144,128]{2,1,0:T(8,128)(2,1)S(1)}, bf16[2,144,128]{2,1,0:T(8,128)(2,1)S(1)}, u32[]{:S(2)}, u32[]{:S(2)}) %collective-permute-start.8) | collective-permute-done | bytes 73760 | tf_op jit(solution)/shard_map/ppermute | solution.py:225
  77.9 2.3 %shard_map.58 = bf16[512,128]{1,0:T(8,128)(2,1)} custom-call(bf16[2,144,128]{2,1,0:T(8,128)(2,1)S(1)} %shard_map.57.own, bf16[2,144,128]{2,1,0:T(8,128)(2,1)S(1)} %collective-permute-done.8.r1, bf16[2,144,128]{2,1,0:T(8,128)(2,1)S(1)} %collective-permute-done.9.r2, bf16[2,144,128]{2,1,0:T(8,128)(2,1)S(1)} %collective-permute-done.10.r3, ...), custom_call_target="tpu_custom_call" | custom-call | flops 764411904 | bytes 2097152 | tf_op jit(solution)/shard_map/pallas_call | solution.py:232
  (17 shorter events, 1.6 us)
Async XLA Ops:
  0.0 1.0 %copy-start = (bf16[16,16,4,256]{3,2,1,0:T(4,128)(2,1)S(1)}, bf16[16,16,4,256]{3,2,1,0:T(4,128)(2,1)}, u32[]{:S(2)}) copy-start(bf16[16,16,4,256]{3,2,1,0:T(4,128)(2,1)} %param.5) | copy-start | bytes 1572868
  1.0 42.2 %copy-start.1 = (bf16[32,16,3,3,3]{0,1,4,3,2:T(8,128)(2,1)S(1)}, bf16[32,16,3,3,3]{0,1,4,3,2:T(8,128)(2,1)}, u32[]{:S(2)}) copy-start(bf16[32,16,3,3,3]{0,1,4,3,2:T(8,128)(2,1)} %param.8) | copy-start | bytes 82948
  1.6 43.1 %collective-permute-start.1 = (bf16[2,256,256]{2,1,0:T(8,128)(2,1)S(1)}, bf16[2,256,256]{2,1,0:T(8,128)(2,1)S(1)}, u32[]{:S(2)}, u32[]{:S(2)}) collective-permute-start(bf16[2,256,256]{2,1,0:T(8,128)(2,1)S(1)} %get-tuple-element.17.top), channel_id=1, source_target_pairs={{1,0},{2,1},{3,2},{5,4},{6,5},{7,6},{9,8},{10,9},{11,10},{13,12},{... | collective-permute-start | bytes 786440 | tf_op jit(solution)/shard_map/ppermute | solution.py:182
  9.0 35.8 %collective-permute-start = (bf16[2,256,256]{2,1,0:T(8,128)(2,1)S(1)}, bf16[2,256,256]{2,1,0:T(8,128)(2,1)S(1)}, u32[]{:S(2)}, u32[]{:S(2)}) collective-permute-start(bf16[2,256,256]{2,1,0:T(8,128)(2,1)S(1)} %get-tuple-element.18.bottom), channel_id=1, source_target_pairs={{0,1},{1,2},{2,3},{3,64},{4,5},{5,6},{6,7},{7,68},{8,9},{9,10},{10... | collective-permute-start | bytes 786440 | tf_op jit(solution)/shard_map/ppermute | solution.py:182
  10.9 19.0 %collective-permute-start.4 = (bf16[2,16,256]{2,1,0:T(8,128)(2,1)S(1)}, bf16[2,16,256]{2,1,0:T(8,128)(2,1)S(1)}, u32[]{:S(2)}, u32[]{:S(2)}) collective-permute-start(bf16[2,16,256]{2,1,0:T(8,128)(2,1)S(1)} %get-tuple-element.21), channel_id=1, source_target_pairs={{0,5},{1,6},{2,7},{3,68},{4,9},{5,10},{6,11},{7,72},{8,13},{9,14},... | collective-permute-start | bytes 49160 | tf_op jit(solution)/shard_map/ppermute | solution.py:182
  12.8 19.0 %collective-permute-start.5 = (bf16[2,16,256]{2,1,0:T(8,128)(2,1)S(1)}, bf16[2,16,256]{2,1,0:T(8,128)(2,1)S(1)}, u32[]{:S(2)}, u32[]{:S(2)}) collective-permute-start(bf16[2,16,256]{2,1,0:T(8,128)(2,1)S(1)} %get-tuple-element.22), channel_id=1, source_target_pairs={{4,1},{5,2},{6,3},{7,64},{8,5},{9,6},{10,7},{11,68},{12,9},{13,10}... | collective-permute-start | bytes 49160 | tf_op jit(solution)/shard_map/ppermute | solution.py:182
  15.4 22.8 %collective-permute-start.6 = (bf16[2,16,256]{2,1,0:T(8,128)(2,1)S(1)}, bf16[2,16,256]{2,1,0:T(8,128)(2,1)S(1)}, u32[]{:S(2)}, u32[]{:S(2)}) collective-permute-start(bf16[2,16,256]{2,1,0:T(8,128)(2,1)S(1)} %get-tuple-element.23), channel_id=1, source_target_pairs={{1,4},{2,5},{3,6},{5,8},{6,9},{7,10},{9,12},{10,13},{11,14},{13,16... | collective-permute-start | bytes 49160 | tf_op jit(solution)/shard_map/ppermute | solution.py:182
  30.0 14.8 %collective-permute-start.2 = (bf16[4,16,256]{2,1,0:T(8,128)(2,1)S(1)}, bf16[4,16,256]{2,1,0:T(8,128)(2,1)S(1)}, u32[]{:S(2)}, u32[]{:S(2)}) collective-permute-start(bf16[4,16,256]{2,1,0:T(8,128)(2,1)S(1)} %get-tuple-element.19), channel_id=1, source_target_pairs={{0,4},{1,5},{2,6},{3,7},{4,8},{5,9},{6,10},{7,11},{8,12},{9,13},{1... | collective-permute-start | bytes 98312 | tf_op jit(solution)/shard_map/ppermute | solution.py:182
  31.9 12.9 %collective-permute-start.3 = (bf16[4,16,256]{2,1,0:T(8,128)(2,1)S(1)}, bf16[4,16,256]{2,1,0:T(8,128)(2,1)S(1)}, u32[]{:S(2)}, u32[]{:S(2)}) collective-permute-start(bf16[4,16,256]{2,1,0:T(8,128)(2,1)S(1)} %get-tuple-element.20), channel_id=1, source_target_pairs={{4,0},{5,1},{6,2},{7,3},{8,4},{9,5},{10,6},{11,7},{12,8},{13,9},{1... | collective-permute-start | bytes 98312 | tf_op jit(solution)/shard_map/ppermute | solution.py:182
  38.2 6.5 %collective-permute-start.7 = (bf16[2,16,256]{2,1,0:T(8,128)(2,1)S(1)}, bf16[2,16,256]{2,1,0:T(8,128)(2,1)S(1)}, u32[]{:S(2)}, u32[]{:S(2)}) collective-permute-start(bf16[2,16,256]{2,1,0:T(8,128)(2,1)S(1)} %get-tuple-element.24), channel_id=1, source_target_pairs={{5,0},{6,1},{7,2},{9,4},{10,5},{11,6},{13,8},{14,9},{15,10},{17,12... | collective-permute-start | bytes 49160 | tf_op jit(solution)/shard_map/ppermute | solution.py:182
  48.7 18.4 %collective-permute-start.14 = (bf16[2,144,128]{2,1,0:T(8,128)(2,1)S(1)}, bf16[2,144,128]{2,1,0:T(8,128)(2,1)S(1)}, u32[]{:S(2)}, u32[]{:S(2)}) collective-permute-start(bf16[2,144,128]{2,1,0:T(8,128)(2,1)S(1)} %shard_map.57.own), channel_id=1, source_target_pairs={{3,67},{67,131},{131,195},{195,259},{259,323},{323,387},{387,451},... | collective-permute-start | bytes 221192 | tf_op jit(solution)/shard_map/ppermute | solution.py:230
  50.6 18.4 %collective-permute-start.13 = (bf16[2,144,128]{2,1,0:T(8,128)(2,1)S(1)}, bf16[2,144,128]{2,1,0:T(8,128)(2,1)S(1)}, u32[]{:S(2)}, u32[]{:S(2)}) collective-permute-start(bf16[2,144,128]{2,1,0:T(8,128)(2,1)S(1)} %shard_map.57.own), channel_id=1, source_target_pairs={{3,66},{67,130},{131,194},{195,258},{259,322},{323,386},{387,450},... | collective-permute-start | bytes 221192 | tf_op jit(solution)/shard_map/ppermute | solution.py:230
  51.9 21.0 %collective-permute-start.12 = (bf16[2,144,128]{2,1,0:T(8,128)(2,1)S(1)}, bf16[2,144,128]{2,1,0:T(8,128)(2,1)S(1)}, u32[]{:S(2)}, u32[]{:S(2)}) collective-permute-start(bf16[2,144,128]{2,1,0:T(8,128)(2,1)S(1)} %shard_map.57.own), channel_id=1, source_target_pairs={{3,65},{67,129},{131,193},{195,257},{259,321},{323,385},{387,449},... | collective-permute-start | bytes 221192 | tf_op jit(solution)/shard_map/ppermute | solution.py:230
  53.2 19.8 %collective-permute-start.11 = (bf16[2,144,128]{2,1,0:T(8,128)(2,1)S(1)}, bf16[2,144,128]{2,1,0:T(8,128)(2,1)S(1)}, u32[]{:S(2)}, u32[]{:S(2)}) collective-permute-start(bf16[2,144,128]{2,1,0:T(8,128)(2,1)S(1)} %shard_map.57.own), channel_id=1, source_target_pairs={{3,64},{67,128},{131,192},{195,256},{259,320},{323,384},{387,448},... | collective-permute-start | bytes 221192 | tf_op jit(solution)/shard_map/ppermute | solution.py:230
  65.1 7.8 %collective-permute-start.10 = (bf16[2,144,128]{2,1,0:T(8,128)(2,1)S(1)}, bf16[2,144,128]{2,1,0:T(8,128)(2,1)S(1)}, u32[]{:S(2)}, u32[]{:S(2)}) collective-permute-start(bf16[2,144,128]{2,1,0:T(8,128)(2,1)S(1)} %shard_map.57.own), channel_id=1, source_target_pairs={{0,3},{1,0},{2,1},{3,2},{4,7},{5,4},{6,5},{7,6},{8,11},{9,8},{10,9... | collective-permute-start | bytes 221192 | tf_op jit(solution)/shard_map/ppermute | solution.py:225
  67.1 7.8 %collective-permute-start.9 = (bf16[2,144,128]{2,1,0:T(8,128)(2,1)S(1)}, bf16[2,144,128]{2,1,0:T(8,128)(2,1)S(1)}, u32[]{:S(2)}, u32[]{:S(2)}) collective-permute-start(bf16[2,144,128]{2,1,0:T(8,128)(2,1)S(1)} %shard_map.57.own), channel_id=1, source_target_pairs={{0,2},{1,3},{2,0},{3,1},{4,6},{5,7},{6,4},{7,5},{8,10},{9,11},{10,... | collective-permute-start | bytes 221192 | tf_op jit(solution)/shard_map/ppermute | solution.py:225
  69.0 8.9 %collective-permute-start.8 = (bf16[2,144,128]{2,1,0:T(8,128)(2,1)S(1)}, bf16[2,144,128]{2,1,0:T(8,128)(2,1)S(1)}, u32[]{:S(2)}, u32[]{:S(2)}) collective-permute-start(bf16[2,144,128]{2,1,0:T(8,128)(2,1)S(1)} %shard_map.57.own), channel_id=1, source_target_pairs={{0,1},{1,2},{2,3},{3,0},{4,5},{5,6},{6,7},{7,4},{8,9},{9,10},{10,1... | collective-permute-start | bytes 221192 | tf_op jit(solution)/shard_map/ppermute | solution.py:225
where the time goes:
time: 80.8 us; the launch traced here: 80.2 us
  starting transfers between devices  56.6 us (70%)
  waiting for transfers between devices  10.9 us (13%)
  Pallas kernels  8.27 us (10%)
  local copies, waits for them, and re-layouts  4.15 us (5%)
    ppermute x8, starting transfers between devices, shift(): return lax.ppermute(cells, ('gx', 'gy', 'dev'), pairs)  32.4 us
    ppermute x4, starting transfers between devices, body(): edge.append(lax.ppermute(pooled, rows, pairs))  16.4 us
    ppermute x3, starting transfers between devices, body(): lax.ppermute(pooled, 'dev', [(i, (i + k) % devs) for i in range(devs)])  7.76 us
    ppermute x8, waiting for transfers between devices, shift(): return lax.ppermute(cells, ('gx', 'gy', 'dev'), pairs)  5.97 us
    ppermute x3, waiting for transfers between devices, body(): lax.ppermute(pooled, 'dev', [(i, (i + k) % devs) for i in range(devs)])  4.95 us
    pallas_call x1, Pallas kernels, body(): call(fine_kernel, sds((2, HALF, 128), BF16), [pltpu.VMEM((8, WIDE, 256),...  3.88 us
    transpose x3, local copies, waits for them, and re-layouts, by_tap(): jnp.transpose(weight, (2, 3, 4, 1, 0))  3.1 us
    pallas_call x1, Pallas kernels, body(): call(coarse_kernel, sds((512, 128), BF16), [pltpu.VMEM((12, HALF, 128), B...  2.34 us
  transfers between devices with their start and end apart: 15, of which 3 were waited for; matrix products, arithmetic and copies ran while one was open for 4% of the time, Pallas kernels for 2%

commit v1 on v0

v1 whole, which is shorter than its diff:
```python
import jax
import jax.numpy as jnp
from jax import lax
from jax.experimental import pallas as pl
from jax.experimental.pallas import tpu as pltpu
from jax.sharding import PartitionSpec as P

F32 = jnp.float32
BF16 = jnp.bfloat16
HALO = 16
COLS = 256
WIDE = COLS + 2 * HALO
HALF = WIDE // 2
VMEM_LIMIT = 48 * 1024 * 1024


def call(kernel, outs, scratch, flops, moved):
    return pl.pallas_call(
        kernel,
        out_shape=outs,
        scratch_shapes=scratch,
        compiler_params=pltpu.CompilerParams(vmem_limit_bytes=VMEM_LIMIT),
        cost_estimate=pl.CostEstimate(flops=flops, bytes_accessed=moved, transcendentals=0),
    )


def pack_kernel(x_ref, top, bottom, left, right, wide):
    wide[...] = x_ref[...].astype(F32)
    for r in range(4):
        image = wide[:, r, :].reshape(16, 16, COLS)
        image = jnp.transpose(image, (1, 0, 2)).reshape(256, COLS)
        image = jnp.transpose(image, (1, 0)).astype(BF16)
        left[r] = image[:HALO]
        right[r] = image[COLS - HALO :]
        half = top if r < 2 else bottom
        half[r % 2] = image


def join_kernel(top, bottom, left, right, top_wide, bottom_wide):
    for at, main, wide in ((0, top, top_wide), (2, bottom, bottom_wide)):
        for r in range(2):
            wide[r, :HALO] = left[at + r]
            wide[r, HALO : HALO + COLS] = main[r]
            wide[r, HALO + COLS :] = right[at + r]


def one_hot(rows, lanes, of_lane):
    row = lax.broadcasted_iota(jnp.int32, (rows, lanes), 0)
    lane = lax.broadcasted_iota(jnp.int32, (rows, lanes), 1)
    return jnp.where(of_lane(lane) == row, 1.0, 0.0).astype(BF16)


def band(w_ref, out_ref, ins, outs, depths, lanes, o_of, z_of, tap_of):
    spread = jnp.dot(w_ref[...], one_hot(outs, lanes, o_of), preferred_element_type=F32)
    lane = lax.broadcasted_iota(jnp.int32, (ins, lanes), 1)
    z = z_of(lane)
    for zin in range(depths):
        tap = tap_of(zin, z)
        masks = [tap == a for a in range(3)]
        for b in range(3):
            for c in range(3):
                block = jnp.zeros((ins, lanes), F32)
                for a in range(3):
                    at = ((a * 3 + b) * 3 + c) * ins
                    block = jnp.where(masks[a], spread[at : at + ins], block)
                row = (b * depths + zin) * ins
                out_ref[row : row + ins, c * lanes : (c + 1) * lanes] = block.astype(BF16)


def weights_kernel(w1, w2, w3, w4, b1, b2, b3, b4):
    def same(zin, z):
        return zin - z + 1

    band(w1, b1, 16, 16, 16, 256, lambda n: n % 16, lambda n: n // 16, same)
    band(w2, b2, 16, 16, 16, 256, lambda n: n % 16, lambda n: 2 * ((n // 16) % 8) + n // 128, same)

    band(w3, b3, 16, 32, 8, 256, lambda n: n % 32, lambda n: n // 32, same)
    band(w4, b4, 32, 32, 8, 256, lambda n: (n % 64) // 2, lambda n: 2 * (n // 64) + n % 2, same)


def taps(rows, band_ref):
    lanes = band_ref.shape[1] // 3
    size = rows[0].shape[0]
    acc = jnp.dot(jnp.concatenate(rows, axis=1), band_ref[...], preferred_element_type=F32)
    total = pltpu.roll(acc[:, :lanes], 1, 0) + acc[:, lanes : 2 * lanes] + pltpu.roll(acc[:, 2 * lanes :], size - 1, 0)
    return jnp.maximum(total, 0.0)


def place():
    tile = lax.axis_index("gx") * lax.axis_size("dev") + lax.axis_index("dev")
    gy = lax.axis_index("gy")
    last_tile = lax.axis_size("gx") * lax.axis_size("dev") - 1
    return tile, last_tile, gy, lax.axis_size("gy") - 1


def fine_kernel(top, bottom, up, down, b1, b2, pooled, level, wide):
    tile, last_tile, gy, last_gy = place()
    x = [part[r] for part in (up, top, bottom, down) for r in range(2)]
    for q in range(6):
        level[q] = taps([x[q], x[q + 1], x[q + 2]], b1).astype(BF16)

    @pl.when(gy == 0)
    def _():
        level[:, :HALO] = jnp.zeros((6, HALO, 256), BF16)

    @pl.when(gy == last_gy)
    def _():
        level[:, HALO + COLS :] = jnp.zeros((6, HALO, 256), BF16)

    @pl.when(tile == 0)
    def _():
        level[0] = jnp.zeros((WIDE, 256), BF16)

    @pl.when(tile == last_tile)
    def _():
        level[5] = jnp.zeros((WIDE, 256), BF16)

    col = lax.broadcasted_iota(jnp.int32, (HALF, 128), 0)
    inside = ((col >= HALO // 2) | (gy > 0)) & ((col < HALF - HALO // 2) | (gy < last_gy))
    for pair in range(2):
        two = [taps([level[q], level[q + 1], level[q + 2]], b2) for q in (2 * pair, 2 * pair + 1)]
        both = jnp.maximum(two[0], two[1])
        wide[...] = jnp.maximum(both[:, :128], both[:, 128:])
        most = jnp.maximum(wide[pl.ds(0, HALF, stride=2), :], wide[pl.ds(1, HALF, stride=2), :])
        pooled[pair] = jnp.where(inside, most, 0.0).astype(BF16)


def coarse_kernel(own, up, down, b3, b4, kept, to_1, to_2, to_3, level, parts):
    tile, last_tile, gy, last_gy = place()
    dev = lax.axis_index("dev")
    x = [part[r] for part in (up, own, down) for r in range(2)]
    col = lax.broadcasted_iota(jnp.int32, (HALF, 256), 0)
    inside = ((col >= HALO // 2) | (gy > 0)) & ((col < HALF - HALO // 2) | (gy < last_gy))
    for q in range(4):
        keep = inside
        if q == 0:
            keep = keep & (tile > 0)
        if q == 3:
            keep = keep & (tile < last_tile)
        level[q] = jnp.where(keep, taps([x[q], x[q + 1], x[q + 2]], b3), 0.0).astype(BF16)
    for q in range(2):
        features = taps([level[q], level[q + 1], level[q + 2]], b4)
        turned = jnp.transpose(features[HALO // 2 : HALO // 2 + 128], (1, 0))
        for part in range(4):
            parts[part, q] = turned[part * 64 : (part + 1) * 64].astype(BF16)
    for k, to in enumerate((kept, to_1, to_2, to_3)):
        to[...] = parts[(dev + k) % 4]


def last_kernel(kept, from_1, from_2, from_3, out, rows, wide):
    dev = lax.axis_index("dev")
    for k, part in enumerate((kept, from_1, from_2, from_3)):
        rows[pl.ds(2 * ((dev + 4 - k) % 4), 2)] = part[...].astype(F32)
    for r in range(8):
        wide[pl.ds(r, 64, stride=8), :] = rows[r]
    out[...] = wide[...].astype(BF16)


def shift(cells, row_step, col_step):
    groups, col_tiles, devs = (lax.axis_size(axis) for axis in ("gx", "gy", "dev"))
    pairs = []
    for g in range(groups):
        for t in range(col_tiles):
            for d in range(devs):
                tile, col_tile = g * devs + d + row_step, t + col_step
                if 0 <= tile < groups * devs and 0 <= col_tile < col_tiles:
                    target = ((tile // devs) * col_tiles + col_tile) * devs + tile % devs
                    pairs.append(((g * col_tiles + t) * devs + d, target))
    return lax.ppermute(cells, ("gx", "gy", "dev"), pairs)


def by_tap(weight):
    return jnp.transpose(weight, (2, 3, 4, 1, 0)).reshape(27 * weight.shape[1], weight.shape[0])


def body(volume, w_first, w_second, w_third, w_fourth):
    devs = lax.axis_size("dev")
    sds = jax.ShapeDtypeStruct
    main = sds((2, COLS, 256), BF16)
    ends = sds((4, HALO, 256), BF16)
    both = sds((2, WIDE, 256), BF16)
    top, bottom, left, right = call(
        pack_kernel, [main, main, ends, ends], [pltpu.VMEM((256, 4, COLS), F32)], 0, 1 << 20
    )(volume.reshape(256, 4, COLS))
    from_left = shift(right, 0, 1)
    from_right = shift(left, 0, -1)
    top, bottom = call(join_kernel, [both, both], [], 0, 1 << 20)(top, bottom, from_left, from_right)
    up = shift(bottom, 1, 0)
    down = shift(top, -1, 0)

    b1, b2, b3, b4 = call(
        weights_kernel,
        [sds((768, 768), BF16), sds((768, 768), BF16), sds((384, 768), BF16), sds((768, 768), BF16)],
        [],
        0,
        4 << 20,
    )(by_tap(w_first), by_tap(w_second), by_tap(w_third), by_tap(w_fourth))

    pooled = call(
        fine_kernel,
        sds((2, HALF, 128), BF16),
        [pltpu.VMEM((6, WIDE, 256), BF16), pltpu.VMEM((WIDE, 128), F32)],
        2 * 10 * WIDE * 768 * 768,
        5 << 20,
    )(top, bottom, up, down, b1, b2)
    up = shift(pooled, 1, 0)
    down = shift(pooled, -1, 0)

    part = sds((2, 64, 128), BF16)
    kept, *sent = call(
        coarse_kernel,
        [part, part, part, part],
        [pltpu.VMEM((4, HALF, 256), BF16), pltpu.VMEM((4, 2, 64, 128), BF16)],
        2 * 4 * HALF * 768 * 768,
        2 << 20,
    )(pooled, up, down, b3, b4)
    received = [lax.ppermute(cells, "dev", [(i, (i + k + 1) % devs) for i in range(devs)]) for k, cells in enumerate(sent)]
    out = call(
        last_kernel, sds((512, 128), BF16), [pltpu.VMEM((8, 64, 128), F32), pltpu.VMEM((512, 128), F32)], 0, 1 << 18
    )(kept, *received)
    return out.reshape(32, 2, 8, 128)


def solution(mesh):
    return jax.shard_map(
        body,
        mesh=mesh,
        in_specs=(P(None, None, ("gx", "dev"), "gy"), P(), P(), P(), P()),
        out_specs=P(None, "dev", "gx", "gy"),
        check_vma=False,
    )
```

time: 80.8 us -> 73.5 us (0.910)
  the two profiles are of different devices: /device:TPU:450 before, /device:TPU:392 now
where the time goes in v1:
time: 73.5 us; the launch traced here: 73.2 us
  starting transfers between devices  44.1 us (60%)
  waiting for transfers between devices  19.2 us (26%)
  Pallas kernels  8.27 us (11%)
  local copies, waits for them, and re-layouts  1.45 us (2%)
    ppermute x6, starting transfers between devices, shift(): return lax.ppermute(cells, ('gx', 'gy', 'dev'), pairs)  29.3 us
    ppermute x6, waiting for transfers between devices, shift(): return lax.ppermute(cells, ('gx', 'gy', 'dev'), pairs)  15.3 us
    ppermute x3, starting transfers between devices, body(): lax.ppermute(cells, 'dev', [(i, (i + k + 1) % devs) for i in range(devs)])  14.8 us
    pallas_call x1, Pallas kernels, body(): call(fine_kernel, sds((2, HALF, 128), BF16), [pltpu.VMEM((6, WIDE, 256),...  3.92 us
    ppermute x3, waiting for transfers between devices, body(): lax.ppermute(cells, 'dev', [(i, (i + k + 1) % devs) for i in range(devs)])  3.86 us
    pallas_call x1, Pallas kernels, body(): call(weights_kernel, [sds((768, 768), BF16), sds((768, 768), BF16), sds((...  1.89 us
  transfers between devices with their start and end apart: 9, of which 7 were waited for; matrix products, arithmetic and copies ran while one was open for 1% of the time, Pallas kernels for 3%

profile of v1, /device:TPU:392, one launch (start us, length us, event | category | flops | bytes accessed | tf_op | source)
XLA Modules:
  0.0 73.2 jit_solution(804369782618914120)
XLA Ops:
  0.0 1.0 %copy-done = bf16[16,16,4,256]{3,2,1,0:T(4,128)(2,1)S(1)} copy-done((bf16[16,16,4,256]{3,2,1,0:T(4,128)(2,1)S(1)}, bf16[16,16,4,256]{3,2,1,0:T(4,128)(2,1)}, u32[]{:S(2)}) %copy-start) | copy-done | bytes 524312
  1.1 0.6 shard_map.55
  1.6 2.9 %collective-permute-start = (bf16[4,16,256]{2,1,0:T(8,128)(2,1)S(1)}, bf16[4,16,256]{2,1,0:T(8,128)(2,1)S(1)}, u32[]{:S(2)}, u32[]{:S(2)}) collective-permute-start(bf16[4,16,256]{2,1,0:T(8,128)(2,1)S(1)} %get-tuple-element.21), channel_id=1, source_target_pairs={{0,4},{1,5},{2,6},{3,7},{4,8},{5,9},{6,10},{7,11},{8,12},{9,13},{1... | collective-permute-start | bytes 98312 | tf_op jit(solution)/shard_map/ppermute | solution.py:169
  4.6 1.3 %collective-permute-start.1 = (bf16[4,16,256]{2,1,0:T(8,128)(2,1)S(1)}, bf16[4,16,256]{2,1,0:T(8,128)(2,1)S(1)}, u32[]{:S(2)}, u32[]{:S(2)}) collective-permute-start(bf16[4,16,256]{2,1,0:T(8,128)(2,1)S(1)} %get-tuple-element.22), channel_id=1, source_target_pairs={{4,0},{5,1},{6,2},{7,3},{8,4},{9,5},{10,6},{11,7},{12,8},{13,9},{1... | collective-permute-start | bytes 98312 | tf_op jit(solution)/shard_map/ppermute | solution.py:169
  5.9 0.3 collective-permute-done.left
  6.2 4.4 %collective-permute-done.1.right = bf16[4,16,256]{2,1,0:T(8,128)(2,1)S(1)} collective-permute-done((bf16[4,16,256]{2,1,0:T(8,128)(2,1)S(1)}, bf16[4,16,256]{2,1,0:T(8,128)(2,1)S(1)}, u32[]{:S(2)}, u32[]{:S(2)}) %collective-permute-start.1) | collective-permute-done | bytes 32800 | tf_op jit(solution)/shard_map/ppermute | solution.py:169
  10.6 2.4 %collective-permute-start.3 = (bf16[2,288,256]{2,1,0:T(8,128)(2,1)S(1)}, bf16[2,288,256]{2,1,0:T(8,128)(2,1)S(1)}, u32[]{:S(2)}, u32[]{:S(2)}) collective-permute-start(bf16[2,288,256]{2,1,0:T(8,128)(2,1)S(1)} %get-tuple-element.23.top), channel_id=1, source_target_pairs={{1,0},{2,1},{3,2},{5,4},{6,5},{7,6},{9,8},{10,9},{11,10},{13,12},{... | collective-permute-start | bytes 884744 | tf_op jit(solution)/shard_map/ppermute | solution.py:169
  12.9 3.5 %collective-permute-start.2 = (bf16[2,288,256]{2,1,0:T(8,128)(2,1)S(1)}, bf16[2,288,256]{2,1,0:T(8,128)(2,1)S(1)}, u32[]{:S(2)}, u32[]{:S(2)}) collective-permute-start(bf16[2,288,256]{2,1,0:T(8,128)(2,1)S(1)} %get-tuple-element.24.bottom), channel_id=1, source_target_pairs={{0,1},{1,2},{2,3},{3,64},{4,5},{5,6},{6,7},{7,68},{8,9},{9,10},{10... | collective-permute-start | bytes 884744 | tf_op jit(solution)/shard_map/ppermute | solution.py:169
  16.4 0.1 copy.6
  16.7 0.2 copy.8
  16.9 1.9 %shard_map.57 = (bf16[768,768]{1,0:T(8,128)(2,1)S(1)}, bf16[768,768]{1,0:T(8,128)(2,1)S(1)}, bf16[384,768]{1,0:T(8,128)(2,1)S(1)}, bf16[768,768]{1,0:T(8,128)(2,1)S(1)}) custom-call(bf16[432,16]{1,0:T(8,128)(2,1)S(1)} %bitcast.13, bf16[432,16]{1,0:T(8,128)(2,1)S(1)} %bitcast.14, bf16[432,32]{1,0:T(8,128)(2,1)S(1)} %bitcast.15, bf16[864,32]{1,0:T(8,128)(2,1)S(1)} %bitcast.11), custom_call_target="tpu_custom_call" | custom-call | bytes 4194304 | tf_op jit(solution)/shard_map/pallas_call | solution.py:191
  18.8 1.2 %collective-permute-done.3.down = bf16[2,288,256]{2,1,0:T(8,128)(2,1)S(1)} collective-permute-done((bf16[2,288,256]{2,1,0:T(8,128)(2,1)S(1)}, bf16[2,288,256]{2,1,0:T(8,128)(2,1)S(1)}, u32[]{:S(2)}, u32[]{:S(2)}) %collective-permute-start.3) | collective-permute-done | bytes 294944 | tf_op jit(solution)/shard_map/ppermute | solution.py:169
  20.0 5.1 %collective-permute-done.2.up = bf16[2,288,256]{2,1,0:T(8,128)(2,1)S(1)} collective-permute-done((bf16[2,288,256]{2,1,0:T(8,128)(2,1)S(1)}, bf16[2,288,256]{2,1,0:T(8,128)(2,1)S(1)}, u32[]{:S(2)}, u32[]{:S(2)}) %collective-permute-start.2) | collective-permute-done | bytes 294944 | tf_op jit(solution)/shard_map/ppermute | solution.py:169
  25.1 3.9 %shard_map.58.own = bf16[2,144,128]{2,1,0:T(8,128)(2,1)S(1)} custom-call(bf16[2,288,256]{2,1,0:T(8,128)(2,1)S(1)} %get-tuple-element.23.top, bf16[2,288,256]{2,1,0:T(8,128)(2,1)S(1)} %get-tuple-element.24.bottom, bf16[2,288,256]{2,1,0:T(8,128)(2,1)S(1)} %collective-permute-done.2.up, bf16[2,288,256]{2,1,0:T(8,128)(2,1)S(1)} %collective-permute-done.3.down, ...), custom_call_target="tpu_custom_call" | custom-call | flops 3397386240 | bytes 5242880 | tf_op jit(solution)/shard_map/pallas_call | solution.py:199
  29.1 17.4 %collective-permute-start.5 = (bf16[2,144,128]{2,1,0:T(8,128)(2,1)S(1)}, bf16[2,144,128]{2,1,0:T(8,128)(2,1)S(1)}, u32[]{:S(2)}, u32[]{:S(2)}) collective-permute-start(bf16[2,144,128]{2,1,0:T(8,128)(2,1)S(1)} %shard_map.58.own), channel_id=1, source_target_pairs={{1,0},{2,1},{3,2},{5,4},{6,5},{7,6},{9,8},{10,9},{11,10},{13,12},{... | collective-permute-start | bytes 221192 | tf_op jit(solution)/shard_map/ppermute | solution.py:169
  46.4 1.9 %collective-permute-start.4 = (bf16[2,144,128]{2,1,0:T(8,128)(2,1)S(1)}, bf16[2,144,128]{2,1,0:T(8,128)(2,1)S(1)}, u32[]{:S(2)}, u32[]{:S(2)}) collective-permute-start(bf16[2,144,128]{2,1,0:T(8,128)(2,1)S(1)} %shard_map.58.own), channel_id=1, source_target_pairs={{0,1},{1,2},{2,3},{3,64},{4,5},{5,6},{6,7},{7,68},{8,9},{9,10},{10... | collective-permute-start | bytes 221192 | tf_op jit(solution)/shard_map/ppermute | solution.py:169
  48.4 0.2 collective-permute-done.5.down
  48.6 4.1 %collective-permute-done.4.up = bf16[2,144,128]{2,1,0:T(8,128)(2,1)S(1)} collective-permute-done((bf16[2,144,128]{2,1,0:T(8,128)(2,1)S(1)}, bf16[2,144,128]{2,1,0:T(8,128)(2,1)S(1)}, u32[]{:S(2)}, u32[]{:S(2)}) %collective-permute-start.4) | collective-permute-done | bytes 73760 | tf_op jit(solution)/shard_map/ppermute | solution.py:169
  52.7 1.1 %shard_map.59 = (bf16[2,64,128]{2,1,0:T(8,128)(2,1)S(1)}, bf16[2,64,128]{2,1,0:T(8,128)(2,1)S(1)}, bf16[2,64,128]{2,1,0:T(8,128)(2,1)S(1)}, bf16[2,64,128]{2,1,0:T(8,128)(2,1)S(1)}) custom-call(bf16[2,144,128]{2,1,0:T(8,128)(2,1)S(1)} %shard_map.58.own, bf16[2,144,128]{2,1,0:T(8,128)(2,1)S(1)} %collective-permute-done.4.up, ...), custom_call_target="tpu_custom_call" | custom-call | flops 679477248 | bytes 2097152 | tf_op jit(solution)/shard_map/pallas_call | solution.py:210
  53.8 1.9 %collective-permute-start.6 = (bf16[2,64,128]{2,1,0:T(8,128)(2,1)S(1)}, bf16[2,64,128]{2,1,0:T(8,128)(2,1)S(1)}, u32[]{:S(2)}, u32[]{:S(2)}) collective-permute-start(bf16[2,64,128]{2,1,0:T(8,128)(2,1)S(1)} %get-tuple-element.30), channel_id=1, source_target_pairs={{0,1},{1,2},{2,3},{3,0},{4,5},{5,6},{6,7},{7,4},{8,9},{9,10},{10,1... | collective-permute-start | bytes 98312 | tf_op jit(solution)/shard_map/ppermute | solution.py:217
  55.7 10.9 %collective-permute-start.7 = (bf16[2,64,128]{2,1,0:T(8,128)(2,1)S(1)}, bf16[2,64,128]{2,1,0:T(8,128)(2,1)S(1)}, u32[]{:S(2)}, u32[]{:S(2)}) collective-permute-start(bf16[2,64,128]{2,1,0:T(8,128)(2,1)S(1)} %get-tuple-element.31), channel_id=1, source_target_pairs={{0,2},{1,3},{2,0},{3,1},{4,6},{5,7},{6,4},{7,5},{8,10},{9,11},{10,... | collective-permute-start | bytes 98312 | tf_op jit(solution)/shard_map/ppermute | solution.py:217
  66.6 1.9 %collective-permute-start.8 = (bf16[2,64,128]{2,1,0:T(8,128)(2,1)S(1)}, bf16[2,64,128]{2,1,0:T(8,128)(2,1)S(1)}, u32[]{:S(2)}, u32[]{:S(2)}) collective-permute-start(bf16[2,64,128]{2,1,0:T(8,128)(2,1)S(1)} %get-tuple-element.32), channel_id=1, source_target_pairs={{0,3},{1,0},{2,1},{3,2},{4,7},{5,4},{6,5},{7,6},{8,11},{9,8},{10,9... | collective-permute-start | bytes 98312 | tf_op jit(solution)/shard_map/ppermute | solution.py:217
  68.6 3.9 %collective-permute-done.8.from_3 = bf16[2,64,128]{2,1,0:T(8,128)(2,1)S(1)} collective-permute-done((bf16[2,64,128]{2,1,0:T(8,128)(2,1)S(1)}, bf16[2,64,128]{2,1,0:T(8,128)(2,1)S(1)}, u32[]{:S(2)}, u32[]{:S(2)}) %collective-permute-start.8) | collective-permute-done | bytes 32800 | tf_op jit(solution)/shard_map/ppermute | solution.py:217
  72.4 0.8 %shard_map.60 = bf16[512,128]{1,0:T(8,128)(2,1)} custom-call(bf16[2,64,128]{2,1,0:T(8,128)(2,1)S(1)} %get-tuple-element.29.kept, bf16[2,64,128]{2,1,0:T(8,128)(2,1)S(1)} %collective-permute-done.6.from_1, bf16[2,64,128]{2,1,0:T(8,128)(2,1)S(1)} %collective-permute-done.7.from_2, bf16[2,64,128]{2,1,0:T(8,128)(2,1)S(1)} %collective-permute-done.8.from_3), custom_call_target="tpu_custom_call" | custom-call | bytes 262144 | tf_op jit(solution)/shard_map/pallas_call | solution.py:218
  (13 shorter events, 0.2 us)
Async XLA Ops:
  0.0 1.0 %copy-start = (bf16[16,16,4,256]{3,2,1,0:T(4,128)(2,1)S(1)}, bf16[16,16,4,256]{3,2,1,0:T(4,128)(2,1)}, u32[]{:S(2)}) copy-start(bf16[16,16,4,256]{3,2,1,0:T(4,128)(2,1)} %param.5) | copy-start | bytes 1572868
  1.0 15.4 %copy-start.3 = (bf16[16,16,3,3,3]{1,0,4,3,2:T(8,128)(2,1)S(1)}, bf16[16,16,3,3,3]{1,0,4,3,2:T(8,128)(2,1)}, u32[]{:S(2)}) copy-start(bf16[16,16,3,3,3]{1,0,4,3,2:T(8,128)(2,1)} %param.6) | copy-start | bytes 41476
  1.0 15.5 %copy-start.4 = (bf16[16,16,3,3,3]{1,0,4,3,2:T(8,128)(2,1)S(1)}, bf16[16,16,3,3,3]{1,0,4,3,2:T(8,128)(2,1)}, u32[]{:S(2)}) copy-start(bf16[16,16,3,3,3]{1,0,4,3,2:T(8,128)(2,1)} %param.7) | copy-start | bytes 41476
  1.0 15.7 %copy-start.2 = (bf16[32,32,3,3,3]{1,0,4,3,2:T(8,128)(2,1)S(1)}, bf16[32,32,3,3,3]{1,0,4,3,2:T(8,128)(2,1)}, u32[]{:S(2)}) copy-start(bf16[32,32,3,3,3]{1,0,4,3,2:T(8,128)(2,1)} %param.9) | copy-start | bytes 165892
  1.0 15.8 %copy-start.1 = (bf16[32,16,3,3,3]{0,1,4,3,2:T(8,128)(2,1)S(1)}, bf16[32,16,3,3,3]{0,1,4,3,2:T(8,128)(2,1)}, u32[]{:S(2)}) copy-start(bf16[32,16,3,3,3]{0,1,4,3,2:T(8,128)(2,1)} %param.8) | copy-start | bytes 82948
  1.6 4.5 %collective-permute-start = (bf16[4,16,256]{2,1,0:T(8,128)(2,1)S(1)}, bf16[4,16,256]{2,1,0:T(8,128)(2,1)S(1)}, u32[]{:S(2)}, u32[]{:S(2)}) collective-permute-start(bf16[4,16,256]{2,1,0:T(8,128)(2,1)S(1)} %get-tuple-element.21), channel_id=1, source_target_pairs={{0,4},{1,5},{2,6},{3,7},{4,8},{5,9},{6,10},{7,11},{8,12},{9,13},{1... | collective-permute-start | bytes 98312 | tf_op jit(solution)/shard_map/ppermute | solution.py:169
  4.6 6.0 %collective-permute-start.1 = (bf16[4,16,256]{2,1,0:T(8,128)(2,1)S(1)}, bf16[4,16,256]{2,1,0:T(8,128)(2,1)S(1)}, u32[]{:S(2)}, u32[]{:S(2)}) collective-permute-start(bf16[4,16,256]{2,1,0:T(8,128)(2,1)S(1)} %get-tuple-element.22), channel_id=1, source_target_pairs={{4,0},{5,1},{6,2},{7,3},{8,4},{9,5},{10,6},{11,7},{12,8},{13,9},{1... | collective-permute-start | bytes 98312 | tf_op jit(solution)/shard_map/ppermute | solution.py:169
  10.6 9.4 %collective-permute-start.3 = (bf16[2,288,256]{2,1,0:T(8,128)(2,1)S(1)}, bf16[2,288,256]{2,1,0:T(8,128)(2,1)S(1)}, u32[]{:S(2)}, u32[]{:S(2)}) collective-permute-start(bf16[2,288,256]{2,1,0:T(8,128)(2,1)S(1)} %get-tuple-element.23.top), channel_id=1, source_target_pairs={{1,0},{2,1},{3,2},{5,4},{6,5},{7,6},{9,8},{10,9},{11,10},{13,12},{... | collective-permute-start | bytes 884744 | tf_op jit(solution)/shard_map/ppermute | solution.py:169
  12.9 12.2 %collective-permute-start.2 = (bf16[2,288,256]{2,1,0:T(8,128)(2,1)S(1)}, bf16[2,288,256]{2,1,0:T(8,128)(2,1)S(1)}, u32[]{:S(2)}, u32[]{:S(2)}) collective-permute-start(bf16[2,288,256]{2,1,0:T(8,128)(2,1)S(1)} %get-tuple-element.24.bottom), channel_id=1, source_target_pairs={{0,1},{1,2},{2,3},{3,64},{4,5},{5,6},{6,7},{7,68},{8,9},{9,10},{10... | collective-permute-start | bytes 884744 | tf_op jit(solution)/shard_map/ppermute | solution.py:169
  29.1 19.5 %collective-permute-start.5 = (bf16[2,144,128]{2,1,0:T(8,128)(2,1)S(1)}, bf16[2,144,128]{2,1,0:T(8,128)(2,1)S(1)}, u32[]{:S(2)}, u32[]{:S(2)}) collective-permute-start(bf16[2,144,128]{2,1,0:T(8,128)(2,1)S(1)} %shard_map.58.own), channel_id=1, source_target_pairs={{1,0},{2,1},{3,2},{5,4},{6,5},{7,6},{9,8},{10,9},{11,10},{13,12},{... | collective-permute-start | bytes 221192 | tf_op jit(solution)/shard_map/ppermute | solution.py:169
  46.4 6.2 %collective-permute-start.4 = (bf16[2,144,128]{2,1,0:T(8,128)(2,1)S(1)}, bf16[2,144,128]{2,1,0:T(8,128)(2,1)S(1)}, u32[]{:S(2)}, u32[]{:S(2)}) collective-permute-start(bf16[2,144,128]{2,1,0:T(8,128)(2,1)S(1)} %shard_map.58.own), channel_id=1, source_target_pairs={{0,1},{1,2},{2,3},{3,64},{4,5},{5,6},{6,7},{7,68},{8,9},{9,10},{10... | collective-permute-start | bytes 221192 | tf_op jit(solution)/shard_map/ppermute | solution.py:169
  53.8 14.8 %collective-permute-start.6 = (bf16[2,64,128]{2,1,0:T(8,128)(2,1)S(1)}, bf16[2,64,128]{2,1,0:T(8,128)(2,1)S(1)}, u32[]{:S(2)}, u32[]{:S(2)}) collective-permute-start(bf16[2,64,128]{2,1,0:T(8,128)(2,1)S(1)} %get-tuple-element.30), channel_id=1, source_target_pairs={{0,1},{1,2},{2,3},{3,0},{4,5},{5,6},{6,7},{7,4},{8,9},{9,10},{10,1... | collective-permute-start | bytes 98312 | tf_op jit(solution)/shard_map/ppermute | solution.py:217
  55.7 12.9 %collective-permute-start.7 = (bf16[2,64,128]{2,1,0:T(8,128)(2,1)S(1)}, bf16[2,64,128]{2,1,0:T(8,128)(2,1)S(1)}, u32[]{:S(2)}, u32[]{:S(2)}) collective-permute-start(bf16[2,64,128]{2,1,0:T(8,128)(2,1)S(1)} %get-tuple-element.31), channel_id=1, source_target_pairs={{0,2},{1,3},{2,0},{3,1},{4,6},{5,7},{6,4},{7,5},{8,10},{9,11},{10,... | collective-permute-start | bytes 98312 | tf_op jit(solution)/shard_map/ppermute | solution.py:217
  66.6 5.8 %collective-permute-start.8 = (bf16[2,64,128]{2,1,0:T(8,128)(2,1)S(1)}, bf16[2,64,128]{2,1,0:T(8,128)(2,1)S(1)}, u32[]{:S(2)}, u32[]{:S(2)}) collective-permute-start(bf16[2,64,128]{2,1,0:T(8,128)(2,1)S(1)} %get-tuple-element.32), channel_id=1, source_target_pairs={{0,3},{1,0},{2,1},{3,2},{4,7},{5,4},{6,5},{7,6},{8,11},{9,8},{10,9... | collective-permute-start | bytes 98312 | tf_op jit(solution)/shard_map/ppermute | solution.py:217

commit v2 on v1

--- a/solution.py
+++ b/solution.py
@@ -125,9 +125,8 @@
         pooled[pair] = jnp.where(inside, most, 0.0).astype(BF16)
 
 
-def coarse_kernel(own, up, down, b3, b4, kept, to_1, to_2, to_3, level, parts):
+def coarse_kernel(own, up, down, b3, b4, parts, level):
     tile, last_tile, gy, last_gy = place()
-    dev = lax.axis_index("dev")
     x = [part[r] for part in (up, own, down) for r in range(2)]
     col = lax.broadcasted_iota(jnp.int32, (HALF, 256), 0)
     inside = ((col >= HALO // 2) | (gy > 0)) & ((col < HALF - HALO // 2) | (gy < last_gy))
@@ -143,16 +142,11 @@
         turned = jnp.transpose(features[HALO // 2 : HALO // 2 + 128], (1, 0))
         for part in range(4):
             parts[part, q] = turned[part * 64 : (part + 1) * 64].astype(BF16)
-    for k, to in enumerate((kept, to_1, to_2, to_3)):
-        to[...] = parts[(dev + k) % 4]
-
-
-def last_kernel(kept, from_1, from_2, from_3, out, rows, wide):
-    dev = lax.axis_index("dev")
-    for k, part in enumerate((kept, from_1, from_2, from_3)):
-        rows[pl.ds(2 * ((dev + 4 - k) % 4), 2)] = part[...].astype(F32)
+
+
+def last_kernel(parts, out, wide):
     for r in range(8):
-        wide[pl.ds(r, 64, stride=8), :] = rows[r]
+        wide[pl.ds(r, 64, stride=8), :] = parts[r // 2, r % 2].astype(F32)
     out[...] = wide[...].astype(BF16)
 
 
@@ -174,7 +168,6 @@
 
 
 def body(volume, w_first, w_second, w_third, w_fourth):
-    devs = lax.axis_size("dev")
     sds = jax.ShapeDtypeStruct
     main = sds((2, COLS, 256), BF16)
     ends = sds((4, HALO, 256), BF16)
@@ -206,18 +199,11 @@
     up = shift(pooled, 1, 0)
     down = shift(pooled, -1, 0)
 
-    part = sds((2, 64, 128), BF16)
-    kept, *sent = call(
-        coarse_kernel,
-        [part, part, part, part],
-        [pltpu.VMEM((4, HALF, 256), BF16), pltpu.VMEM((4, 2, 64, 128), BF16)],
-        2 * 4 * HALF * 768 * 768,
-        2 << 20,
+    parts = call(
+        coarse_kernel, sds((4, 2, 64, 128), BF16), [pltpu.VMEM((4, HALF, 256), BF16)], 2 * 4 * HALF * 768 * 768, 2 << 20
     )(pooled, up, down, b3, b4)
-    received = [lax.ppermute(cells, "dev", [(i, (i + k + 1) % devs) for i in range(devs)]) for k, cells in enumerate(sent)]
-    out = call(
-        last_kernel, sds((512, 128), BF16), [pltpu.VMEM((8, 64, 128), F32), pltpu.VMEM((512, 128), F32)], 0, 1 << 18
-    )(kept, *received)
+    parts = lax.all_to_all(parts, "dev", split_axis=0, concat_axis=0, tiled=True)
+    out = call(last_kernel, sds((512, 128), BF16), [pltpu.VMEM((512, 128), F32)], 0, 1 << 18)(parts)
     return out.reshape(32, 2, 8, 128)
 
 

time: 73.5 us -> 69.7 us (0.948)
  the two profiles are of different devices: /device:TPU:392 before, /device:TPU:384 now
where the time goes in v2:
time: 69.7 us; the launch traced here: 69.3 us
  waiting for transfers between devices  33.1 us (47%)
  starting transfers between devices  18.1 us (26%)
  blocking collectives  8.36 us (12%)
  Pallas kernels  8.23 us (12%)
  local copies, waits for them, and re-layouts  1.45 us (2%)
    ppermute x6, waiting for transfers between devices, shift(): return lax.ppermute(cells, ('gx', 'gy', 'dev'), pairs)  33.1 us
    ppermute x6, starting transfers between devices, shift(): return lax.ppermute(cells, ('gx', 'gy', 'dev'), pairs)  18.1 us
    all_to_all x1, blocking collectives, body(): lax.all_to_all(parts, 'dev', split_axis=0, concat_axis=0, tiled=True)  8.36 us
    pallas_call x1, Pallas kernels, body(): call(fine_kernel, sds((2, HALF, 128), BF16), [pltpu.VMEM((6, WIDE, 256),...  3.92 us
    pallas_call x1, Pallas kernels, body(): call(weights_kernel, [sds((768, 768), BF16), sds((768, 768), BF16), sds((...  1.9 us
  transfers between devices with their start and end apart: 6, of which 6 were waited for; matrix products, arithmetic and copies ran while one was open for 1% of the time, Pallas kernels for 3%

profile of v2, /device:TPU:384, one launch (start us, length us, event | category | flops | bytes accessed | tf_op | source)
XLA Modules:
  0.0 69.3 jit_solution(16211628532546612020)
XLA Ops:
  0.0 1.0 %copy-done = bf16[16,16,4,256]{3,2,1,0:T(4,128)(2,1)S(1)} copy-done((bf16[16,16,4,256]{3,2,1,0:T(4,128)(2,1)S(1)}, bf16[16,16,4,256]{3,2,1,0:T(4,128)(2,1)}, u32[]{:S(2)}) %copy-start) | copy-done | bytes 524312
  1.1 0.6 shard_map.55
  1.6 2.9 %collective-permute-start = (bf16[4,16,256]{2,1,0:T(8,128)(2,1)S(1)}, bf16[4,16,256]{2,1,0:T(8,128)(2,1)S(1)}, u32[]{:S(2)}, u32[]{:S(2)}) collective-permute-start(bf16[4,16,256]{2,1,0:T(8,128)(2,1)S(1)} %get-tuple-element.17), channel_id=1, source_target_pairs={{0,4},{1,5},{2,6},{3,7},{4,8},{5,9},{6,10},{7,11},{8,12},{9,13},{1... | collective-permute-start | bytes 98312 | tf_op jit(solution)/shard_map/ppermute | solution.py:163
  4.6 1.3 %collective-permute-start.1 = (bf16[4,16,256]{2,1,0:T(8,128)(2,1)S(1)}, bf16[4,16,256]{2,1,0:T(8,128)(2,1)S(1)}, u32[]{:S(2)}, u32[]{:S(2)}) collective-permute-start(bf16[4,16,256]{2,1,0:T(8,128)(2,1)S(1)} %get-tuple-element.18), channel_id=1, source_target_pairs={{4,0},{5,1},{6,2},{7,3},{8,4},{9,5},{10,6},{11,7},{12,8},{13,9},{1... | collective-permute-start | bytes 98312 | tf_op jit(solution)/shard_map/ppermute | solution.py:163
  5.9 0.3 collective-permute-done.left
  6.2 4.4 %collective-permute-done.1.right = bf16[4,16,256]{2,1,0:T(8,128)(2,1)S(1)} collective-permute-done((bf16[4,16,256]{2,1,0:T(8,128)(2,1)S(1)}, bf16[4,16,256]{2,1,0:T(8,128)(2,1)S(1)}, u32[]{:S(2)}, u32[]{:S(2)}) %collective-permute-start.1) | collective-permute-done | bytes 32800 | tf_op jit(solution)/shard_map/ppermute | solution.py:163
  10.6 6.1 %collective-permute-start.3 = (bf16[2,288,256]{2,1,0:T(8,128)(2,1)S(1)}, bf16[2,288,256]{2,1,0:T(8,128)(2,1)S(1)}, u32[]{:S(2)}, u32[]{:S(2)}) collective-permute-start(bf16[2,288,256]{2,1,0:T(8,128)(2,1)S(1)} %get-tuple-element.19.top), channel_id=1, source_target_pairs={{1,0},{2,1},{3,2},{5,4},{6,5},{7,6},{9,8},{10,9},{11,10},{13,12},{... | collective-permute-start | bytes 884744 | tf_op jit(solution)/shard_map/ppermute | solution.py:163
  16.7 1.9 %collective-permute-start.2 = (bf16[2,288,256]{2,1,0:T(8,128)(2,1)S(1)}, bf16[2,288,256]{2,1,0:T(8,128)(2,1)S(1)}, u32[]{:S(2)}, u32[]{:S(2)}) collective-permute-start(bf16[2,288,256]{2,1,0:T(8,128)(2,1)S(1)} %get-tuple-element.20.bottom), channel_id=1, source_target_pairs={{0,1},{1,2},{2,3},{3,64},{4,5},{5,6},{6,7},{7,68},{8,9},{9,10},{10... | collective-permute-start | bytes 884744 | tf_op jit(solution)/shard_map/ppermute | solution.py:163
  18.6 0.0 copy-done.3
  18.6 0.1 copy.6
  18.8 0.1 copy.7
  18.9 0.0 copy-done.2
  18.9 0.2 copy.8
  19.1 1.9 %shard_map.57 = (bf16[768,768]{1,0:T(8,128)(2,1)S(1)}, bf16[768,768]{1,0:T(8,128)(2,1)S(1)}, bf16[384,768]{1,0:T(8,128)(2,1)S(1)}, bf16[768,768]{1,0:T(8,128)(2,1)S(1)}) custom-call(bf16[432,16]{1,0:T(8,128)(2,1)S(1)} %bitcast.13, bf16[432,16]{1,0:T(8,128)(2,1)S(1)} %bitcast.14, bf16[432,32]{1,0:T(8,128)(2,1)S(1)} %bitcast.15, bf16[864,32]{1,0:T(8,128)(2,1)S(1)} %bitcast.11), custom_call_target="tpu_custom_call" | custom-call | bytes 4194304 | tf_op jit(solution)/shard_map/pallas_call | solution.py:184
  21.0 9.5 %collective-permute-done.3.down = bf16[2,288,256]{2,1,0:T(8,128)(2,1)S(1)} collective-permute-done((bf16[2,288,256]{2,1,0:T(8,128)(2,1)S(1)}, bf16[2,288,256]{2,1,0:T(8,128)(2,1)S(1)}, u32[]{:S(2)}, u32[]{:S(2)}) %collective-permute-start.3) | collective-permute-done | bytes 294944 | tf_op jit(solution)/shard_map/ppermute | solution.py:163
  30.5 9.7 %collective-permute-done.2.up = bf16[2,288,256]{2,1,0:T(8,128)(2,1)S(1)} collective-permute-done((bf16[2,288,256]{2,1,0:T(8,128)(2,1)S(1)}, bf16[2,288,256]{2,1,0:T(8,128)(2,1)S(1)}, u32[]{:S(2)}, u32[]{:S(2)}) %collective-permute-start.2) | collective-permute-done | bytes 294944 | tf_op jit(solution)/shard_map/ppermute | solution.py:163
  40.1 3.9 %shard_map.58.own = bf16[2,144,128]{2,1,0:T(8,128)(2,1)S(1)} custom-call(bf16[2,288,256]{2,1,0:T(8,128)(2,1)S(1)} %get-tuple-element.19.top, bf16[2,288,256]{2,1,0:T(8,128)(2,1)S(1)} %get-tuple-element.20.bottom, bf16[2,288,256]{2,1,0:T(8,128)(2,1)S(1)} %collective-permute-done.2.up, bf16[2,288,256]{2,1,0:T(8,128)(2,1)S(1)} %collective-permute-done.3.down, ...), custom_call_target="tpu_custom_call" | custom-call | flops 3397386240 | bytes 5242880 | tf_op jit(solution)/shard_map/pallas_call | solution.py:192
  44.1 1.9 %collective-permute-start.5 = (bf16[2,144,128]{2,1,0:T(8,128)(2,1)S(1)}, bf16[2,144,128]{2,1,0:T(8,128)(2,1)S(1)}, u32[]{:S(2)}, u32[]{:S(2)}) collective-permute-start(bf16[2,144,128]{2,1,0:T(8,128)(2,1)S(1)} %shard_map.58.own), channel_id=1, source_target_pairs={{1,0},{2,1},{3,2},{5,4},{6,5},{7,6},{9,8},{10,9},{11,10},{13,12},{... | collective-permute-start | bytes 221192 | tf_op jit(solution)/shard_map/ppermute | solution.py:163
  46.0 3.9 %collective-permute-start.4 = (bf16[2,144,128]{2,1,0:T(8,128)(2,1)S(1)}, bf16[2,144,128]{2,1,0:T(8,128)(2,1)S(1)}, u32[]{:S(2)}, u32[]{:S(2)}) collective-permute-start(bf16[2,144,128]{2,1,0:T(8,128)(2,1)S(1)} %shard_map.58.own), channel_id=1, source_target_pairs={{0,1},{1,2},{2,3},{3,64},{4,5},{5,6},{6,7},{7,68},{8,9},{9,10},{10... | collective-permute-start | bytes 221192 | tf_op jit(solution)/shard_map/ppermute | solution.py:163
  49.9 0.4 collective-permute-done.5.down
  50.3 8.9 %collective-permute-done.4.up = bf16[2,144,128]{2,1,0:T(8,128)(2,1)S(1)} collective-permute-done((bf16[2,144,128]{2,1,0:T(8,128)(2,1)S(1)}, bf16[2,144,128]{2,1,0:T(8,128)(2,1)S(1)}, u32[]{:S(2)}, u32[]{:S(2)}) %collective-permute-start.4) | collective-permute-done | bytes 73760 | tf_op jit(solution)/shard_map/ppermute | solution.py:163
  59.2 1.1 %shard_map.59 = bf16[4,2,64,128]{3,2,1,0:T(8,128)(2,1)S(1)} custom-call(bf16[2,144,128]{2,1,0:T(8,128)(2,1)S(1)} %shard_map.58.own, bf16[2,144,128]{2,1,0:T(8,128)(2,1)S(1)} %collective-permute-done.4.up, bf16[2,144,128]{2,1,0:T(8,128)(2,1)S(1)} %collective-permute-done.5.down, bf16[384,768]{1,0:T(8,128)(2,1)S(1)} %get-tuple-element.23.b3, ...), custom_call_target="tpu_custom_call" | custom-call | flops 679477248 | bytes 2097152 | tf_op jit(solution)/shard_map/pallas_call | solution.py:202
  60.3 8.4 %all_to_all.5.parts = bf16[4,2,64,128]{3,2,1,0:T(8,128)(2,1)S(1)} all-to-all(bf16[4,2,64,128]{3,2,1,0:T(8,128)(2,1)S(1)} %shard_map.59), channel_id=1, replica_groups=mesh['gx'=8,'gy'=16,'dev'=4] {'dev'}, dimensions={0} | all-to-all | bytes 262144 | tf_op jit(solution)/shard_map/all_to_all | solution.py:205
  68.6 0.7 %shard_map.60 = bf16[512,128]{1,0:T(8,128)(2,1)} custom-call(bf16[4,2,64,128]{3,2,1,0:T(8,128)(2,1)S(1)} %all_to_all.5.parts), custom_call_target="tpu_custom_call" | custom-call | bytes 262144 | tf_op jit(solution)/shard_map/pallas_call | solution.py:206
  (8 shorter events, 0.1 us)
Async XLA Ops:
  0.0 1.0 %copy-start = (bf16[16,16,4,256]{3,2,1,0:T(4,128)(2,1)S(1)}, bf16[16,16,4,256]{3,2,1,0:T(4,128)(2,1)}, u32[]{:S(2)}) copy-start(bf16[16,16,4,256]{3,2,1,0:T(4,128)(2,1)} %param.5) | copy-start | bytes 1572868
  1.0 17.6 %copy-start.3 = (bf16[16,16,3,3,3]{1,0,4,3,2:T(8,128)(2,1)S(1)}, bf16[16,16,3,3,3]{1,0,4,3,2:T(8,128)(2,1)}, u32[]{:S(2)}) copy-start(bf16[16,16,3,3,3]{1,0,4,3,2:T(8,128)(2,1)} %param.6) | copy-start | bytes 41476
  1.0 17.7 %copy-start.4 = (bf16[16,16,3,3,3]{1,0,4,3,2:T(8,128)(2,1)S(1)}, bf16[16,16,3,3,3]{1,0,4,3,2:T(8,128)(2,1)}, u32[]{:S(2)}) copy-start(bf16[16,16,3,3,3]{1,0,4,3,2:T(8,128)(2,1)} %param.7) | copy-start | bytes 41476
  1.0 17.9 %copy-start.2 = (bf16[32,32,3,3,3]{1,0,4,3,2:T(8,128)(2,1)S(1)}, bf16[32,32,3,3,3]{1,0,4,3,2:T(8,128)(2,1)}, u32[]{:S(2)}) copy-start(bf16[32,32,3,3,3]{1,0,4,3,2:T(8,128)(2,1)} %param.9) | copy-start | bytes 165892
  1.0 18.0 %copy-start.1 = (bf16[32,16,3,3,3]{0,1,4,3,2:T(8,128)(2,1)S(1)}, bf16[32,16,3,3,3]{0,1,4,3,2:T(8,128)(2,1)}, u32[]{:S(2)}) copy-start(bf16[32,16,3,3,3]{0,1,4,3,2:T(8,128)(2,1)} %param.8) | copy-start | bytes 82948
  1.6 4.5 %collective-permute-start = (bf16[4,16,256]{2,1,0:T(8,128)(2,1)S(1)}, bf16[4,16,256]{2,1,0:T(8,128)(2,1)S(1)}, u32[]{:S(2)}, u32[]{:S(2)}) collective-permute-start(bf16[4,16,256]{2,1,0:T(8,128)(2,1)S(1)} %get-tuple-element.17), channel_id=1, source_target_pairs={{0,4},{1,5},{2,6},{3,7},{4,8},{5,9},{6,10},{7,11},{8,12},{9,13},{1... | collective-permute-start | bytes 98312 | tf_op jit(solution)/shard_map/ppermute | solution.py:163
  4.6 6.0 %collective-permute-start.1 = (bf16[4,16,256]{2,1,0:T(8,128)(2,1)S(1)}, bf16[4,16,256]{2,1,0:T(8,128)(2,1)S(1)}, u32[]{:S(2)}, u32[]{:S(2)}) collective-permute-start(bf16[4,16,256]{2,1,0:T(8,128)(2,1)S(1)} %get-tuple-element.18), channel_id=1, source_target_pairs={{4,0},{5,1},{6,2},{7,3},{8,4},{9,5},{10,6},{11,7},{12,8},{13,9},{1... | collective-permute-start | bytes 98312 | tf_op jit(solution)/shard_map/ppermute | solution.py:163
  10.6 19.9 %collective-permute-start.3 = (bf16[2,288,256]{2,1,0:T(8,128)(2,1)S(1)}, bf16[2,288,256]{2,1,0:T(8,128)(2,1)S(1)}, u32[]{:S(2)}, u32[]{:S(2)}) collective-permute-start(bf16[2,288,256]{2,1,0:T(8,128)(2,1)S(1)} %get-tuple-element.19.top), channel_id=1, source_target_pairs={{1,0},{2,1},{3,2},{5,4},{6,5},{7,6},{9,8},{10,9},{11,10},{13,12},{... | collective-permute-start | bytes 884744 | tf_op jit(solution)/shard_map/ppermute | solution.py:163
  16.7 23.4 %collective-permute-start.2 = (bf16[2,288,256]{2,1,0:T(8,128)(2,1)S(1)}, bf16[2,288,256]{2,1,0:T(8,128)(2,1)S(1)}, u32[]{:S(2)}, u32[]{:S(2)}) collective-permute-start(bf16[2,288,256]{2,1,0:T(8,128)(2,1)S(1)} %get-tuple-element.20.bottom), channel_id=1, source_target_pairs={{0,1},{1,2},{2,3},{3,64},{4,5},{5,6},{6,7},{7,68},{8,9},{9,10},{10... | collective-permute-start | bytes 884744 | tf_op jit(solution)/shard_map/ppermute | solution.py:163
  44.1 6.2 %collective-permute-start.5 = (bf16[2,144,128]{2,1,0:T(8,128)(2,1)S(1)}, bf16[2,144,128]{2,1,0:T(8,128)(2,1)S(1)}, u32[]{:S(2)}, u32[]{:S(2)}) collective-permute-start(bf16[2,144,128]{2,1,0:T(8,128)(2,1)S(1)} %shard_map.58.own), channel_id=1, source_target_pairs={{1,0},{2,1},{3,2},{5,4},{6,5},{7,6},{9,8},{10,9},{11,10},{13,12},{... | collective-permute-start | bytes 221192 | tf_op jit(solution)/shard_map/ppermute | solution.py:163
  46.0 13.2 %collective-permute-start.4 = (bf16[2,144,128]{2,1,0:T(8,128)(2,1)S(1)}, bf16[2,144,128]{2,1,0:T(8,128)(2,1)S(1)}, u32[]{:S(2)}, u32[]{:S(2)}) collective-permute-start(bf16[2,144,128]{2,1,0:T(8,128)(2,1)S(1)} %shard_map.58.own), channel_id=1, source_target_pairs={{0,1},{1,2},{2,3},{3,64},{4,5},{5,6},{6,7},{7,68},{8,9},{9,10},{10... | collective-permute-start | bytes 221192 | tf_op jit(solution)/shard_map/ppermute | solution.py:163

commit v3 on v2

--- a/solution.py
+++ b/solution.py
@@ -24,24 +24,20 @@
     )
 
 
-def pack_kernel(x_ref, top, bottom, left, right, wide):
+def pack_kernel(x_ref, top, bottom, wide):
     wide[...] = x_ref[...].astype(F32)
     for r in range(4):
         image = wide[:, r, :].reshape(16, 16, COLS)
         image = jnp.transpose(image, (1, 0, 2)).reshape(256, COLS)
-        image = jnp.transpose(image, (1, 0)).astype(BF16)
-        left[r] = image[:HALO]
-        right[r] = image[COLS - HALO :]
         half = top if r < 2 else bottom
-        half[r % 2] = image
-
-
-def join_kernel(top, bottom, left, right, top_wide, bottom_wide):
-    for at, main, wide in ((0, top, top_wide), (2, bottom, bottom_wide)):
+        half[r % 2] = jnp.transpose(image, (1, 0)).astype(BF16)
+
+
+def ends_kernel(up, top, bottom, down, left, right):
+    for at, part in enumerate((up, top, bottom, down)):
         for r in range(2):
-            wide[r, :HALO] = left[at + r]
-            wide[r, HALO : HALO + COLS] = main[r]
-            wide[r, HALO + COLS :] = right[at + r]
+            left[2 * at + r] = part[r, :HALO]
+            right[2 * at + r] = part[r, COLS - HALO :]
 
 
 def one_hot(rows, lanes, of_lane):
@@ -93,9 +89,13 @@
     return tile, last_tile, gy, lax.axis_size("gy") - 1
 
 
-def fine_kernel(top, bottom, up, down, b1, b2, pooled, level, wide):
+def fine_kernel(up, top, bottom, down, left, right, b1, b2, pooled, x, level, wide):
     tile, last_tile, gy, last_gy = place()
-    x = [part[r] for part in (up, top, bottom, down) for r in range(2)]
+    for at, part in enumerate((up, top, bottom, down)):
+        for r in range(2):
+            x[2 * at + r, :HALO] = left[2 * at + r]
+            x[2 * at + r, HALO : HALO + COLS] = part[r]
+            x[2 * at + r, HALO + COLS :] = right[2 * at + r]
     for q in range(6):
         level[q] = taps([x[q], x[q + 1], x[q + 2]], b1).astype(BF16)
 
@@ -170,16 +170,13 @@
 def body(volume, w_first, w_second, w_third, w_fourth):
     sds = jax.ShapeDtypeStruct
     main = sds((2, COLS, 256), BF16)
-    ends = sds((4, HALO, 256), BF16)
-    both = sds((2, WIDE, 256), BF16)
-    top, bottom, left, right = call(
-        pack_kernel, [main, main, ends, ends], [pltpu.VMEM((256, 4, COLS), F32)], 0, 1 << 20
-    )(volume.reshape(256, 4, COLS))
+    ends = sds((8, HALO, 256), BF16)
+    top, bottom = call(pack_kernel, [main, main], [pltpu.VMEM((256, 4, COLS), F32)], 0, 1 << 20)(volume.reshape(256, 4, COLS))
+    up = shift(bottom, 1, 0)
+    down = shift(top, -1, 0)
+    left, right = call(ends_kernel, [ends, ends], [], 0, 1 << 18)(up, top, bottom, down)
     from_left = shift(right, 0, 1)
     from_right = shift(left, 0, -1)
-    top, bottom = call(join_kernel, [both, both], [], 0, 1 << 20)(top, bottom, from_left, from_right)
-    up = shift(bottom, 1, 0)
-    down = shift(top, -1, 0)
 
     b1, b2, b3, b4 = call(
         weights_kernel,
@@ -192,10 +189,10 @@
     pooled = call(
         fine_kernel,
         sds((2, HALF, 128), BF16),
-        [pltpu.VMEM((6, WIDE, 256), BF16), pltpu.VMEM((WIDE, 128), F32)],
+        [pltpu.VMEM((8, WIDE, 256), BF16), pltpu.VMEM((6, WIDE, 256), BF16), pltpu.VMEM((WIDE, 128), F32)],
         2 * 10 * WIDE * 768 * 768,
         5 << 20,
-    )(top, bottom, up, down, b1, b2)
+    )(up, top, bottom, down, from_left, from_right, b1, b2)
     up = shift(pooled, 1, 0)
     down = shift(pooled, -1, 0)
 

time: 69.7 us -> 74.1 us (1.063)
  the two profiles are of different devices: /device:TPU:384 before, /device:TPU:484 now
where the time goes in v3:
time: 74.1 us; the launch traced here: 73.8 us
  starting transfers between devices  29.9 us (40%)
  waiting for transfers between devices  25.8 us (35%)
  blocking collectives  8.36 us (11%)
  Pallas kernels  8.13 us (11%)
  local copies, waits for them, and re-layouts  1.45 us (2%)
    ppermute x6, starting transfers between devices, shift(): return lax.ppermute(cells, ('gx', 'gy', 'dev'), pairs)  29.9 us
    ppermute x6, waiting for transfers between devices, shift(): return lax.ppermute(cells, ('gx', 'gy', 'dev'), pairs)  25.8 us
    all_to_all x1, blocking collectives, body(): lax.all_to_all(parts, 'dev', split_axis=0, concat_axis=0, tiled=True)  8.36 us
    pallas_call x1, Pallas kernels, body(): call(fine_kernel, sds((2, HALF, 128), BF16), [pltpu.VMEM((8, WIDE, 256),...  3.85 us
    pallas_call x1, Pallas kernels, body(): call(weights_kernel, [sds((768, 768), BF16), sds((768, 768), BF16), sds((...  1.89 us
  transfers between devices with their start and end apart: 6, of which 3 were waited for; matrix products, arithmetic and copies ran while one was open for 1% of the time, Pallas kernels for 3%

profile of v3, /device:TPU:484, one launch (start us, length us, event | category | flops | bytes accessed | tf_op | source)
XLA Modules:
  0.0 73.8 jit_solution(5888153180627202445)
XLA Ops:
  0.0 1.0 %copy-done = bf16[16,16,4,256]{3,2,1,0:T(4,128)(2,1)S(1)} copy-done((bf16[16,16,4,256]{3,2,1,0:T(4,128)(2,1)S(1)}, bf16[16,16,4,256]{3,2,1,0:T(4,128)(2,1)}, u32[]{:S(2)}) %copy-start) | copy-done | bytes 524312
  1.1 0.6 shard_map.55
  1.6 3.5 %collective-permute-start = (bf16[2,256,256]{2,1,0:T(8,128)(2,1)S(1)}, bf16[2,256,256]{2,1,0:T(8,128)(2,1)S(1)}, u32[]{:S(2)}, u32[]{:S(2)}) collective-permute-start(bf16[2,256,256]{2,1,0:T(8,128)(2,1)S(1)} %get-tuple-element.13.bottom), channel_id=1, source_target_pairs={{0,1},{1,2},{2,3},{3,64},{4,5},{5,6},{6,7},{7,68},{8,9},{9,10},{10... | collective-permute-start | bytes 786440 | tf_op jit(solution)/shard_map/ppermute | solution.py:163
  5.1 8.1 %collective-permute-start.1 = (bf16[2,256,256]{2,1,0:T(8,128)(2,1)S(1)}, bf16[2,256,256]{2,1,0:T(8,128)(2,1)S(1)}, u32[]{:S(2)}, u32[]{:S(2)}) collective-permute-start(bf16[2,256,256]{2,1,0:T(8,128)(2,1)S(1)} %get-tuple-element.14.top), channel_id=1, source_target_pairs={{1,0},{2,1},{3,2},{5,4},{6,5},{7,6},{9,8},{10,9},{11,10},{13,12},{... | collective-permute-start | bytes 786440 | tf_op jit(solution)/shard_map/ppermute | solution.py:163
  13.2 10.7 %collective-permute-done.up = bf16[2,256,256]{2,1,0:T(8,128)(2,1)S(1)} collective-permute-done((bf16[2,256,256]{2,1,0:T(8,128)(2,1)S(1)}, bf16[2,256,256]{2,1,0:T(8,128)(2,1)S(1)}, u32[]{:S(2)}, u32[]{:S(2)}) %collective-permute-start) | collective-permute-done | bytes 262176 | tf_op jit(solution)/shard_map/ppermute | solution.py:163
  24.0 0.0 collective-permute-done.1.down
  24.0 6.0 %collective-permute-start.2 = (bf16[8,16,256]{2,1,0:T(8,128)(2,1)S(1)}, bf16[8,16,256]{2,1,0:T(8,128)(2,1)S(1)}, u32[]{:S(2)}, u32[]{:S(2)}) collective-permute-start(bf16[8,16,256]{2,1,0:T(8,128)(2,1)S(1)} %get-tuple-element.15), channel_id=1, source_target_pairs={{0,4},{1,5},{2,6},{3,7},{4,8},{5,9},{6,10},{7,11},{8,12},{9,13},{1... | collective-permute-start | bytes 196616 | tf_op jit(solution)/shard_map/ppermute | solution.py:163
  30.0 1.9 %collective-permute-start.3 = (bf16[8,16,256]{2,1,0:T(8,128)(2,1)S(1)}, bf16[8,16,256]{2,1,0:T(8,128)(2,1)S(1)}, u32[]{:S(2)}, u32[]{:S(2)}) collective-permute-start(bf16[8,16,256]{2,1,0:T(8,128)(2,1)S(1)} %get-tuple-element.16), channel_id=1, source_target_pairs={{4,0},{5,1},{6,2},{7,3},{8,4},{9,5},{10,6},{11,7},{12,8},{13,9},{1... | collective-permute-start | bytes 196616 | tf_op jit(solution)/shard_map/ppermute | solution.py:163
  32.0 0.0 copy-done.3
  32.0 0.1 copy.6
  32.1 0.1 copy.7
  32.2 0.2 copy.8
  32.4 0.0 copy-done.1
  32.4 1.9 %shard_map.57 = (bf16[768,768]{1,0:T(8,128)(2,1)S(1)}, bf16[768,768]{1,0:T(8,128)(2,1)S(1)}, bf16[384,768]{1,0:T(8,128)(2,1)S(1)}, bf16[768,768]{1,0:T(8,128)(2,1)S(1)}) custom-call(bf16[432,16]{1,0:T(8,128)(2,1)S(1)} %bitcast.13, bf16[432,16]{1,0:T(8,128)(2,1)S(1)} %bitcast.14, bf16[432,32]{1,0:T(8,128)(2,1)S(1)} %bitcast.15, bf16[864,32]{1,0:T(8,128)(2,1)S(1)} %bitcast.11), custom_call_target="tpu_custom_call" | custom-call | bytes 4194304 | tf_op jit(solution)/shard_map/pallas_call | solution.py:181
  34.3 0.0 collective-permute-done.2.left
  34.3 4.6 %collective-permute-done.3.right = bf16[8,16,256]{2,1,0:T(8,128)(2,1)S(1)} collective-permute-done((bf16[8,16,256]{2,1,0:T(8,128)(2,1)S(1)}, bf16[8,16,256]{2,1,0:T(8,128)(2,1)S(1)}, u32[]{:S(2)}, u32[]{:S(2)}) %collective-permute-start.3) | collective-permute-done | bytes 65568 | tf_op jit(solution)/shard_map/ppermute | solution.py:163
  38.9 3.8 %shard_map.58.own = bf16[2,144,128]{2,1,0:T(8,128)(2,1)S(1)} custom-call(bf16[2,256,256]{2,1,0:T(8,128)(2,1)S(1)} %collective-permute-done.up, bf16[2,256,256]{2,1,0:T(8,128)(2,1)S(1)} %get-tuple-element.14.top, bf16[2,256,256]{2,1,0:T(8,128)(2,1)S(1)} %get-tuple-element.13.bottom, bf16[2,256,256]{2,1,0:T(8,128)(2,1)S(1)} %collective-permute-done.1.down, ...), custom_call_target="tpu_custom_call" | custom-call | flops 3397386240 | bytes 5242880 | tf_op jit(solution)/shard_map/pallas_call | solution.py:189
  42.7 8.5 %collective-permute-start.5 = (bf16[2,144,128]{2,1,0:T(8,128)(2,1)S(1)}, bf16[2,144,128]{2,1,0:T(8,128)(2,1)S(1)}, u32[]{:S(2)}, u32[]{:S(2)}) collective-permute-start(bf16[2,144,128]{2,1,0:T(8,128)(2,1)S(1)} %shard_map.58.own), channel_id=1, source_target_pairs={{1,0},{2,1},{3,2},{5,4},{6,5},{7,6},{9,8},{10,9},{11,10},{13,12},{... | collective-permute-start | bytes 221192 | tf_op jit(solution)/shard_map/ppermute | solution.py:163
  51.2 1.9 %collective-permute-start.4 = (bf16[2,144,128]{2,1,0:T(8,128)(2,1)S(1)}, bf16[2,144,128]{2,1,0:T(8,128)(2,1)S(1)}, u32[]{:S(2)}, u32[]{:S(2)}) collective-permute-start(bf16[2,144,128]{2,1,0:T(8,128)(2,1)S(1)} %shard_map.58.own), channel_id=1, source_target_pairs={{0,1},{1,2},{2,3},{3,64},{4,5},{5,6},{6,7},{7,68},{8,9},{9,10},{10... | collective-permute-start | bytes 221192 | tf_op jit(solution)/shard_map/ppermute | solution.py:163
  53.1 0.0 collective-permute-done.5.down
  53.2 10.4 %collective-permute-done.4.up = bf16[2,144,128]{2,1,0:T(8,128)(2,1)S(1)} collective-permute-done((bf16[2,144,128]{2,1,0:T(8,128)(2,1)S(1)}, bf16[2,144,128]{2,1,0:T(8,128)(2,1)S(1)}, u32[]{:S(2)}, u32[]{:S(2)}) %collective-permute-start.4) | collective-permute-done | bytes 73760 | tf_op jit(solution)/shard_map/ppermute | solution.py:163
  63.6 1.1 %shard_map.59 = bf16[4,2,64,128]{3,2,1,0:T(8,128)(2,1)S(1)} custom-call(bf16[2,144,128]{2,1,0:T(8,128)(2,1)S(1)} %shard_map.58.own, bf16[2,144,128]{2,1,0:T(8,128)(2,1)S(1)} %collective-permute-done.4.up, bf16[2,144,128]{2,1,0:T(8,128)(2,1)S(1)} %collective-permute-done.5.down, bf16[384,768]{1,0:T(8,128)(2,1)S(1)} %get-tuple-element.19.b3, ...), custom_call_target="tpu_custom_call" | custom-call | flops 679477248 | bytes 2097152 | tf_op jit(solution)/shard_map/pallas_call | solution.py:199
  64.7 8.4 %all_to_all.5.parts = bf16[4,2,64,128]{3,2,1,0:T(8,128)(2,1)S(1)} all-to-all(bf16[4,2,64,128]{3,2,1,0:T(8,128)(2,1)S(1)} %shard_map.59), channel_id=1, replica_groups=mesh['gx'=8,'gy'=16,'dev'=4] {'dev'}, dimensions={0} | all-to-all | bytes 262144 | tf_op jit(solution)/shard_map/all_to_all | solution.py:202
  73.0 0.7 shard_map.60
  (8 shorter events, 0.0 us)
Async XLA Ops:
  0.0 1.0 %copy-start = (bf16[16,16,4,256]{3,2,1,0:T(4,128)(2,1)S(1)}, bf16[16,16,4,256]{3,2,1,0:T(4,128)(2,1)}, u32[]{:S(2)}) copy-start(bf16[16,16,4,256]{3,2,1,0:T(4,128)(2,1)} %param.5) | copy-start | bytes 1572868
  1.0 30.9 %copy-start.3 = (bf16[16,16,3,3,3]{1,0,4,3,2:T(8,128)(2,1)S(1)}, bf16[16,16,3,3,3]{1,0,4,3,2:T(8,128)(2,1)}, u32[]{:S(2)}) copy-start(bf16[16,16,3,3,3]{1,0,4,3,2:T(8,128)(2,1)} %param.6) | copy-start | bytes 41476
  1.0 31.1 %copy-start.4 = (bf16[16,16,3,3,3]{1,0,4,3,2:T(8,128)(2,1)S(1)}, bf16[16,16,3,3,3]{1,0,4,3,2:T(8,128)(2,1)}, u32[]{:S(2)}) copy-start(bf16[16,16,3,3,3]{1,0,4,3,2:T(8,128)(2,1)} %param.7) | copy-start | bytes 41476
  1.0 31.2 %copy-start.2 = (bf16[32,32,3,3,3]{1,0,4,3,2:T(8,128)(2,1)S(1)}, bf16[32,32,3,3,3]{1,0,4,3,2:T(8,128)(2,1)}, u32[]{:S(2)}) copy-start(bf16[32,32,3,3,3]{1,0,4,3,2:T(8,128)(2,1)} %param.9) | copy-start | bytes 165892
  1.0 31.4 %copy-start.1 = (bf16[32,16,3,3,3]{0,1,4,3,2:T(8,128)(2,1)S(1)}, bf16[32,16,3,3,3]{0,1,4,3,2:T(8,128)(2,1)}, u32[]{:S(2)}) copy-start(bf16[32,16,3,3,3]{0,1,4,3,2:T(8,128)(2,1)} %param.8) | copy-start | bytes 82948
  1.6 22.3 %collective-permute-start = (bf16[2,256,256]{2,1,0:T(8,128)(2,1)S(1)}, bf16[2,256,256]{2,1,0:T(8,128)(2,1)S(1)}, u32[]{:S(2)}, u32[]{:S(2)}) collective-permute-start(bf16[2,256,256]{2,1,0:T(8,128)(2,1)S(1)} %get-tuple-element.13.bottom), channel_id=1, source_target_pairs={{0,1},{1,2},{2,3},{3,64},{4,5},{5,6},{6,7},{7,68},{8,9},{9,10},{10... | collective-permute-start | bytes 786440 | tf_op jit(solution)/shard_map/ppermute | solution.py:163
  5.1 18.8 %collective-permute-start.1 = (bf16[2,256,256]{2,1,0:T(8,128)(2,1)S(1)}, bf16[2,256,256]{2,1,0:T(8,128)(2,1)S(1)}, u32[]{:S(2)}, u32[]{:S(2)}) collective-permute-start(bf16[2,256,256]{2,1,0:T(8,128)(2,1)S(1)} %get-tuple-element.14.top), channel_id=1, source_target_pairs={{1,0},{2,1},{3,2},{5,4},{6,5},{7,6},{9,8},{10,9},{11,10},{13,12},{... | collective-permute-start | bytes 786440 | tf_op jit(solution)/shard_map/ppermute | solution.py:163
  24.0 10.3 %collective-permute-start.2 = (bf16[8,16,256]{2,1,0:T(8,128)(2,1)S(1)}, bf16[8,16,256]{2,1,0:T(8,128)(2,1)S(1)}, u32[]{:S(2)}, u32[]{:S(2)}) collective-permute-start(bf16[8,16,256]{2,1,0:T(8,128)(2,1)S(1)} %get-tuple-element.15), channel_id=1, source_target_pairs={{0,4},{1,5},{2,6},{3,7},{4,8},{5,9},{6,10},{7,11},{8,12},{9,13},{1... | collective-permute-start | bytes 196616 | tf_op jit(solution)/shard_map/ppermute | solution.py:163
  30.0 8.9 %collective-permute-start.3 = (bf16[8,16,256]{2,1,0:T(8,128)(2,1)S(1)}, bf16[8,16,256]{2,1,0:T(8,128)(2,1)S(1)}, u32[]{:S(2)}, u32[]{:S(2)}) collective-permute-start(bf16[8,16,256]{2,1,0:T(8,128)(2,1)S(1)} %get-tuple-element.16), channel_id=1, source_target_pairs={{4,0},{5,1},{6,2},{7,3},{8,4},{9,5},{10,6},{11,7},{12,8},{13,9},{1... | collective-permute-start | bytes 196616 | tf_op jit(solution)/shard_map/ppermute | solution.py:163
  42.7 10.4 %collective-permute-start.5 = (bf16[2,144,128]{2,1,0:T(8,128)(2,1)S(1)}, bf16[2,144,128]{2,1,0:T(8,128)(2,1)S(1)}, u32[]{:S(2)}, u32[]{:S(2)}) collective-permute-start(bf16[2,144,128]{2,1,0:T(8,128)(2,1)S(1)} %shard_map.58.own), channel_id=1, source_target_pairs={{1,0},{2,1},{3,2},{5,4},{6,5},{7,6},{9,8},{10,9},{11,10},{13,12},{... | collective-permute-start | bytes 221192 | tf_op jit(solution)/shard_map/ppermute | solution.py:163
  51.2 12.4 %collective-permute-start.4 = (bf16[2,144,128]{2,1,0:T(8,128)(2,1)S(1)}, bf16[2,144,128]{2,1,0:T(8,128)(2,1)S(1)}, u32[]{:S(2)}, u32[]{:S(2)}) collective-permute-start(bf16[2,144,128]{2,1,0:T(8,128)(2,1)S(1)} %shard_map.58.own), channel_id=1, source_target_pairs={{0,1},{1,2},{2,3},{3,64},{4,5},{5,6},{6,7},{7,68},{8,9},{9,10},{10... | collective-permute-start | bytes 221192 | tf_op jit(solution)/shard_map/ppermute | solution.py:163

commit v4 on v3

--- a/solution.py
+++ b/solution.py
@@ -24,20 +24,30 @@
     )
 
 
-def pack_kernel(x_ref, top, bottom, wide):
+def pack_kernel(x_ref, to_a, to_b, wide, images):
     wide[...] = x_ref[...].astype(F32)
     for r in range(4):
         image = wide[:, r, :].reshape(16, 16, COLS)
         image = jnp.transpose(image, (1, 0, 2)).reshape(256, COLS)
-        half = top if r < 2 else bottom
-        half[r % 2] = jnp.transpose(image, (1, 0)).astype(BF16)
-
-
-def ends_kernel(up, top, bottom, down, left, right):
-    for at, part in enumerate((up, top, bottom, down)):
+        images[r] = jnp.transpose(image, (1, 0)).astype(BF16)
+    odd = lax.axis_index("dev") % 2
+    to_a[...] = images[pl.ds(2 - 2 * odd, 2)]
+    to_b[...] = images[pl.ds(2 * odd, 2)]
+
+
+def row_parts(from_a, from_b, to_a, to_b):
+    odd = lax.axis_index("dev") % 2
+    return ((6 - 6 * odd, from_a), (6 * odd, from_b), (4 - 2 * odd, to_a), (2 + 2 * odd, to_b))
+
+
+def ends_kernel(from_b, from_a, to_a, to_b, after, to_c, to_d, ends):
+    for at, part in row_parts(from_a, from_b, to_a, to_b):
         for r in range(2):
-            left[2 * at + r] = part[r, :HALO]
-            right[2 * at + r] = part[r, COLS - HALO :]
+            ends[0, at + r] = part[r, :HALO]
+            ends[1, at + r] = part[r, COLS - HALO :]
+    odd = lax.axis_index("gy") % 2
+    to_c[...] = ends[1 - odd]
+    to_d[...] = ends[odd]
 
 
 def one_hot(rows, lanes, of_lane):
@@ -89,45 +99,79 @@
     return tile, last_tile, gy, lax.axis_size("gy") - 1
 
 
-def fine_kernel(up, top, bottom, down, left, right, b1, b2, pooled, x, level, wide):
+def halved(cells, wide):
+    size = cells.shape[0]
+    wide[0:size, :] = jnp.maximum(cells[:, :128], cells[:, 128:])
+    return jnp.maximum(wide[pl.ds(0, size // 2, stride=2), :], wide[pl.ds(1, size // 2, stride=2), :])
+
+
+def centre_kernel(from_b, from_a, to_a, to_b, b1, b2, pooled, x, level, wide):
     tile, last_tile, gy, last_gy = place()
-    for at, part in enumerate((up, top, bottom, down)):
-        for r in range(2):
-            x[2 * at + r, :HALO] = left[2 * at + r]
-            x[2 * at + r, HALO : HALO + COLS] = part[r]
-            x[2 * at + r, HALO + COLS :] = right[2 * at + r]
+    for at, part in row_parts(from_a, from_b, to_a, to_b):
+        x[pl.ds(at, 2)] = part[...]
     for q in range(6):
         level[q] = taps([x[q], x[q + 1], x[q + 2]], b1).astype(BF16)
 
-    @pl.when(gy == 0)
-    def _():
-        level[:, :HALO] = jnp.zeros((6, HALO, 256), BF16)
-
-    @pl.when(gy == last_gy)
-    def _():
-        level[:, HALO + COLS :] = jnp.zeros((6, HALO, 256), BF16)
-
     @pl.when(tile == 0)
     def _():
-        level[0] = jnp.zeros((WIDE, 256), BF16)
+        level[0] = jnp.zeros((COLS, 256), BF16)
 
     @pl.when(tile == last_tile)
     def _():
-        level[5] = jnp.zeros((WIDE, 256), BF16)
-
-    col = lax.broadcasted_iota(jnp.int32, (HALF, 128), 0)
-    inside = ((col >= HALO // 2) | (gy > 0)) & ((col < HALF - HALO // 2) | (gy < last_gy))
+        level[5] = jnp.zeros((COLS, 256), BF16)
+
     for pair in range(2):
         two = [taps([level[q], level[q + 1], level[q + 2]], b2) for q in (2 * pair, 2 * pair + 1)]
-        both = jnp.maximum(two[0], two[1])
-        wide[...] = jnp.maximum(both[:, :128], both[:, 128:])
-        most = jnp.maximum(wide[pl.ds(0, HALF, stride=2), :], wide[pl.ds(1, HALF, stride=2), :])
-        pooled[pair] = jnp.where(inside, most, 0.0).astype(BF16)
-
-
-def coarse_kernel(own, up, down, b3, b4, parts, level):
+        pooled[pair] = halved(jnp.maximum(two[0], two[1]), wide)
+
+
+def strips_kernel(from_d, from_c, to_c, to_d, centre, b1, b2, pooled, x, level, wide):
     tile, last_tile, gy, last_gy = place()
-    x = [part[r] for part in (up, own, down) for r in range(2)]
+    odd = gy % 2
+    x[3 - 3 * odd] = from_c[...]
+    x[3 * odd] = from_d[...]
+    x[2 - odd] = to_c[...]
+    x[1 + odd] = to_d[...]
+    rows = jnp.concatenate([x[part, r] for r in range(8) for part in range(4)], axis=0)
+    level[...] = taps([rows[0:384], rows[64:448], rows[128:512]], b1).astype(BF16)
+    for q in range(6):
+
+        @pl.when(gy == 0)
+        def _():
+            level[64 * q : 64 * q + 16] = jnp.zeros((16, 256), BF16)
+
+        @pl.when(gy == last_gy)
+        def _():
+            level[64 * q + 48 : 64 * q + 64] = jnp.zeros((16, 256), BF16)
+
+    @pl.when(tile == 0)
+    def _():
+        level[0:64] = jnp.zeros((64, 256), BF16)
+
+    @pl.when(tile == last_tile)
+    def _():
+        level[320:384] = jnp.zeros((64, 256), BF16)
+
+    two = taps([level[0:256], level[64:320], level[128:384]], b2)
+    col = lax.broadcasted_iota(jnp.int32, (32, 128), 0)
+    inside = ((col >= 8) | (gy > 0)) & ((col < 24) | (gy < last_gy))
+    outer = lax.broadcasted_iota(jnp.int32, (8, 128), 0) < 4
+    for pair in range(2):
+        at = 128 * pair
+        strip = halved(jnp.maximum(two[at : at + 64], two[at + 64 : at + 128]), wide)
+        strip = jnp.where(inside, strip, 0.0)
+        main = centre[pair]
+        low = jnp.where(outer, strip[8:16], main[0:8])
+        high = jnp.where(outer, main[120:128], strip[16:24])
+        pooled[pair] = jnp.concatenate([strip[0:8], low, main[8:120], high, strip[24:32]], axis=0).astype(BF16)
+
+
+def coarse_kernel(own, from_b, from_a, b3, b4, parts, x, level):
+    tile, last_tile, gy, last_gy = place()
+    odd = lax.axis_index("dev") % 2
+    x[2:4] = own[...]
+    x[pl.ds(4 - 4 * odd, 2)] = from_a[...]
+    x[pl.ds(4 * odd, 2)] = from_b[...]
     col = lax.broadcasted_iota(jnp.int32, (HALF, 256), 0)
     inside = ((col >= HALO // 2) | (gy > 0)) & ((col < HALF - HALO // 2) | (gy < last_gy))
     for q in range(4):
@@ -150,17 +194,21 @@
     out[...] = wide[...].astype(BF16)
 
 
-def shift(cells, row_step, col_step):
+def swap_rows(cells, first):
     groups, col_tiles, devs = (lax.axis_size(axis) for axis in ("gx", "gy", "dev"))
     pairs = []
-    for g in range(groups):
+    for low in range(first, groups * devs - 1, 2):
         for t in range(col_tiles):
-            for d in range(devs):
-                tile, col_tile = g * devs + d + row_step, t + col_step
-                if 0 <= tile < groups * devs and 0 <= col_tile < col_tiles:
-                    target = ((tile // devs) * col_tiles + col_tile) * devs + tile % devs
-                    pairs.append(((g * col_tiles + t) * devs + d, target))
+            one, two = (((tile // devs) * col_tiles + t) * devs + tile % devs for tile in (low, low + 1))
+            pairs += [(one, two), (two, one)]
     return lax.ppermute(cells, ("gx", "gy", "dev"), pairs)
+
+
+def swap_cols(cells, first):
+    pairs = []
+    for low in range(first, lax.axis_size("gy") - 1, 2):
+        pairs += [(low, low + 1), (low + 1, low)]
+    return lax.ppermute(cells, "gy", pairs)
 
 
 def by_tap(weight):
@@ -171,12 +219,11 @@
     sds = jax.ShapeDtypeStruct
     main = sds((2, COLS, 256), BF16)
     ends = sds((8, HALO, 256), BF16)
-    top, bottom = call(pack_kernel, [main, main], [pltpu.VMEM((256, 4, COLS), F32)], 0, 1 << 20)(volume.reshape(256, 4, COLS))
-    up = shift(bottom, 1, 0)
-    down = shift(top, -1, 0)
-    left, right = call(ends_kernel, [ends, ends], [], 0, 1 << 18)(up, top, bottom, down)
-    from_left = shift(right, 0, 1)
-    from_right = shift(left, 0, -1)
+    to_a, to_b = call(
+        pack_kernel, [main, main], [pltpu.VMEM((256, 4, COLS), F32), pltpu.VMEM((4, COLS, 256), BF16)], 0, 1 << 20
+    )(volume.reshape(256, 4, COLS))
+    from_b = swap_rows(to_b, 1)
+    from_a = swap_rows(to_a, 0)
 
     b1, b2, b3, b4 = call(
         weights_kernel,
@@ -186,19 +233,31 @@
         4 << 20,
     )(by_tap(w_first), by_tap(w_second), by_tap(w_third), by_tap(w_fourth))
 
+    to_c, to_d = call(ends_kernel, [ends, ends], [pltpu.VMEM((2, 8, HALO, 256), BF16)], 0, 1 << 18)(
+        from_b, from_a, to_a, to_b, b3
+    )
+    from_d = swap_cols(to_d, 1)
+    from_c = swap_cols(to_c, 0)
+    centre = call(
+        centre_kernel,
+        sds((2, 128, 128), F32),
+        [pltpu.VMEM((8, COLS, 256), BF16), pltpu.VMEM((6, COLS, 256), BF16), pltpu.VMEM((COLS, 128), F32)],
+        2 * 10 * COLS * 768 * 768,
+        5 << 20,
+    )(from_b, from_a, to_a, to_b, b1, b2)
     pooled = call(
-        fine_kernel,
+        strips_kernel,
         sds((2, HALF, 128), BF16),
-        [pltpu.VMEM((8, WIDE, 256), BF16), pltpu.VMEM((6, WIDE, 256), BF16), pltpu.VMEM((WIDE, 128), F32)],
-        2 * 10 * WIDE * 768 * 768,
-        5 << 20,
-    )(up, top, bottom, down, from_left, from_right, b1, b2)
-    up = shift(pooled, 1, 0)
-    down = shift(pooled, -1, 0)
+        [pltpu.VMEM((4, 8, HALO, 256), BF16), pltpu.VMEM((384, 256), BF16), pltpu.VMEM((64, 128), F32)],
+        2 * 640 * 768 * 768,
+        4 << 20,
+    )(from_d, from_c, to_c, to_d, centre, b1, b2)
+    from_b = swap_rows(pooled, 1)
+    from_a = swap_rows(pooled, 0)
 
     parts = call(
-        coarse_kernel, sds((4, 2, 64, 128), BF16), [pltpu.VMEM((4, HALF, 256), BF16)], 2 * 4 * HALF * 768 * 768, 2 << 20
-    )(pooled, up, down, b3, b4)
+        coarse_kernel, sds((4, 2, 64, 128), BF16), [pltpu.VMEM((6, HALF, 128), BF16), pltpu.VMEM((4, HALF, 256), BF16)], 2 * 4 * HALF * 768 * 768, 2 << 20
+    )(pooled, from_b, from_a, b3, b4)
     parts = lax.all_to_all(parts, "dev", split_axis=0, concat_axis=0, tiled=True)
     out = call(last_kernel, sds((512, 128), BF16), [pltpu.VMEM((512, 128), F32)], 0, 1 << 18)(parts)
     return out.reshape(32, 2, 8, 128)

time: 74.1 us -> 62.1 us (0.84)
  the two profiles are of different devices: /device:TPU:484 before, /device:TPU:7 now
where the time goes in v4:
time: 62.1 us; the launch traced here: 61.8 us
  starting transfers between devices  23.8 us (38%)
  blocking collectives  20.5 us (33%)
  Pallas kernels  9.33 us (15%)
  waiting for transfers between devices  4.73 us (8%)
  local copies, waits for them, and re-layouts  3.26 us (5%)
    all_to_all x1, blocking collectives, body(): lax.all_to_all(parts, 'dev', split_axis=0, concat_axis=0, tiled=True)  20.5 us
    ppermute x4, starting transfers between devices, swap_rows(): return lax.ppermute(cells, ('gx', 'gy', 'dev'), pairs)  15.4 us
    ppermute x2, starting transfers between devices, swap_cols(): return lax.ppermute(cells, 'gy', pairs)  8.44 us
    ppermute x4, waiting for transfers between devices, swap_rows(): return lax.ppermute(cells, ('gx', 'gy', 'dev'), pairs)  4.54 us
    pallas_call x1, Pallas kernels, body(): call(centre_kernel, sds((2, 128, 128), F32), [pltpu.VMEM((8, COLS, 256),...  3.56 us
    transpose x3, local copies, waits for them, and re-layouts, by_tap(): jnp.transpose(weight, (2, 3, 4, 1, 0))  2.21 us
    pallas_call x1, Pallas kernels, body(): call(weights_kernel, [sds((768, 768), BF16), sds((768, 768), BF16), sds((...  1.89 us
    pallas_call x1, Pallas kernels, body(): call(strips_kernel, sds((2, HALF, 128), BF16), [pltpu.VMEM((4, 8, HALO, 2...  1.39 us
  transfers between devices with their start and end apart: 6, of which 3 were waited for; matrix products, arithmetic and copies ran while one was open for 4% of the time, Pallas kernels for 9%

profile of v4, /device:TPU:7, one launch (start us, length us, event | category | flops | bytes accessed | tf_op | source)
XLA Modules:
  0.0 61.8 jit_solution(6626235491405441295)
XLA Ops:
  0.0 1.0 %copy-done = bf16[16,16,4,256]{3,2,1,0:T(4,128)(2,1)S(1)} copy-done((bf16[16,16,4,256]{3,2,1,0:T(4,128)(2,1)S(1)}, bf16[16,16,4,256]{3,2,1,0:T(4,128)(2,1)}, u32[]{:S(2)}) %copy-start) | copy-done | bytes 524312
  1.0 0.7 %shard_map.55 = (bf16[2,256,256]{2,1,0:T(8,128)(2,1)S(1)}, bf16[2,256,256]{2,1,0:T(8,128)(2,1)S(1)}) custom-call(bf16[256,4,256]{2,1,0:T(4,128)(2,1)S(1)} %bitcast.12), custom_call_target="tpu_custom_call" | custom-call | bytes 1048576 | tf_op jit(solution)/shard_map/pallas_call | solution.py:222
  1.7 5.2 %collective-permute-start = (bf16[2,256,256]{2,1,0:T(8,128)(2,1)S(1)}, bf16[2,256,256]{2,1,0:T(8,128)(2,1)S(1)}, u32[]{:S(2)}, u32[]{:S(2)}) collective-permute-start(bf16[2,256,256]{2,1,0:T(8,128)(2,1)S(1)} %get-tuple-element.13.to_b), channel_id=1, source_target_pairs={{1,2},{2,1},{5,6},{6,5},{9,10},{10,9},{13,14},{14,13},{17,18},{18,... | collective-permute-start | bytes 786440 | tf_op jit(solution)/shard_map/ppermute | solution.py:204
  6.9 1.9 %collective-permute-start.1 = (bf16[2,256,256]{2,1,0:T(8,128)(2,1)S(1)}, bf16[2,256,256]{2,1,0:T(8,128)(2,1)S(1)}, u32[]{:S(2)}, u32[]{:S(2)}) collective-permute-start(bf16[2,256,256]{2,1,0:T(8,128)(2,1)S(1)} %get-tuple-element.14.to_a), channel_id=1, source_target_pairs={{0,1},{1,0},{4,5},{5,4},{8,9},{9,8},{12,13},{13,12},{16,17},{17,16... | collective-permute-start | bytes 786440 | tf_op jit(solution)/shard_map/ppermute | solution.py:204
  8.8 1.1 %copy.8 = bf16[3,3,3,32,32]{4,3,2,1,0:T(8,128)(2,1)S(1)} copy(bf16[3,3,3,32,32]{3,4,2,1,0:T(8,128)(2,1)} %bitcast.16) | data formatting | bytes 110592 | tf_op jit(solution)/shard_map/transpose | solution.py:215
  9.9 1.0 %copy.6 = bf16[3,3,3,16,16]{4,3,2,1,0:T(8,128)(2,1)S(1)} copy(bf16[3,3,3,16,16]{3,4,2,1,0:T(8,128)(2,1)} %bitcast.17) | data formatting | bytes 27648 | tf_op jit(solution)/shard_map/transpose | solution.py:215
  11.0 0.0 copy-done.2
  11.0 0.1 copy.7
  11.1 1.9 %shard_map.56 = (bf16[768,768]{1,0:T(8,128)(2,1)S(1)}, bf16[768,768]{1,0:T(8,128)(2,1)S(1)}, bf16[384,768]{1,0:T(8,128)(2,1)S(1)}, bf16[768,768]{1,0:T(8,128)(2,1)S(1)}) custom-call(bf16[432,16]{1,0:T(8,128)(2,1)S(1)} %bitcast.13, bf16[432,16]{1,0:T(8,128)(2,1)S(1)} %bitcast.14, bf16[432,32]{1,0:T(8,128)(2,1)S(1)} %bitcast.15, bf16[864,32]{1,0:T(8,128)(2,1)S(1)} %bitcast.11), custom_call_target="tpu_custom_call" | custom-call | bytes 4194304 | tf_op jit(solution)/shard_map/pallas_call | solution.py:228
  13.0 0.0 collective-permute-done.from_b
  13.0 2.8 %collective-permute-done.1.from_a = bf16[2,256,256]{2,1,0:T(8,128)(2,1)S(1)} collective-permute-done((bf16[2,256,256]{2,1,0:T(8,128)(2,1)S(1)}, bf16[2,256,256]{2,1,0:T(8,128)(2,1)S(1)}, u32[]{:S(2)}, u32[]{:S(2)}) %collective-permute-start.1) | collective-permute-done | bytes 262176 | tf_op jit(solution)/shard_map/ppermute | solution.py:204
  15.9 6.5 %collective-permute-start.2 = (bf16[8,16,256]{2,1,0:T(8,128)(2,1)S(1)}, bf16[8,16,256]{2,1,0:T(8,128)(2,1)S(1)}, u32[]{:S(2)}, u32[]{:S(2)}) collective-permute-start(bf16[8,16,256]{2,1,0:T(8,128)(2,1)S(1)} %get-tuple-element.16.to_d), channel_id=1, source_target_pairs={{4,8},{8,4},{12,16},{16,12},{20,24},{24,20},{28,32},{32,28},{36,40... | collective-permute-start | bytes 196616 | tf_op jit(solution)/shard_map/ppermute | solution.py:211
  22.4 1.9 %collective-permute-start.3 = (bf16[8,16,256]{2,1,0:T(8,128)(2,1)S(1)}, bf16[8,16,256]{2,1,0:T(8,128)(2,1)S(1)}, u32[]{:S(2)}, u32[]{:S(2)}) collective-permute-start(bf16[8,16,256]{2,1,0:T(8,128)(2,1)S(1)} %get-tuple-element.17.to_c), channel_id=1, source_target_pairs={{0,4},{4,0},{8,12},{12,8},{16,20},{20,16},{24,28},{28,24},{32,36},... | collective-permute-start | bytes 196616 | tf_op jit(solution)/shard_map/ppermute | solution.py:211
  24.3 3.6 %shard_map.58.centre = f32[2,128,128]{2,1,0:T(8,128)S(1)} custom-call(bf16[2,256,256]{2,1,0:T(8,128)(2,1)S(1)} %collective-permute-done.from_b, bf16[2,256,256]{2,1,0:T(8,128)(2,1)S(1)} %collective-permute-done.1.from_a, bf16[2,256,256]{2,1,0:T(8,128)(2,1)S(1)} %get-tuple-element.14.to_a, bf16[2,256,256]{2,1,0:T(8,128)(2,1)S(1)} %get-tuple-element.13.to_b, ...), custom_call_target="tpu_custom_call" | custom-call | flops 3019898880 | bytes 5242880 | tf_op jit(solution)/shard_map/pallas_call | solution.py:241
  27.9 0.0 collective-permute-done.2.from_d
  27.9 0.2 collective-permute-done.3.from_c
  28.1 1.4 %shard_map.59.own = bf16[2,144,128]{2,1,0:T(8,128)(2,1)S(1)} custom-call(bf16[8,16,256]{2,1,0:T(8,128)(2,1)S(1)} %collective-permute-done.2.from_d, bf16[8,16,256]{2,1,0:T(8,128)(2,1)S(1)} %collective-permute-done.3.from_c, bf16[8,16,256]{2,1,0:T(8,128)(2,1)S(1)} %get-tuple-element.17.to_c, bf16[8,16,256]{2,1,0:T(8,128)(2,1)S(1)} %get-tuple-element.16.to_d, ...), custom_call_target="tpu_custom_call" | custom-call | flops 754974720 | bytes 4194304 | tf_op jit(solution)/shard_map/pallas_call | solution.py:248
  29.5 2.0 %collective-permute-start.4 = (bf16[2,144,128]{2,1,0:T(8,128)(2,1)S(1)}, bf16[2,144,128]{2,1,0:T(8,128)(2,1)S(1)}, u32[]{:S(2)}, u32[]{:S(2)}) collective-permute-start(bf16[2,144,128]{2,1,0:T(8,128)(2,1)S(1)} %shard_map.59.own), channel_id=1, source_target_pairs={{1,2},{2,1},{5,6},{6,5},{9,10},{10,9},{13,14},{14,13},{17,18},{18,... | collective-permute-start | bytes 221192 | tf_op jit(solution)/shard_map/ppermute | solution.py:204
  31.5 6.2 %collective-permute-start.5 = (bf16[2,144,128]{2,1,0:T(8,128)(2,1)S(1)}, bf16[2,144,128]{2,1,0:T(8,128)(2,1)S(1)}, u32[]{:S(2)}, u32[]{:S(2)}) collective-permute-start(bf16[2,144,128]{2,1,0:T(8,128)(2,1)S(1)} %shard_map.59.own), channel_id=1, source_target_pairs={{0,1},{1,0},{4,5},{5,4},{8,9},{9,8},{12,13},{13,12},{16,17},{17,16... | collective-permute-start | bytes 221192 | tf_op jit(solution)/shard_map/ppermute | solution.py:204
  37.7 0.0 collective-permute-done.4.from_b
  37.8 1.7 %collective-permute-done.5.from_a = bf16[2,144,128]{2,1,0:T(8,128)(2,1)S(1)} collective-permute-done((bf16[2,144,128]{2,1,0:T(8,128)(2,1)S(1)}, bf16[2,144,128]{2,1,0:T(8,128)(2,1)S(1)}, u32[]{:S(2)}, u32[]{:S(2)}) %collective-permute-start.5) | collective-permute-done | bytes 73760 | tf_op jit(solution)/shard_map/ppermute | solution.py:204
  39.5 1.1 %shard_map.60 = bf16[4,2,64,128]{3,2,1,0:T(8,128)(2,1)S(1)} custom-call(bf16[2,144,128]{2,1,0:T(8,128)(2,1)S(1)} %shard_map.59.own, bf16[2,144,128]{2,1,0:T(8,128)(2,1)S(1)} %collective-permute-done.4.from_b, bf16[2,144,128]{2,1,0:T(8,128)(2,1)S(1)} %collective-permute-done.5.from_a, bf16[384,768]{1,0:T(8,128)(2,1)S(1)} %get-tuple-element.15.after.b3, ...), custom_call_target="tpu_custom_call" | custom-call | flops 679477248 | bytes 2097152 | tf_op jit(solution)/shard_map/pallas_call | solution.py:258
  40.5 20.5 %all_to_all.5.parts = bf16[4,2,64,128]{3,2,1,0:T(8,128)(2,1)S(1)} all-to-all(bf16[4,2,64,128]{3,2,1,0:T(8,128)(2,1)S(1)} %shard_map.60), channel_id=1, replica_groups=mesh['gx'=8,'gy'=16,'dev'=4] {'dev'}, dimensions={0} | all-to-all | bytes 262144 | tf_op jit(solution)/shard_map/all_to_all | solution.py:261
  61.0 0.7 %shard_map.61 = bf16[512,128]{1,0:T(8,128)(2,1)} custom-call(bf16[4,2,64,128]{3,2,1,0:T(8,128)(2,1)S(1)} %all_to_all.5.parts), custom_call_target="tpu_custom_call" | custom-call | bytes 262144 | tf_op jit(solution)/shard_map/pallas_call | solution.py:262
  (5 shorter events, 0.0 us)
Async XLA Ops:
  0.0 1.0 %copy-start = (bf16[16,16,4,256]{3,2,1,0:T(4,128)(2,1)S(1)}, bf16[16,16,4,256]{3,2,1,0:T(4,128)(2,1)}, u32[]{:S(2)}) copy-start(bf16[16,16,4,256]{3,2,1,0:T(4,128)(2,1)} %param.5) | copy-start | bytes 1572868
  1.0 9.9 %copy-start.2 = (bf16[16,16,3,3,3]{1,0,4,3,2:T(8,128)(2,1)S(1)}, bf16[16,16,3,3,3]{1,0,4,3,2:T(8,128)(2,1)}, u32[]{:S(2)}) copy-start(bf16[16,16,3,3,3]{1,0,4,3,2:T(8,128)(2,1)} %param.7) | copy-start | bytes 41476
  1.0 10.0 %copy-start.1 = (bf16[32,16,3,3,3]{0,1,4,3,2:T(8,128)(2,1)S(1)}, bf16[32,16,3,3,3]{0,1,4,3,2:T(8,128)(2,1)}, u32[]{:S(2)}) copy-start(bf16[32,16,3,3,3]{0,1,4,3,2:T(8,128)(2,1)} %param.8) | copy-start | bytes 82948
  1.7 11.3 %collective-permute-start = (bf16[2,256,256]{2,1,0:T(8,128)(2,1)S(1)}, bf16[2,256,256]{2,1,0:T(8,128)(2,1)S(1)}, u32[]{:S(2)}, u32[]{:S(2)}) collective-permute-start(bf16[2,256,256]{2,1,0:T(8,128)(2,1)S(1)} %get-tuple-element.13.to_b), channel_id=1, source_target_pairs={{1,2},{2,1},{5,6},{6,5},{9,10},{10,9},{13,14},{14,13},{17,18},{18,... | collective-permute-start | bytes 786440 | tf_op jit(solution)/shard_map/ppermute | solution.py:204
  6.9 8.9 %collective-permute-start.1 = (bf16[2,256,256]{2,1,0:T(8,128)(2,1)S(1)}, bf16[2,256,256]{2,1,0:T(8,128)(2,1)S(1)}, u32[]{:S(2)}, u32[]{:S(2)}) collective-permute-start(bf16[2,256,256]{2,1,0:T(8,128)(2,1)S(1)} %get-tuple-element.14.to_a), channel_id=1, source_target_pairs={{0,1},{1,0},{4,5},{5,4},{8,9},{9,8},{12,13},{13,12},{16,17},{17,16... | collective-permute-start | bytes 786440 | tf_op jit(solution)/shard_map/ppermute | solution.py:204
  15.9 12.0 %collective-permute-start.2 = (bf16[8,16,256]{2,1,0:T(8,128)(2,1)S(1)}, bf16[8,16,256]{2,1,0:T(8,128)(2,1)S(1)}, u32[]{:S(2)}, u32[]{:S(2)}) collective-permute-start(bf16[8,16,256]{2,1,0:T(8,128)(2,1)S(1)} %get-tuple-element.16.to_d), channel_id=1, source_target_pairs={{4,8},{8,4},{12,16},{16,12},{20,24},{24,20},{28,32},{32,28},{36,40... | collective-permute-start | bytes 196616 | tf_op jit(solution)/shard_map/ppermute | solution.py:211
  22.4 5.7 %collective-permute-start.3 = (bf16[8,16,256]{2,1,0:T(8,128)(2,1)S(1)}, bf16[8,16,256]{2,1,0:T(8,128)(2,1)S(1)}, u32[]{:S(2)}, u32[]{:S(2)}) collective-permute-start(bf16[8,16,256]{2,1,0:T(8,128)(2,1)S(1)} %get-tuple-element.17.to_c), channel_id=1, source_target_pairs={{0,4},{4,0},{8,12},{12,8},{16,20},{20,16},{24,28},{28,24},{32,36},... | collective-permute-start | bytes 196616 | tf_op jit(solution)/shard_map/ppermute | solution.py:211
  29.5 8.3 %collective-permute-start.4 = (bf16[2,144,128]{2,1,0:T(8,128)(2,1)S(1)}, bf16[2,144,128]{2,1,0:T(8,128)(2,1)S(1)}, u32[]{:S(2)}, u32[]{:S(2)}) collective-permute-start(bf16[2,144,128]{2,1,0:T(8,128)(2,1)S(1)} %shard_map.59.own), channel_id=1, source_target_pairs={{1,2},{2,1},{5,6},{6,5},{9,10},{10,9},{13,14},{14,13},{17,18},{18,... | collective-permute-start | bytes 221192 | tf_op jit(solution)/shard_map/ppermute | solution.py:204
  31.5 8.0 %collective-permute-start.5 = (bf16[2,144,128]{2,1,0:T(8,128)(2,1)S(1)}, bf16[2,144,128]{2,1,0:T(8,128)(2,1)S(1)}, u32[]{:S(2)}, u32[]{:S(2)}) collective-permute-start(bf16[2,144,128]{2,1,0:T(8,128)(2,1)S(1)} %shard_map.59.own), channel_id=1, source_target_pairs={{0,1},{1,0},{4,5},{5,4},{8,9},{9,8},{12,13},{13,12},{16,17},{17,16... | collective-permute-start | bytes 221192 | tf_op jit(solution)/shard_map/ppermute | solution.py:204

commit v5 on v4

--- a/solution.py
+++ b/solution.py
@@ -42,9 +42,10 @@
 
 def ends_kernel(from_b, from_a, to_a, to_b, after, to_c, to_d, ends):
     for at, part in row_parts(from_a, from_b, to_a, to_b):
-        for r in range(2):
-            ends[0, at + r] = part[r, :HALO]
-            ends[1, at + r] = part[r, COLS - HALO :]
+        low = [part[r, :16].astype(F32)[:8] for r in range(2)]
+        high = [part[r, COLS - 16 :].astype(F32)[8:] for r in range(2)]
+        ends[0, at // 2] = jnp.concatenate(low, axis=0).astype(BF16)
+        ends[1, at // 2] = jnp.concatenate(high, axis=0).astype(BF16)
     odd = lax.axis_index("gy") % 2
     to_c[...] = ends[1 - odd]
     to_d[...] = ends[odd]
@@ -125,45 +126,39 @@
         pooled[pair] = halved(jnp.maximum(two[0], two[1]), wide)
 
 
-def strips_kernel(from_d, from_c, to_c, to_d, centre, b1, b2, pooled, x, level, wide):
+def strips_kernel(from_d, from_c, to_c, to_d, centre, b1, b2, pooled, x, wide):
     tile, last_tile, gy, last_gy = place()
     odd = gy % 2
     x[3 - 3 * odd] = from_c[...]
     x[3 * odd] = from_d[...]
     x[2 - odd] = to_c[...]
     x[1 + odd] = to_d[...]
-    rows = jnp.concatenate([x[part, r] for r in range(8) for part in range(4)], axis=0)
-    level[...] = taps([rows[0:384], rows[64:448], rows[128:512]], b1).astype(BF16)
-    for q in range(6):
-
-        @pl.when(gy == 0)
-        def _():
-            level[64 * q : 64 * q + 16] = jnp.zeros((16, 256), BF16)
-
-        @pl.when(gy == last_gy)
-        def _():
-            level[64 * q + 48 : 64 * q + 64] = jnp.zeros((16, 256), BF16)
-
-    @pl.when(tile == 0)
-    def _():
-        level[0:64] = jnp.zeros((64, 256), BF16)
-
-    @pl.when(tile == last_tile)
-    def _():
-        level[320:384] = jnp.zeros((64, 256), BF16)
-
-    two = taps([level[0:256], level[64:320], level[128:384]], b2)
-    col = lax.broadcasted_iota(jnp.int32, (32, 128), 0)
-    inside = ((col >= 8) | (gy > 0)) & ((col < 24) | (gy < last_gy))
-    outer = lax.broadcasted_iota(jnp.int32, (8, 128), 0) < 4
+    pieces = []
+    for two in range(4):
+        parts = [x[part, two].astype(F32) for part in range(4)]
+        pieces += [part[8 * r : 8 * r + 8] for r in range(2) for part in parts]
+    rows = jnp.concatenate(pieces, axis=0).astype(BF16)
+    level = taps([rows[0:192], rows[32:224], rows[64:256]], b1)
+    at = lax.broadcasted_iota(jnp.int32, (192, 256), 0)
+    col = at % 32
+    keep = ((col >= 8) | (gy > 0)) & ((col < 24) | (gy < last_gy))
+    keep = keep & ((at >= 32) | (tile > 0)) & ((at < 160) | (tile < last_tile))
+    level = jnp.where(keep, level, 0.0).astype(BF16)
+    two = taps([level[0:128], level[32:160], level[64:192]], b2)
+    row = lax.broadcasted_iota(jnp.int32, (8, 128), 0)
     for pair in range(2):
-        at = 128 * pair
-        strip = halved(jnp.maximum(two[at : at + 64], two[at + 64 : at + 128]), wide)
-        strip = jnp.where(inside, strip, 0.0)
+        at = 64 * pair
+        strip = halved(jnp.maximum(two[at : at + 32], two[at + 32 : at + 64]), wide)
+        low, high = pltpu.roll(strip[0:8], 4, 0), pltpu.roll(strip[8:16], 4, 0)
         main = centre[pair]
-        low = jnp.where(outer, strip[8:16], main[0:8])
-        high = jnp.where(outer, main[120:128], strip[16:24])
-        pooled[pair] = jnp.concatenate([strip[0:8], low, main[8:120], high, strip[24:32]], axis=0).astype(BF16)
+        parts = [
+            jnp.where(gy > 0, low, 0.0),
+            jnp.where(row < 2, low, main[0:8]),
+            main[8:120],
+            jnp.where(row < 6, main[120:128], high),
+            jnp.where(gy < last_gy, high, 0.0),
+        ]
+        pooled[pair] = jnp.concatenate(parts, axis=0).astype(BF16)
 
 
 def coarse_kernel(own, from_b, from_a, b3, b4, parts, x, level):
@@ -218,7 +213,7 @@
 def body(volume, w_first, w_second, w_third, w_fourth):
     sds = jax.ShapeDtypeStruct
     main = sds((2, COLS, 256), BF16)
-    ends = sds((8, HALO, 256), BF16)
+    ends = sds((4, 16, 256), BF16)
     to_a, to_b = call(
         pack_kernel, [main, main], [pltpu.VMEM((256, 4, COLS), F32), pltpu.VMEM((4, COLS, 256), BF16)], 0, 1 << 20
     )(volume.reshape(256, 4, COLS))
@@ -233,7 +228,7 @@
         4 << 20,
     )(by_tap(w_first), by_tap(w_second), by_tap(w_third), by_tap(w_fourth))
 
-    to_c, to_d = call(ends_kernel, [ends, ends], [pltpu.VMEM((2, 8, HALO, 256), BF16)], 0, 1 << 18)(
+    to_c, to_d = call(ends_kernel, [ends, ends], [pltpu.VMEM((2, 4, 16, 256), BF16)], 0, 1 << 18)(
         from_b, from_a, to_a, to_b, b3
     )
     from_d = swap_cols(to_d, 1)
@@ -248,8 +243,8 @@
     pooled = call(
         strips_kernel,
         sds((2, HALF, 128), BF16),
-        [pltpu.VMEM((4, 8, HALO, 256), BF16), pltpu.VMEM((384, 256), BF16), pltpu.VMEM((64, 128), F32)],
-        2 * 640 * 768 * 768,
+        [pltpu.VMEM((4, 4, 16, 256), BF16), pltpu.VMEM((32, 128), F32)],
+        2 * 320 * 768 * 768,
         4 << 20,
     )(from_d, from_c, to_c, to_d, centre, b1, b2)
     from_b = swap_rows(pooled, 1)

time: 62.1 us -> 61.2 us (0.986)
  transfers between devices with their start and end apart: 6 -> 6, of which waited for: 3 -> 2; matrix products, arithmetic and copies ran while one was open for 4% -> 4% of each run, Pallas kernels for 9% -> 9%
where the time goes in v5:
time: 61.2 us; the launch traced here: 60.9 us
  starting transfers between devices  24 us (39%)
  blocking collectives  20.1 us (33%)
  Pallas kernels  8.77 us (14%)
  waiting for transfers between devices  4.55 us (7%)
  local copies, waits for them, and re-layouts  3.26 us (5%)
    all_to_all x1, blocking collectives, body(): lax.all_to_all(parts, 'dev', split_axis=0, concat_axis=0, tiled=True)  20.1 us
    ppermute x4, starting transfers between devices, swap_rows(): return lax.ppermute(cells, ('gx', 'gy', 'dev'), pairs)  15.6 us
    ppermute x2, starting transfers between devices, swap_cols(): return lax.ppermute(cells, 'gy', pairs)  8.44 us
    ppermute x4, waiting for transfers between devices, swap_rows(): return lax.ppermute(cells, ('gx', 'gy', 'dev'), pairs)  4.54 us
    pallas_call x1, Pallas kernels, body(): call(centre_kernel, sds((2, 128, 128), F32), [pltpu.VMEM((8, COLS, 256),...  3.56 us
    transpose x3, local copies, waits for them, and re-layouts, by_tap(): jnp.transpose(weight, (2, 3, 4, 1, 0))  2.21 us
    pallas_call x1, Pallas kernels, body(): call(weights_kernel, [sds((768, 768), BF16), sds((768, 768), BF16), sds((...  1.89 us
  transfers between devices with their start and end apart: 6, of which 2 were waited for; matrix products, arithmetic and copies ran while one was open for 4% of the time, Pallas kernels for 9%

profile of v5, /device:TPU:7, one launch (start us, length us, event | category | flops | bytes accessed | tf_op | source)
XLA Modules:
  0.0 60.9 jit_solution(8273771901064881450)
XLA Ops:
  0.0 1.0 %copy-done = bf16[16,16,4,256]{3,2,1,0:T(4,128)(2,1)S(1)} copy-done((bf16[16,16,4,256]{3,2,1,0:T(4,128)(2,1)S(1)}, bf16[16,16,4,256]{3,2,1,0:T(4,128)(2,1)}, u32[]{:S(2)}) %copy-start) | copy-done | bytes 524312
  1.0 0.7 %shard_map.55 = (bf16[2,256,256]{2,1,0:T(8,128)(2,1)S(1)}, bf16[2,256,256]{2,1,0:T(8,128)(2,1)S(1)}) custom-call(bf16[256,4,256]{2,1,0:T(4,128)(2,1)S(1)} %bitcast.12), custom_call_target="tpu_custom_call" | custom-call | bytes 1048576 | tf_op jit(solution)/shard_map/pallas_call | solution.py:217
  1.7 5.2 %collective-permute-start = (bf16[2,256,256]{2,1,0:T(8,128)(2,1)S(1)}, bf16[2,256,256]{2,1,0:T(8,128)(2,1)S(1)}, u32[]{:S(2)}, u32[]{:S(2)}) collective-permute-start(bf16[2,256,256]{2,1,0:T(8,128)(2,1)S(1)} %get-tuple-element.13.to_b), channel_id=1, source_target_pairs={{1,2},{2,1},{5,6},{6,5},{9,10},{10,9},{13,14},{14,13},{17,18},{18,... | collective-permute-start | bytes 786440 | tf_op jit(solution)/shard_map/ppermute | solution.py:199
  6.9 1.9 %collective-permute-start.1 = (bf16[2,256,256]{2,1,0:T(8,128)(2,1)S(1)}, bf16[2,256,256]{2,1,0:T(8,128)(2,1)S(1)}, u32[]{:S(2)}, u32[]{:S(2)}) collective-permute-start(bf16[2,256,256]{2,1,0:T(8,128)(2,1)S(1)} %get-tuple-element.14.to_a), channel_id=1, source_target_pairs={{0,1},{1,0},{4,5},{5,4},{8,9},{9,8},{12,13},{13,12},{16,17},{17,16... | collective-permute-start | bytes 786440 | tf_op jit(solution)/shard_map/ppermute | solution.py:199
  8.8 1.1 %copy.8 = bf16[3,3,3,32,32]{4,3,2,1,0:T(8,128)(2,1)S(1)} copy(bf16[3,3,3,32,32]{3,4,2,1,0:T(8,128)(2,1)} %bitcast.16) | data formatting | bytes 110592 | tf_op jit(solution)/shard_map/transpose | solution.py:210
  9.9 1.0 %copy.6 = bf16[3,3,3,16,16]{4,3,2,1,0:T(8,128)(2,1)S(1)} copy(bf16[3,3,3,16,16]{3,4,2,1,0:T(8,128)(2,1)} %bitcast.17) | data formatting | bytes 27648 | tf_op jit(solution)/shard_map/transpose | solution.py:210
  11.0 0.0 copy-done.2
  11.0 0.1 copy.7
  11.1 1.9 %shard_map.56 = (bf16[768,768]{1,0:T(8,128)(2,1)S(1)}, bf16[768,768]{1,0:T(8,128)(2,1)S(1)}, bf16[384,768]{1,0:T(8,128)(2,1)S(1)}, bf16[768,768]{1,0:T(8,128)(2,1)S(1)}) custom-call(bf16[432,16]{1,0:T(8,128)(2,1)S(1)} %bitcast.13, bf16[432,16]{1,0:T(8,128)(2,1)S(1)} %bitcast.14, bf16[432,32]{1,0:T(8,128)(2,1)S(1)} %bitcast.15, bf16[864,32]{1,0:T(8,128)(2,1)S(1)} %bitcast.11), custom_call_target="tpu_custom_call" | custom-call | bytes 4194304 | tf_op jit(solution)/shard_map/pallas_call | solution.py:223
  13.0 0.0 collective-permute-done.from_b
  13.0 2.8 %collective-permute-done.1.from_a = bf16[2,256,256]{2,1,0:T(8,128)(2,1)S(1)} collective-permute-done((bf16[2,256,256]{2,1,0:T(8,128)(2,1)S(1)}, bf16[2,256,256]{2,1,0:T(8,128)(2,1)S(1)}, u32[]{:S(2)}, u32[]{:S(2)}) %collective-permute-start.1) | collective-permute-done | bytes 262176 | tf_op jit(solution)/shard_map/ppermute | solution.py:199
  15.8 6.5 %collective-permute-start.2 = (bf16[4,16,256]{2,1,0:T(8,128)(2,1)S(1)}, bf16[4,16,256]{2,1,0:T(8,128)(2,1)S(1)}, u32[]{:S(2)}, u32[]{:S(2)}) collective-permute-start(bf16[4,16,256]{2,1,0:T(8,128)(2,1)S(1)} %get-tuple-element.16.to_d), channel_id=1, source_target_pairs={{4,8},{8,4},{12,16},{16,12},{20,24},{24,20},{28,32},{32,28},{36,40... | collective-permute-start | bytes 98312 | tf_op jit(solution)/shard_map/ppermute | solution.py:206
  22.4 1.9 %collective-permute-start.3 = (bf16[4,16,256]{2,1,0:T(8,128)(2,1)S(1)}, bf16[4,16,256]{2,1,0:T(8,128)(2,1)S(1)}, u32[]{:S(2)}, u32[]{:S(2)}) collective-permute-start(bf16[4,16,256]{2,1,0:T(8,128)(2,1)S(1)} %get-tuple-element.17.to_c), channel_id=1, source_target_pairs={{0,4},{4,0},{8,12},{12,8},{16,20},{20,16},{24,28},{28,24},{32,36},... | collective-permute-start | bytes 98312 | tf_op jit(solution)/shard_map/ppermute | solution.py:206
  24.3 3.6 %shard_map.58.centre = f32[2,128,128]{2,1,0:T(8,128)S(1)} custom-call(bf16[2,256,256]{2,1,0:T(8,128)(2,1)S(1)} %collective-permute-done.from_b, bf16[2,256,256]{2,1,0:T(8,128)(2,1)S(1)} %collective-permute-done.1.from_a, bf16[2,256,256]{2,1,0:T(8,128)(2,1)S(1)} %get-tuple-element.14.to_a, bf16[2,256,256]{2,1,0:T(8,128)(2,1)S(1)} %get-tuple-element.13.to_b, ...), custom_call_target="tpu_custom_call" | custom-call | flops 3019898880 | bytes 5242880 | tf_op jit(solution)/shard_map/pallas_call | solution.py:236
  27.9 0.0 collective-permute-done.2.from_d
  27.9 0.0 collective-permute-done.3.from_c
  27.9 0.8 %shard_map.59.own = bf16[2,144,128]{2,1,0:T(8,128)(2,1)S(1)} custom-call(bf16[4,16,256]{2,1,0:T(8,128)(2,1)S(1)} %collective-permute-done.2.from_d, bf16[4,16,256]{2,1,0:T(8,128)(2,1)S(1)} %collective-permute-done.3.from_c, bf16[4,16,256]{2,1,0:T(8,128)(2,1)S(1)} %get-tuple-element.17.to_c, bf16[4,16,256]{2,1,0:T(8,128)(2,1)S(1)} %get-tuple-element.16.to_d, ...), custom_call_target="tpu_custom_call" | custom-call | flops 377487360 | bytes 4194304 | tf_op jit(solution)/shard_map/pallas_call | solution.py:243
  28.7 1.9 %collective-permute-start.4 = (bf16[2,144,128]{2,1,0:T(8,128)(2,1)S(1)}, bf16[2,144,128]{2,1,0:T(8,128)(2,1)S(1)}, u32[]{:S(2)}, u32[]{:S(2)}) collective-permute-start(bf16[2,144,128]{2,1,0:T(8,128)(2,1)S(1)} %shard_map.59.own), channel_id=1, source_target_pairs={{1,2},{2,1},{5,6},{6,5},{9,10},{10,9},{13,14},{14,13},{17,18},{18,... | collective-permute-start | bytes 221192 | tf_op jit(solution)/shard_map/ppermute | solution.py:199
  30.7 6.5 %collective-permute-start.5 = (bf16[2,144,128]{2,1,0:T(8,128)(2,1)S(1)}, bf16[2,144,128]{2,1,0:T(8,128)(2,1)S(1)}, u32[]{:S(2)}, u32[]{:S(2)}) collective-permute-start(bf16[2,144,128]{2,1,0:T(8,128)(2,1)S(1)} %shard_map.59.own), channel_id=1, source_target_pairs={{0,1},{1,0},{4,5},{5,4},{8,9},{9,8},{12,13},{13,12},{16,17},{17,16... | collective-permute-start | bytes 221192 | tf_op jit(solution)/shard_map/ppermute | solution.py:199
  37.2 0.0 collective-permute-done.4.from_b
  37.2 1.7 %collective-permute-done.5.from_a = bf16[2,144,128]{2,1,0:T(8,128)(2,1)S(1)} collective-permute-done((bf16[2,144,128]{2,1,0:T(8,128)(2,1)S(1)}, bf16[2,144,128]{2,1,0:T(8,128)(2,1)S(1)}, u32[]{:S(2)}, u32[]{:S(2)}) %collective-permute-start.5) | collective-permute-done | bytes 73760 | tf_op jit(solution)/shard_map/ppermute | solution.py:199
  38.9 1.1 %shard_map.60 = bf16[4,2,64,128]{3,2,1,0:T(8,128)(2,1)S(1)} custom-call(bf16[2,144,128]{2,1,0:T(8,128)(2,1)S(1)} %shard_map.59.own, bf16[2,144,128]{2,1,0:T(8,128)(2,1)S(1)} %collective-permute-done.4.from_b, bf16[2,144,128]{2,1,0:T(8,128)(2,1)S(1)} %collective-permute-done.5.from_a, bf16[384,768]{1,0:T(8,128)(2,1)S(1)} %get-tuple-element.15.after.b3, ...), custom_call_target="tpu_custom_call" | custom-call | flops 679477248 | bytes 2097152 | tf_op jit(solution)/shard_map/pallas_call | solution.py:253
  40.0 20.1 %all_to_all.5.parts = bf16[4,2,64,128]{3,2,1,0:T(8,128)(2,1)S(1)} all-to-all(bf16[4,2,64,128]{3,2,1,0:T(8,128)(2,1)S(1)} %shard_map.60), channel_id=1, replica_groups=mesh['gx'=8,'gy'=16,'dev'=4] {'dev'}, dimensions={0} | all-to-all | bytes 262144 | tf_op jit(solution)/shard_map/all_to_all | solution.py:256
  60.1 0.7 %shard_map.61 = bf16[512,128]{1,0:T(8,128)(2,1)} custom-call(bf16[4,2,64,128]{3,2,1,0:T(8,128)(2,1)S(1)} %all_to_all.5.parts), custom_call_target="tpu_custom_call" | custom-call | bytes 262144 | tf_op jit(solution)/shard_map/pallas_call | solution.py:257
  (5 shorter events, 0.0 us)
Async XLA Ops:
  0.0 1.0 %copy-start = (bf16[16,16,4,256]{3,2,1,0:T(4,128)(2,1)S(1)}, bf16[16,16,4,256]{3,2,1,0:T(4,128)(2,1)}, u32[]{:S(2)}) copy-start(bf16[16,16,4,256]{3,2,1,0:T(4,128)(2,1)} %param.5) | copy-start | bytes 1572868
  1.0 9.9 %copy-start.2 = (bf16[16,16,3,3,3]{1,0,4,3,2:T(8,128)(2,1)S(1)}, bf16[16,16,3,3,3]{1,0,4,3,2:T(8,128)(2,1)}, u32[]{:S(2)}) copy-start(bf16[16,16,3,3,3]{1,0,4,3,2:T(8,128)(2,1)} %param.7) | copy-start | bytes 41476
  1.0 10.0 %copy-start.1 = (bf16[32,16,3,3,3]{0,1,4,3,2:T(8,128)(2,1)S(1)}, bf16[32,16,3,3,3]{0,1,4,3,2:T(8,128)(2,1)}, u32[]{:S(2)}) copy-start(bf16[32,16,3,3,3]{0,1,4,3,2:T(8,128)(2,1)} %param.8) | copy-start | bytes 82948
  1.7 11.3 %collective-permute-start = (bf16[2,256,256]{2,1,0:T(8,128)(2,1)S(1)}, bf16[2,256,256]{2,1,0:T(8,128)(2,1)S(1)}, u32[]{:S(2)}, u32[]{:S(2)}) collective-permute-start(bf16[2,256,256]{2,1,0:T(8,128)(2,1)S(1)} %get-tuple-element.13.to_b), channel_id=1, source_target_pairs={{1,2},{2,1},{5,6},{6,5},{9,10},{10,9},{13,14},{14,13},{17,18},{18,... | collective-permute-start | bytes 786440 | tf_op jit(solution)/shard_map/ppermute | solution.py:199
  6.9 8.9 %collective-permute-start.1 = (bf16[2,256,256]{2,1,0:T(8,128)(2,1)S(1)}, bf16[2,256,256]{2,1,0:T(8,128)(2,1)S(1)}, u32[]{:S(2)}, u32[]{:S(2)}) collective-permute-start(bf16[2,256,256]{2,1,0:T(8,128)(2,1)S(1)} %get-tuple-element.14.to_a), channel_id=1, source_target_pairs={{0,1},{1,0},{4,5},{5,4},{8,9},{9,8},{12,13},{13,12},{16,17},{17,16... | collective-permute-start | bytes 786440 | tf_op jit(solution)/shard_map/ppermute | solution.py:199
  15.8 12.0 %collective-permute-start.2 = (bf16[4,16,256]{2,1,0:T(8,128)(2,1)S(1)}, bf16[4,16,256]{2,1,0:T(8,128)(2,1)S(1)}, u32[]{:S(2)}, u32[]{:S(2)}) collective-permute-start(bf16[4,16,256]{2,1,0:T(8,128)(2,1)S(1)} %get-tuple-element.16.to_d), channel_id=1, source_target_pairs={{4,8},{8,4},{12,16},{16,12},{20,24},{24,20},{28,32},{32,28},{36,40... | collective-permute-start | bytes 98312 | tf_op jit(solution)/shard_map/ppermute | solution.py:206
  22.4 5.5 %collective-permute-start.3 = (bf16[4,16,256]{2,1,0:T(8,128)(2,1)S(1)}, bf16[4,16,256]{2,1,0:T(8,128)(2,1)S(1)}, u32[]{:S(2)}, u32[]{:S(2)}) collective-permute-start(bf16[4,16,256]{2,1,0:T(8,128)(2,1)S(1)} %get-tuple-element.17.to_c), channel_id=1, source_target_pairs={{0,4},{4,0},{8,12},{12,8},{16,20},{20,16},{24,28},{28,24},{32,36},... | collective-permute-start | bytes 98312 | tf_op jit(solution)/shard_map/ppermute | solution.py:206
  28.7 8.5 %collective-permute-start.4 = (bf16[2,144,128]{2,1,0:T(8,128)(2,1)S(1)}, bf16[2,144,128]{2,1,0:T(8,128)(2,1)S(1)}, u32[]{:S(2)}, u32[]{:S(2)}) collective-permute-start(bf16[2,144,128]{2,1,0:T(8,128)(2,1)S(1)} %shard_map.59.own), channel_id=1, source_target_pairs={{1,2},{2,1},{5,6},{6,5},{9,10},{10,9},{13,14},{14,13},{17,18},{18,... | collective-permute-start | bytes 221192 | tf_op jit(solution)/shard_map/ppermute | solution.py:199
  30.7 8.3 %collective-permute-start.5 = (bf16[2,144,128]{2,1,0:T(8,128)(2,1)S(1)}, bf16[2,144,128]{2,1,0:T(8,128)(2,1)S(1)}, u32[]{:S(2)}, u32[]{:S(2)}) collective-permute-start(bf16[2,144,128]{2,1,0:T(8,128)(2,1)S(1)} %shard_map.59.own), channel_id=1, source_target_pairs={{0,1},{1,0},{4,5},{5,4},{8,9},{9,8},{12,13},{13,12},{16,17},{17,16... | collective-permute-start | bytes 221192 | tf_op jit(solution)/shard_map/ppermute | solution.py:199

commit v6 on v5

--- a/solution.py
+++ b/solution.py
@@ -81,8 +81,14 @@
     band(w1, b1, 16, 16, 16, 256, lambda n: n % 16, lambda n: n // 16, same)
     band(w2, b2, 16, 16, 16, 256, lambda n: n % 16, lambda n: 2 * ((n // 16) % 8) + n // 128, same)
 
-    band(w3, b3, 16, 32, 8, 256, lambda n: n % 32, lambda n: n // 32, same)
-    band(w4, b4, 32, 32, 8, 256, lambda n: (n % 64) // 2, lambda n: 2 * (n // 64) + n % 2, same)
+    dev = lax.axis_index("dev")
+
+    def near(zin, z):
+        at = 2 * dev - 1 + z
+        return jnp.where((at >= 0) & (at < 8), zin - at + 1, -1)
+
+    band(w3, b3, 16, 32, 8, 128, lambda n: n % 32, lambda n: n // 32, near)
+    band(w4, b4, 32, 32, 4, 128, lambda n: n // 2, lambda n: n % 2, lambda zin, z: zin - z)
 
 
 def taps(rows, band_ref):
@@ -158,34 +164,54 @@
             jnp.where(row < 6, main[120:128], high),
             jnp.where(gy < last_gy, high, 0.0),
         ]
-        pooled[pair] = jnp.concatenate(parts, axis=0).astype(BF16)
-
-
-def coarse_kernel(own, from_b, from_a, b3, b4, parts, x, level):
-    tile, last_tile, gy, last_gy = place()
-    odd = lax.axis_index("dev") % 2
-    x[2:4] = own[...]
-    x[pl.ds(4 - 4 * odd, 2)] = from_a[...]
-    x[pl.ds(4 * odd, 2)] = from_b[...]
-    col = lax.broadcasted_iota(jnp.int32, (HALF, 256), 0)
-    inside = ((col >= HALO // 2) | (gy > 0)) & ((col < HALF - HALO // 2) | (gy < last_gy))
+        done = jnp.concatenate(parts, axis=0).astype(BF16)
+        for copy in range(4):
+            pooled[copy, pair] = done
+
+
+def edges_kernel(group, to_a, to_b):
+    odd = lax.axis_index("gx") % 2
+    to_a[...] = group[3 - 3 * odd]
+    to_b[...] = group[3 * odd]
+
+
+def coarse_row(rows, b3, keep):
+    gy, last_gy = lax.axis_index("gy"), lax.axis_size("gy") - 1
+    col = lax.broadcasted_iota(jnp.int32, (HALF, 128), 0)
+    inside = ((col >= HALO // 2) | (gy > 0)) & ((col < HALF - HALO // 2) | (gy < last_gy)) & keep
+    return jnp.where(inside, taps(rows, b3), 0.0).astype(BF16)
+
+
+def feature_row(rows, b4):
+    features = taps(rows, b4)
+    return jnp.transpose(features[HALO // 2 : HALO // 2 + 128], (1, 0))[:64]
+
+
+def inner_kernel(group, b3, b4, level, turned):
+    x = [group[part, r] for part in range(4) for r in range(2)]
+    for q in range(6):
+        level[q] = coarse_row([x[q], x[q + 1], x[q + 2]], b3, True)
     for q in range(4):
-        keep = inside
-        if q == 0:
-            keep = keep & (tile > 0)
-        if q == 3:
-            keep = keep & (tile < last_tile)
-        level[q] = jnp.where(keep, taps([x[q], x[q + 1], x[q + 2]], b3), 0.0).astype(BF16)
+        turned[q] = feature_row([level[q], level[q + 1], level[q + 2]], b4)
+
+
+def outer_kernel(from_b, from_a, group, inner, turned, b3, b4, out, x, level, wide):
+    gx = lax.axis_index("gx")
+    odd = gx % 2
+    x[pl.ds(2 - 2 * odd, 2)] = from_a[...]
+    x[pl.ds(2 * odd, 2)] = from_b[...]
+    above = [x[0], x[1], group[0, 0], group[0, 1]]
+    below = [group[3, 0], group[3, 1], x[2], x[3]]
     for q in range(2):
-        features = taps([level[q], level[q + 1], level[q + 2]], b4)
-        turned = jnp.transpose(features[HALO // 2 : HALO // 2 + 128], (1, 0))
-        for part in range(4):
-            parts[part, q] = turned[part * 64 : (part + 1) * 64].astype(BF16)
-
-
-def last_kernel(parts, out, wide):
-    for r in range(8):
-        wide[pl.ds(r, 64, stride=8), :] = parts[r // 2, r % 2].astype(F32)
+        level[q] = coarse_row(above[q : q + 3], b3, (gx > 0) | (q > 0))
+        level[2 + q] = coarse_row(below[q : q + 3], b3, (gx < lax.axis_size("gx") - 1) | (q < 1))
+    above = [level[0], level[1], inner[0], inner[1]]
+    below = [inner[4], inner[5], level[2], level[3]]
+    for q in range(2):
+        wide[pl.ds(q, 64, stride=8), :] = feature_row(above[q : q + 3], b4)
+        wide[pl.ds(6 + q, 64, stride=8), :] = feature_row(below[q : q + 3], b4)
+    for q in range(4):
+        wide[pl.ds(2 + q, 64, stride=8), :] = turned[q]
     out[...] = wide[...].astype(BF16)
 
 
@@ -199,11 +225,11 @@
     return lax.ppermute(cells, ("gx", "gy", "dev"), pairs)
 
 
-def swap_cols(cells, first):
+def swap(cells, axis, first):
     pairs = []
-    for low in range(first, lax.axis_size("gy") - 1, 2):
+    for low in range(first, lax.axis_size(axis) - 1, 2):
         pairs += [(low, low + 1), (low + 1, low)]
-    return lax.ppermute(cells, "gy", pairs)
+    return lax.ppermute(cells, axis, pairs)
 
 
 def by_tap(weight):
@@ -222,7 +248,7 @@
 
     b1, b2, b3, b4 = call(
         weights_kernel,
-        [sds((768, 768), BF16), sds((768, 768), BF16), sds((384, 768), BF16), sds((768, 768), BF16)],
+        [sds((768, 768), BF16), sds((768, 768), BF16), sds((384, 384), BF16), sds((384, 384), BF16)],
         [],
         0,
         4 << 20,
@@ -231,8 +257,8 @@
     to_c, to_d = call(ends_kernel, [ends, ends], [pltpu.VMEM((2, 4, 16, 256), BF16)], 0, 1 << 18)(
         from_b, from_a, to_a, to_b, b3
     )
-    from_d = swap_cols(to_d, 1)
-    from_c = swap_cols(to_c, 0)
+    from_d = swap(to_d, "gy", 1)
+    from_c = swap(to_c, "gy", 0)
     centre = call(
         centre_kernel,
         sds((2, 128, 128), F32),
@@ -240,21 +266,28 @@
         2 * 10 * COLS * 768 * 768,
         5 << 20,
     )(from_b, from_a, to_a, to_b, b1, b2)
-    pooled = call(
+    group = call(
         strips_kernel,
-        sds((2, HALF, 128), BF16),
+        sds((4, 2, HALF, 128), BF16),
         [pltpu.VMEM((4, 4, 16, 256), BF16), pltpu.VMEM((32, 128), F32)],
         2 * 320 * 768 * 768,
         4 << 20,
     )(from_d, from_c, to_c, to_d, centre, b1, b2)
-    from_b = swap_rows(pooled, 1)
-    from_a = swap_rows(pooled, 0)
-
-    parts = call(
-        coarse_kernel, sds((4, 2, 64, 128), BF16), [pltpu.VMEM((6, HALF, 128), BF16), pltpu.VMEM((4, HALF, 256), BF16)], 2 * 4 * HALF * 768 * 768, 2 << 20
-    )(pooled, from_b, from_a, b3, b4)
-    parts = lax.all_to_all(parts, "dev", split_axis=0, concat_axis=0, tiled=True)
-    out = call(last_kernel, sds((512, 128), BF16), [pltpu.VMEM((512, 128), F32)], 0, 1 << 18)(parts)
+    group = lax.all_to_all(group, "dev", split_axis=0, concat_axis=0, tiled=True)
+    edge = sds((2, HALF, 128), BF16)
+    to_a, to_b = call(edges_kernel, [edge, edge], [], 0, 1 << 18)(group)
+    from_b = swap(to_b, "gx", 1)
+    from_a = swap(to_a, "gx", 0)
+    inner, turned = call(
+        inner_kernel, [sds((6, HALF, 128), BF16), sds((4, 64, 128), F32)], [], 2 * 10 * HALF * 384 * 384, 1 << 20
+    )(group, b3, b4)
+    out = call(
+        outer_kernel,
+        sds((512, 128), BF16),
+        [pltpu.VMEM((4, HALF, 128), BF16), pltpu.VMEM((4, HALF, 128), BF16), pltpu.VMEM((512, 128), F32)],
+        2 * 8 * HALF * 384 * 384,
+        1 << 20,
+    )(from_b, from_a, group, inner, turned, b3, b4)
     return out.reshape(32, 2, 8, 128)
 
 

time: 61.2 us -> 61 us (level)
  the two profiles are of different devices: /device:TPU:7 before, /device:TPU:3 now
where the time goes in v6:
time: 61 us; the launch traced here: 60.6 us
  starting transfers between devices  28.5 us (47%)
  blocking collectives  14.8 us (24%)
  Pallas kernels  9.09 us (15%)
  waiting for transfers between devices  4.74 us (8%)
  local copies, waits for them, and re-layouts  3.26 us (5%)
    ppermute x4, starting transfers between devices, swap(): return lax.ppermute(cells, axis, pairs)  21.4 us
    all_to_all x1, blocking collectives, body(): lax.all_to_all(group, 'dev', split_axis=0, concat_axis=0, tiled=True)  14.8 us
    ppermute x2, starting transfers between devices, swap_rows(): return lax.ppermute(cells, ('gx', 'gy', 'dev'), pairs)  7.12 us
    pallas_call x1, Pallas kernels, body(): call(centre_kernel, sds((2, 128, 128), F32), [pltpu.VMEM((8, COLS, 256),...  3.51 us
    ppermute x2, waiting for transfers between devices, swap_rows(): return lax.ppermute(cells, ('gx', 'gy', 'dev'), pairs)  3.25 us
    transpose x3, local copies, waits for them, and re-layouts, by_tap(): jnp.transpose(weight, (2, 3, 4, 1, 0))  2.21 us
    pallas_call x1, Pallas kernels, body(): call(outer_kernel, sds((512, 128), BF16), [pltpu.VMEM((4, HALF, 128), BF1...  1.6 us
    ppermute x4, waiting for transfers between devices, swap(): return lax.ppermute(cells, axis, pairs)  1.49 us
  transfers between devices with their start and end apart: 6, of which 2 were waited for; matrix products, arithmetic and copies ran while one was open for 4% of the time, Pallas kernels for 10%

profile of v6, /device:TPU:3, one launch (start us, length us, event | category | flops | bytes accessed | tf_op | source)
XLA Modules:
  0.0 60.6 jit_solution(16188887611638980464)
XLA Ops:
  0.0 1.0 %copy-done = bf16[16,16,4,256]{3,2,1,0:T(4,128)(2,1)S(1)} copy-done((bf16[16,16,4,256]{3,2,1,0:T(4,128)(2,1)S(1)}, bf16[16,16,4,256]{3,2,1,0:T(4,128)(2,1)}, u32[]{:S(2)}) %copy-start) | copy-done | bytes 524312
  1.0 0.7 %shard_map.55 = (bf16[2,256,256]{2,1,0:T(8,128)(2,1)S(1)}, bf16[2,256,256]{2,1,0:T(8,128)(2,1)S(1)}) custom-call(bf16[256,4,256]{2,1,0:T(4,128)(2,1)S(1)} %bitcast.12), custom_call_target="tpu_custom_call" | custom-call | bytes 1048576 | tf_op jit(solution)/shard_map/pallas_call | solution.py:243
  1.7 5.2 %collective-permute-start = (bf16[2,256,256]{2,1,0:T(8,128)(2,1)S(1)}, bf16[2,256,256]{2,1,0:T(8,128)(2,1)S(1)}, u32[]{:S(2)}, u32[]{:S(2)}) collective-permute-start(bf16[2,256,256]{2,1,0:T(8,128)(2,1)S(1)} %get-tuple-element.17.to_b), channel_id=1, source_target_pairs={{1,2},{2,1},{5,6},{6,5},{9,10},{10,9},{13,14},{14,13},{17,18},{18,... | collective-permute-start | bytes 786440 | tf_op jit(solution)/shard_map/ppermute | solution.py:225
  6.9 1.9 %collective-permute-start.1 = (bf16[2,256,256]{2,1,0:T(8,128)(2,1)S(1)}, bf16[2,256,256]{2,1,0:T(8,128)(2,1)S(1)}, u32[]{:S(2)}, u32[]{:S(2)}) collective-permute-start(bf16[2,256,256]{2,1,0:T(8,128)(2,1)S(1)} %get-tuple-element.18.to_a), channel_id=1, source_target_pairs={{0,1},{1,0},{4,5},{5,4},{8,9},{9,8},{12,13},{13,12},{16,17},{17,16... | collective-permute-start | bytes 786440 | tf_op jit(solution)/shard_map/ppermute | solution.py:225
  8.8 1.1 %copy.8 = bf16[3,3,3,32,32]{4,3,2,1,0:T(8,128)(2,1)S(1)} copy(bf16[3,3,3,32,32]{3,4,2,1,0:T(8,128)(2,1)} %bitcast.16) | data formatting | bytes 110592 | tf_op jit(solution)/shard_map/transpose | solution.py:236
  9.9 1.0 %copy.6 = bf16[3,3,3,16,16]{4,3,2,1,0:T(8,128)(2,1)S(1)} copy(bf16[3,3,3,16,16]{3,4,2,1,0:T(8,128)(2,1)} %bitcast.17) | data formatting | bytes 27648 | tf_op jit(solution)/shard_map/transpose | solution.py:236
  11.0 0.1 copy.7
  11.1 0.0 copy-done.1
  11.1 1.5 %shard_map.56 = (bf16[768,768]{1,0:T(8,128)(2,1)S(1)}, bf16[768,768]{1,0:T(8,128)(2,1)S(1)}, bf16[384,384]{1,0:T(8,128)(2,1)S(1)}, bf16[384,384]{1,0:T(8,128)(2,1)S(1)}) custom-call(bf16[432,16]{1,0:T(8,128)(2,1)S(1)} %bitcast.13, bf16[432,16]{1,0:T(8,128)(2,1)S(1)} %bitcast.14, bf16[432,32]{1,0:T(8,128)(2,1)S(1)} %bitcast.15, bf16[864,32]{1,0:T(8,128)(2,1)S(1)} %bitcast.11), custom_call_target="tpu_custom_call" | custom-call | bytes 4194304 | tf_op jit(solution)/shard_map/pallas_call | solution.py:249
  12.6 0.0 collective-permute-done.from_b
  12.6 3.2 %collective-permute-done.1.from_a = bf16[2,256,256]{2,1,0:T(8,128)(2,1)S(1)} collective-permute-done((bf16[2,256,256]{2,1,0:T(8,128)(2,1)S(1)}, bf16[2,256,256]{2,1,0:T(8,128)(2,1)S(1)}, u32[]{:S(2)}, u32[]{:S(2)}) %collective-permute-start.1) | collective-permute-done | bytes 262176 | tf_op jit(solution)/shard_map/ppermute | solution.py:225
  15.8 6.2 %collective-permute-start.2 = (bf16[4,16,256]{2,1,0:T(8,128)(2,1)S(1)}, bf16[4,16,256]{2,1,0:T(8,128)(2,1)S(1)}, u32[]{:S(2)}, u32[]{:S(2)}) collective-permute-start(bf16[4,16,256]{2,1,0:T(8,128)(2,1)S(1)} %get-tuple-element.20.to_d), channel_id=1, source_target_pairs={{4,8},{8,4},{12,16},{16,12},{20,24},{24,20},{28,32},{32,28},{36,40... | collective-permute-start | bytes 98312 | tf_op jit(solution)/shard_map/ppermute | solution.py:232
  22.1 1.9 %collective-permute-start.3 = (bf16[4,16,256]{2,1,0:T(8,128)(2,1)S(1)}, bf16[4,16,256]{2,1,0:T(8,128)(2,1)S(1)}, u32[]{:S(2)}, u32[]{:S(2)}) collective-permute-start(bf16[4,16,256]{2,1,0:T(8,128)(2,1)S(1)} %get-tuple-element.21.to_c), channel_id=1, source_target_pairs={{0,4},{4,0},{8,12},{12,8},{16,20},{20,16},{24,28},{28,24},{32,36},... | collective-permute-start | bytes 98312 | tf_op jit(solution)/shard_map/ppermute | solution.py:232
  24.0 3.5 %shard_map.58.centre = f32[2,128,128]{2,1,0:T(8,128)S(1)} custom-call(bf16[2,256,256]{2,1,0:T(8,128)(2,1)S(1)} %collective-permute-done.from_b, bf16[2,256,256]{2,1,0:T(8,128)(2,1)S(1)} %collective-permute-done.1.from_a, bf16[2,256,256]{2,1,0:T(8,128)(2,1)S(1)} %get-tuple-element.18.to_a, bf16[2,256,256]{2,1,0:T(8,128)(2,1)S(1)} %get-tuple-element.17.to_b, ...), custom_call_target="tpu_custom_call" | custom-call | flops 3019898880 | bytes 5242880 | tf_op jit(solution)/shard_map/pallas_call | solution.py:262
  27.5 0.0 collective-permute-done.2.from_d
  27.5 0.0 collective-permute-done.3.from_c
  27.5 0.8 %shard_map.59 = bf16[4,2,144,128]{3,2,1,0:T(8,128)(2,1)S(1)} custom-call(bf16[4,16,256]{2,1,0:T(8,128)(2,1)S(1)} %collective-permute-done.2.from_d, bf16[4,16,256]{2,1,0:T(8,128)(2,1)S(1)} %collective-permute-done.3.from_c, bf16[4,16,256]{2,1,0:T(8,128)(2,1)S(1)} %get-tuple-element.21.to_c, bf16[4,16,256]{2,1,0:T(8,128)(2,1)S(1)} %get-tuple-element.20.to_d, ...), custom_call_target="tpu_custom_call" | custom-call | flops 377487360 | bytes 4194304 | tf_op jit(solution)/shard_map/pallas_call | solution.py:269
  28.4 14.8 %all_to_all.5.group = bf16[4,2,144,128]{3,2,1,0:T(8,128)(2,1)S(1)} all-to-all(bf16[4,2,144,128]{3,2,1,0:T(8,128)(2,1)S(1)} %shard_map.59), channel_id=1, replica_groups=mesh['gx'=8,'gy'=16,'dev'=4] {'dev'}, dimensions={0} | all-to-all | bytes 589824 | tf_op jit(solution)/shard_map/all_to_all | solution.py:276
  43.2 11.3 %collective-permute-start.4 = (bf16[2,144,128]{2,1,0:T(8,128)(2,1)S(1)}, bf16[2,144,128]{2,1,0:T(8,128)(2,1)S(1)}, u32[]{:S(2)}, u32[]{:S(2)}) collective-permute-start(bf16[2,144,128]{2,1,0:T(8,128)(2,1)S(1)} %get-tuple-element.24), channel_id=1, source_target_pairs={{64,128},{128,64},{192,256},{256,192},{320,384},{384,320},{65,129}... | collective-permute-start | bytes 221192 | tf_op jit(solution)/shard_map/ppermute | solution.py:232
  54.6 1.9 %collective-permute-start.5 = (bf16[2,144,128]{2,1,0:T(8,128)(2,1)S(1)}, bf16[2,144,128]{2,1,0:T(8,128)(2,1)S(1)}, u32[]{:S(2)}, u32[]{:S(2)}) collective-permute-start(bf16[2,144,128]{2,1,0:T(8,128)(2,1)S(1)} %get-tuple-element.25), channel_id=1, source_target_pairs={{0,64},{64,0},{128,192},{192,128},{256,320},{320,256},{384,448},{4... | collective-permute-start | bytes 221192 | tf_op jit(solution)/shard_map/ppermute | solution.py:232
  56.5 1.0 %shard_map.61 = (bf16[6,144,128]{2,1,0:T(8,128)(2,1)S(1)}, f32[4,64,128]{2,1,0:T(8,128)S(1)}) custom-call(bf16[4,2,144,128]{3,2,1,0:T(8,128)(2,1)S(1)} %all_to_all.5.group, bf16[384,384]{1,0:T(8,128)(2,1)S(1)} %get-tuple-element.19.after.b3, bf16[384,384]{1,0:T(8,128)(2,1)S(1)} %get-tuple-element.26.b4), custom_call_target="tpu_custom_call" | custom-call | flops 424673280 | bytes 1048576 | tf_op jit(solution)/shard_map/pallas_call | solution.py:281
  57.5 1.5 %collective-permute-done.4.from_b = bf16[2,144,128]{2,1,0:T(8,128)(2,1)S(1)} collective-permute-done((bf16[2,144,128]{2,1,0:T(8,128)(2,1)S(1)}, bf16[2,144,128]{2,1,0:T(8,128)(2,1)S(1)}, u32[]{:S(2)}, u32[]{:S(2)}) %collective-permute-start.4) | collective-permute-done | bytes 73760 | tf_op jit(solution)/shard_map/ppermute | solution.py:232
  59.0 0.0 collective-permute-done.5.from_a
  59.0 1.6 %shard_map.62 = bf16[512,128]{1,0:T(8,128)(2,1)} custom-call(bf16[2,144,128]{2,1,0:T(8,128)(2,1)S(1)} %collective-permute-done.4.from_b, bf16[2,144,128]{2,1,0:T(8,128)(2,1)S(1)} %collective-permute-done.5.from_a, bf16[4,2,144,128]{3,2,1,0:T(8,128)(2,1)S(1)} %all_to_all.5.group, bf16[6,144,128]{2,1,0:T(8,128)(2,1)S(1)} %get-tuple-element.27.inner, ...), custom_call_target="tpu_custom_call" | custom-call | flops 339738624 | bytes 1048576 | tf_op jit(solution)/shard_map/pallas_call | solution.py:284
  (6 shorter events, 0.0 us)
Async XLA Ops:
  0.0 1.0 %copy-start = (bf16[16,16,4,256]{3,2,1,0:T(4,128)(2,1)S(1)}, bf16[16,16,4,256]{3,2,1,0:T(4,128)(2,1)}, u32[]{:S(2)}) copy-start(bf16[16,16,4,256]{3,2,1,0:T(4,128)(2,1)} %param.5) | copy-start | bytes 1572868
  1.0 9.9 %copy-start.2 = (bf16[16,16,3,3,3]{1,0,4,3,2:T(8,128)(2,1)S(1)}, bf16[16,16,3,3,3]{1,0,4,3,2:T(8,128)(2,1)}, u32[]{:S(2)}) copy-start(bf16[16,16,3,3,3]{1,0,4,3,2:T(8,128)(2,1)} %param.7) | copy-start | bytes 41476
  1.0 10.0 %copy-start.1 = (bf16[32,16,3,3,3]{0,1,4,3,2:T(8,128)(2,1)S(1)}, bf16[32,16,3,3,3]{0,1,4,3,2:T(8,128)(2,1)}, u32[]{:S(2)}) copy-start(bf16[32,16,3,3,3]{0,1,4,3,2:T(8,128)(2,1)} %param.8) | copy-start | bytes 82948
  1.7 10.9 %collective-permute-start = (bf16[2,256,256]{2,1,0:T(8,128)(2,1)S(1)}, bf16[2,256,256]{2,1,0:T(8,128)(2,1)S(1)}, u32[]{:S(2)}, u32[]{:S(2)}) collective-permute-start(bf16[2,256,256]{2,1,0:T(8,128)(2,1)S(1)} %get-tuple-element.17.to_b), channel_id=1, source_target_pairs={{1,2},{2,1},{5,6},{6,5},{9,10},{10,9},{13,14},{14,13},{17,18},{18,... | collective-permute-start | bytes 786440 | tf_op jit(solution)/shard_map/ppermute | solution.py:225
  6.9 8.9 %collective-permute-start.1 = (bf16[2,256,256]{2,1,0:T(8,128)(2,1)S(1)}, bf16[2,256,256]{2,1,0:T(8,128)(2,1)S(1)}, u32[]{:S(2)}, u32[]{:S(2)}) collective-permute-start(bf16[2,256,256]{2,1,0:T(8,128)(2,1)S(1)} %get-tuple-element.18.to_a), channel_id=1, source_target_pairs={{0,1},{1,0},{4,5},{5,4},{8,9},{9,8},{12,13},{13,12},{16,17},{17,16... | collective-permute-start | bytes 786440 | tf_op jit(solution)/shard_map/ppermute | solution.py:225
  15.8 11.7 %collective-permute-start.2 = (bf16[4,16,256]{2,1,0:T(8,128)(2,1)S(1)}, bf16[4,16,256]{2,1,0:T(8,128)(2,1)S(1)}, u32[]{:S(2)}, u32[]{:S(2)}) collective-permute-start(bf16[4,16,256]{2,1,0:T(8,128)(2,1)S(1)} %get-tuple-element.20.to_d), channel_id=1, source_target_pairs={{4,8},{8,4},{12,16},{16,12},{20,24},{24,20},{28,32},{32,28},{36,40... | collective-permute-start | bytes 98312 | tf_op jit(solution)/shard_map/ppermute | solution.py:232
  22.1 5.5 %collective-permute-start.3 = (bf16[4,16,256]{2,1,0:T(8,128)(2,1)S(1)}, bf16[4,16,256]{2,1,0:T(8,128)(2,1)S(1)}, u32[]{:S(2)}, u32[]{:S(2)}) collective-permute-start(bf16[4,16,256]{2,1,0:T(8,128)(2,1)S(1)} %get-tuple-element.21.to_c), channel_id=1, source_target_pairs={{0,4},{4,0},{8,12},{12,8},{16,20},{20,16},{24,28},{28,24},{32,36},... | collective-permute-start | bytes 98312 | tf_op jit(solution)/shard_map/ppermute | solution.py:232
  43.2 15.7 %collective-permute-start.4 = (bf16[2,144,128]{2,1,0:T(8,128)(2,1)S(1)}, bf16[2,144,128]{2,1,0:T(8,128)(2,1)S(1)}, u32[]{:S(2)}, u32[]{:S(2)}) collective-permute-start(bf16[2,144,128]{2,1,0:T(8,128)(2,1)S(1)} %get-tuple-element.24), channel_id=1, source_target_pairs={{64,128},{128,64},{192,256},{256,192},{320,384},{384,320},{65,129}... | collective-permute-start | bytes 221192 | tf_op jit(solution)/shard_map/ppermute | solution.py:232
  54.6 4.4 %collective-permute-start.5 = (bf16[2,144,128]{2,1,0:T(8,128)(2,1)S(1)}, bf16[2,144,128]{2,1,0:T(8,128)(2,1)S(1)}, u32[]{:S(2)}, u32[]{:S(2)}) collective-permute-start(bf16[2,144,128]{2,1,0:T(8,128)(2,1)S(1)} %get-tuple-element.25), channel_id=1, source_target_pairs={{0,64},{64,0},{128,192},{192,128},{256,320},{320,256},{384,448},{4... | collective-permute-start | bytes 221192 | tf_op jit(solution)/shard_map/ppermute | solution.py:232

commit v7 on v6

--- a/solution.py
+++ b/solution.py
@@ -112,12 +112,26 @@
     return jnp.maximum(wide[pl.ds(0, size // 2, stride=2), :], wide[pl.ds(1, size // 2, stride=2), :])
 
 
-def centre_kernel(from_b, from_a, to_a, to_b, b1, b2, pooled, x, level, wide):
+def early_kernel(to_a, to_b, b1, level):
+    odd = lax.axis_index("dev") % 2
+    for q in range(2):
+        @pl.when(odd == 0)
+        def _():
+            rows = [to_b[q], to_b[1] if q == 0 else to_a[0], to_a[q]]
+            level[q] = taps(rows, b1).astype(BF16)
+
+        @pl.when(odd == 1)
+        def _():
+            rows = [to_a[q], to_a[1] if q == 0 else to_b[0], to_b[q]]
+            level[q] = taps(rows, b1).astype(BF16)
+
+
+def centre_kernel(from_b, from_a, to_a, to_b, early, b1, b2, pooled, x, level, wide):
     tile, last_tile, gy, last_gy = place()
     for at, part in row_parts(from_a, from_b, to_a, to_b):
         x[pl.ds(at, 2)] = part[...]
     for q in range(6):
-        level[q] = taps([x[q], x[q + 1], x[q + 2]], b1).astype(BF16)
+        level[q] = early[q - 2] if q in (2, 3) else taps([x[q], x[q + 1], x[q + 2]], b1).astype(BF16)
 
     @pl.when(tile == 0)
     def _():
@@ -254,8 +268,9 @@
         4 << 20,
     )(by_tap(w_first), by_tap(w_second), by_tap(w_third), by_tap(w_fourth))
 
+    early = call(early_kernel, sds((2, COLS, 256), BF16), [], 2 * 2 * COLS * 768 * 768, 2 << 20)(to_a, to_b, b1)
     to_c, to_d = call(ends_kernel, [ends, ends], [pltpu.VMEM((2, 4, 16, 256), BF16)], 0, 1 << 18)(
-        from_b, from_a, to_a, to_b, b3
+        from_b, from_a, to_a, to_b, early
     )
     from_d = swap(to_d, "gy", 1)
     from_c = swap(to_c, "gy", 0)
@@ -265,7 +280,7 @@
         [pltpu.VMEM((8, COLS, 256), BF16), pltpu.VMEM((6, COLS, 256), BF16), pltpu.VMEM((COLS, 128), F32)],
         2 * 10 * COLS * 768 * 768,
         5 << 20,
-    )(from_b, from_a, to_a, to_b, b1, b2)
+    )(from_b, from_a, to_a, to_b, early, b1, b2)
     group = call(
         strips_kernel,
         sds((4, 2, HALF, 128), BF16),

time: 61 us -> 60.9 us (level)
  the two profiles are of different devices: /device:TPU:3 before, /device:TPU:5 now
where the time goes in v7:
time: 60.9 us; the launch traced here: 60.5 us
  starting transfers between devices  29.1 us (48%)
  blocking collectives  14.8 us (24%)
  Pallas kernels  9.46 us (16%)
  local copies, waits for them, and re-layouts  4.15 us (7%)
  waiting for transfers between devices  2.88 us (5%)
    ppermute x4, starting transfers between devices, swap(): return lax.ppermute(cells, axis, pairs)  22 us
    all_to_all x1, blocking collectives, body(): lax.all_to_all(group, 'dev', split_axis=0, concat_axis=0, tiled=True)  14.8 us
    ppermute x2, starting transfers between devices, swap_rows(): return lax.ppermute(cells, ('gx', 'gy', 'dev'), pairs)  7.12 us
    transpose x3, local copies, waits for them, and re-layouts, by_tap(): jnp.transpose(weight, (2, 3, 4, 1, 0))  3.1 us
    pallas_call x1, Pallas kernels, body(): call(centre_kernel, sds((2, 128, 128), F32), [pltpu.VMEM((8, COLS, 256),...  2.91 us
    pallas_call x1, Pallas kernels, body(): call(outer_kernel, sds((512, 128), BF16), [pltpu.VMEM((4, HALF, 128), BF1...  1.6 us
    ppermute x4, waiting for transfers between devices, swap(): return lax.ppermute(cells, axis, pairs)  1.49 us
    pallas_call x1, Pallas kernels, body(): call(weights_kernel, [sds((768, 768), BF16), sds((768, 768), BF16), sds((...  1.46 us
  transfers between devices with their start and end apart: 6, of which 2 were waited for; matrix products, arithmetic and copies ran while one was open for 5% of the time, Pallas kernels for 10%

profile of v7, /device:TPU:5, one launch (start us, length us, event | category | flops | bytes accessed | tf_op | source)
XLA Modules:
  0.0 60.5 jit_solution(6366784893570651626)
XLA Ops:
  0.0 1.0 %copy-done = bf16[16,16,4,256]{3,2,1,0:T(4,128)(2,1)S(1)} copy-done((bf16[16,16,4,256]{3,2,1,0:T(4,128)(2,1)S(1)}, bf16[16,16,4,256]{3,2,1,0:T(4,128)(2,1)}, u32[]{:S(2)}) %copy-start) | copy-done | bytes 524312
  1.0 0.7 %shard_map.55 = (bf16[2,256,256]{2,1,0:T(8,128)(2,1)S(1)}, bf16[2,256,256]{2,1,0:T(8,128)(2,1)S(1)}) custom-call(bf16[256,4,256]{2,1,0:T(4,128)(2,1)S(1)} %bitcast.12), custom_call_target="tpu_custom_call" | custom-call | bytes 1048576 | tf_op jit(solution)/shard_map/pallas_call | solution.py:257
  1.7 5.2 %collective-permute-start = (bf16[2,256,256]{2,1,0:T(8,128)(2,1)S(1)}, bf16[2,256,256]{2,1,0:T(8,128)(2,1)S(1)}, u32[]{:S(2)}, u32[]{:S(2)}) collective-permute-start(bf16[2,256,256]{2,1,0:T(8,128)(2,1)S(1)} %get-tuple-element.17.to_b), channel_id=1, source_target_pairs={{1,2},{2,1},{5,6},{6,5},{9,10},{10,9},{13,14},{14,13},{17,18},{18,... | collective-permute-start | bytes 786440 | tf_op jit(solution)/shard_map/ppermute | solution.py:239
  6.9 1.9 %collective-permute-start.1 = (bf16[2,256,256]{2,1,0:T(8,128)(2,1)S(1)}, bf16[2,256,256]{2,1,0:T(8,128)(2,1)S(1)}, u32[]{:S(2)}, u32[]{:S(2)}) collective-permute-start(bf16[2,256,256]{2,1,0:T(8,128)(2,1)S(1)} %get-tuple-element.18.to_a), channel_id=1, source_target_pairs={{0,1},{1,0},{4,5},{5,4},{8,9},{9,8},{12,13},{13,12},{16,17},{17,16... | collective-permute-start | bytes 786440 | tf_op jit(solution)/shard_map/ppermute | solution.py:239
  8.8 1.0 %copy.6 = bf16[3,3,3,16,16]{4,3,2,1,0:T(8,128)(2,1)S(1)} copy(bf16[3,3,3,16,16]{3,4,2,1,0:T(8,128)(2,1)} %bitcast.17) | data formatting | bytes 27648 | tf_op jit(solution)/shard_map/transpose | solution.py:250
  9.9 1.0 %copy.7 = bf16[3,3,3,16,16]{4,3,2,1,0:T(8,128)(2,1)S(1)} copy(bf16[3,3,3,16,16]{3,4,2,1,0:T(8,128)(2,1)} %bitcast.18) | data formatting | bytes 27648 | tf_op jit(solution)/shard_map/transpose | solution.py:250
  10.9 1.1 %copy.8 = bf16[3,3,3,32,32]{4,3,2,1,0:T(8,128)(2,1)S(1)} copy(bf16[3,3,3,32,32]{3,4,2,1,0:T(8,128)(2,1)} %bitcast.16) | data formatting | bytes 110592 | tf_op jit(solution)/shard_map/transpose | solution.py:250
  12.0 1.5 %shard_map.56 = (bf16[768,768]{1,0:T(8,128)(2,1)S(1)}, bf16[768,768]{1,0:T(8,128)(2,1)S(1)}, bf16[384,384]{1,0:T(8,128)(2,1)S(1)}, bf16[384,384]{1,0:T(8,128)(2,1)S(1)}) custom-call(bf16[432,16]{1,0:T(8,128)(2,1)S(1)} %bitcast.13, bf16[432,16]{1,0:T(8,128)(2,1)S(1)} %bitcast.14, bf16[432,32]{1,0:T(8,128)(2,1)S(1)} %bitcast.15, bf16[864,32]{1,0:T(8,128)(2,1)S(1)} %bitcast.11), custom_call_target="tpu_custom_call" | custom-call | bytes 4194304 | tf_op jit(solution)/shard_map/pallas_call | solution.py:263
  13.4 1.0 %shard_map.57.after.early = bf16[2,256,256]{2,1,0:T(8,128)(2,1)S(1)} custom-call(bf16[2,256,256]{2,1,0:T(8,128)(2,1)S(1)} %get-tuple-element.18.to_a, bf16[2,256,256]{2,1,0:T(8,128)(2,1)S(1)} %get-tuple-element.17.to_b, bf16[768,768]{1,0:T(8,128)(2,1)S(1)} %get-tuple-element.19.b1), custom_call_target="tpu_custom_call" | custom-call | flops 603979776 | bytes 2097152 | tf_op jit(solution)/shard_map/pallas_call | solution.py:271
  14.4 0.0 collective-permute-done.from_b
  14.4 1.4 %collective-permute-done.1.from_a = bf16[2,256,256]{2,1,0:T(8,128)(2,1)S(1)} collective-permute-done((bf16[2,256,256]{2,1,0:T(8,128)(2,1)S(1)}, bf16[2,256,256]{2,1,0:T(8,128)(2,1)S(1)}, u32[]{:S(2)}, u32[]{:S(2)}) %collective-permute-start.1) | collective-permute-done | bytes 262176 | tf_op jit(solution)/shard_map/ppermute | solution.py:239
  15.8 6.2 %collective-permute-start.2 = (bf16[4,16,256]{2,1,0:T(8,128)(2,1)S(1)}, bf16[4,16,256]{2,1,0:T(8,128)(2,1)S(1)}, u32[]{:S(2)}, u32[]{:S(2)}) collective-permute-start(bf16[4,16,256]{2,1,0:T(8,128)(2,1)S(1)} %get-tuple-element.20.to_d), channel_id=1, source_target_pairs={{4,8},{8,4},{12,16},{16,12},{20,24},{24,20},{28,32},{32,28},{36,40... | collective-permute-start | bytes 98312 | tf_op jit(solution)/shard_map/ppermute | solution.py:246
  22.1 1.9 %collective-permute-start.3 = (bf16[4,16,256]{2,1,0:T(8,128)(2,1)S(1)}, bf16[4,16,256]{2,1,0:T(8,128)(2,1)S(1)}, u32[]{:S(2)}, u32[]{:S(2)}) collective-permute-start(bf16[4,16,256]{2,1,0:T(8,128)(2,1)S(1)} %get-tuple-element.21.to_c), channel_id=1, source_target_pairs={{0,4},{4,0},{8,12},{12,8},{16,20},{20,16},{24,28},{28,24},{32,36},... | collective-permute-start | bytes 98312 | tf_op jit(solution)/shard_map/ppermute | solution.py:246
  24.0 2.9 %shard_map.59.centre = f32[2,128,128]{2,1,0:T(8,128)S(1)} custom-call(bf16[2,256,256]{2,1,0:T(8,128)(2,1)S(1)} %collective-permute-done.from_b, bf16[2,256,256]{2,1,0:T(8,128)(2,1)S(1)} %collective-permute-done.1.from_a, bf16[2,256,256]{2,1,0:T(8,128)(2,1)S(1)} %get-tuple-element.18.to_a, bf16[2,256,256]{2,1,0:T(8,128)(2,1)S(1)} %get-tuple-element.17.to_b, ...), custom_call_target="tpu_custom_call" | custom-call | flops 3019898880 | bytes 5242880 | tf_op jit(solution)/shard_map/pallas_call | solution.py:277
  26.9 0.0 collective-permute-done.2.from_d
  26.9 0.0 collective-permute-done.3.from_c
  26.9 0.8 %shard_map.60 = bf16[4,2,144,128]{3,2,1,0:T(8,128)(2,1)S(1)} custom-call(bf16[4,16,256]{2,1,0:T(8,128)(2,1)S(1)} %collective-permute-done.2.from_d, bf16[4,16,256]{2,1,0:T(8,128)(2,1)S(1)} %collective-permute-done.3.from_c, bf16[4,16,256]{2,1,0:T(8,128)(2,1)S(1)} %get-tuple-element.21.to_c, bf16[4,16,256]{2,1,0:T(8,128)(2,1)S(1)} %get-tuple-element.20.to_d, ...), custom_call_target="tpu_custom_call" | custom-call | flops 377487360 | bytes 4194304 | tf_op jit(solution)/shard_map/pallas_call | solution.py:284
  27.8 14.8 %all_to_all.5.group = bf16[4,2,144,128]{3,2,1,0:T(8,128)(2,1)S(1)} all-to-all(bf16[4,2,144,128]{3,2,1,0:T(8,128)(2,1)S(1)} %shard_map.60), channel_id=1, replica_groups=mesh['gx'=8,'gy'=16,'dev'=4] {'dev'}, dimensions={0} | all-to-all | bytes 589824 | tf_op jit(solution)/shard_map/all_to_all | solution.py:291
  42.6 11.9 %collective-permute-start.4 = (bf16[2,144,128]{2,1,0:T(8,128)(2,1)S(1)}, bf16[2,144,128]{2,1,0:T(8,128)(2,1)S(1)}, u32[]{:S(2)}, u32[]{:S(2)}) collective-permute-start(bf16[2,144,128]{2,1,0:T(8,128)(2,1)S(1)} %get-tuple-element.23), channel_id=1, source_target_pairs={{64,128},{128,64},{192,256},{256,192},{320,384},{384,320},{65,129}... | collective-permute-start | bytes 221192 | tf_op jit(solution)/shard_map/ppermute | solution.py:246
  54.5 1.9 %collective-permute-start.5 = (bf16[2,144,128]{2,1,0:T(8,128)(2,1)S(1)}, bf16[2,144,128]{2,1,0:T(8,128)(2,1)S(1)}, u32[]{:S(2)}, u32[]{:S(2)}) collective-permute-start(bf16[2,144,128]{2,1,0:T(8,128)(2,1)S(1)} %get-tuple-element.24), channel_id=1, source_target_pairs={{0,64},{64,0},{128,192},{192,128},{256,320},{320,256},{384,448},{4... | collective-permute-start | bytes 221192 | tf_op jit(solution)/shard_map/ppermute | solution.py:246
  56.5 1.0 %shard_map.62 = (bf16[6,144,128]{2,1,0:T(8,128)(2,1)S(1)}, f32[4,64,128]{2,1,0:T(8,128)S(1)}) custom-call(bf16[4,2,144,128]{3,2,1,0:T(8,128)(2,1)S(1)} %all_to_all.5.group, bf16[384,384]{1,0:T(8,128)(2,1)S(1)} %get-tuple-element.25.b3, bf16[384,384]{1,0:T(8,128)(2,1)S(1)} %get-tuple-element.26.b4), custom_call_target="tpu_custom_call" | custom-call | flops 424673280 | bytes 1048576 | tf_op jit(solution)/shard_map/pallas_call | solution.py:296
  57.4 1.5 %collective-permute-done.4.from_b = bf16[2,144,128]{2,1,0:T(8,128)(2,1)S(1)} collective-permute-done((bf16[2,144,128]{2,1,0:T(8,128)(2,1)S(1)}, bf16[2,144,128]{2,1,0:T(8,128)(2,1)S(1)}, u32[]{:S(2)}, u32[]{:S(2)}) %collective-permute-start.4) | collective-permute-done | bytes 73760 | tf_op jit(solution)/shard_map/ppermute | solution.py:246
  58.9 0.0 collective-permute-done.5.from_a
  58.9 1.6 %shard_map.63 = bf16[512,128]{1,0:T(8,128)(2,1)} custom-call(bf16[2,144,128]{2,1,0:T(8,128)(2,1)S(1)} %collective-permute-done.4.from_b, bf16[2,144,128]{2,1,0:T(8,128)(2,1)S(1)} %collective-permute-done.5.from_a, bf16[4,2,144,128]{3,2,1,0:T(8,128)(2,1)S(1)} %all_to_all.5.group, bf16[6,144,128]{2,1,0:T(8,128)(2,1)S(1)} %get-tuple-element.27.inner, ...), custom_call_target="tpu_custom_call" | custom-call | flops 339738624 | bytes 1048576 | tf_op jit(solution)/shard_map/pallas_call | solution.py:299
  (5 shorter events, 0.0 us)
Async XLA Ops:
  0.0 1.0 %copy-start = (bf16[16,16,4,256]{3,2,1,0:T(4,128)(2,1)S(1)}, bf16[16,16,4,256]{3,2,1,0:T(4,128)(2,1)}, u32[]{:S(2)}) copy-start(bf16[16,16,4,256]{3,2,1,0:T(4,128)(2,1)} %param.5) | copy-start | bytes 1572868
  1.0 10.9 %copy-start.1 = (bf16[32,16,3,3,3]{0,1,4,3,2:T(8,128)(2,1)S(1)}, bf16[32,16,3,3,3]{0,1,4,3,2:T(8,128)(2,1)}, u32[]{:S(2)}) copy-start(bf16[32,16,3,3,3]{0,1,4,3,2:T(8,128)(2,1)} %param.8) | copy-start | bytes 82948
  1.7 12.7 %collective-permute-start = (bf16[2,256,256]{2,1,0:T(8,128)(2,1)S(1)}, bf16[2,256,256]{2,1,0:T(8,128)(2,1)S(1)}, u32[]{:S(2)}, u32[]{:S(2)}) collective-permute-start(bf16[2,256,256]{2,1,0:T(8,128)(2,1)S(1)} %get-tuple-element.17.to_b), channel_id=1, source_target_pairs={{1,2},{2,1},{5,6},{6,5},{9,10},{10,9},{13,14},{14,13},{17,18},{18,... | collective-permute-start | bytes 786440 | tf_op jit(solution)/shard_map/ppermute | solution.py:239
  6.9 8.9 %collective-permute-start.1 = (bf16[2,256,256]{2,1,0:T(8,128)(2,1)S(1)}, bf16[2,256,256]{2,1,0:T(8,128)(2,1)S(1)}, u32[]{:S(2)}, u32[]{:S(2)}) collective-permute-start(bf16[2,256,256]{2,1,0:T(8,128)(2,1)S(1)} %get-tuple-element.18.to_a), channel_id=1, source_target_pairs={{0,1},{1,0},{4,5},{5,4},{8,9},{9,8},{12,13},{13,12},{16,17},{17,16... | collective-permute-start | bytes 786440 | tf_op jit(solution)/shard_map/ppermute | solution.py:239
  15.8 11.1 %collective-permute-start.2 = (bf16[4,16,256]{2,1,0:T(8,128)(2,1)S(1)}, bf16[4,16,256]{2,1,0:T(8,128)(2,1)S(1)}, u32[]{:S(2)}, u32[]{:S(2)}) collective-permute-start(bf16[4,16,256]{2,1,0:T(8,128)(2,1)S(1)} %get-tuple-element.20.to_d), channel_id=1, source_target_pairs={{4,8},{8,4},{12,16},{16,12},{20,24},{24,20},{28,32},{32,28},{36,40... | collective-permute-start | bytes 98312 | tf_op jit(solution)/shard_map/ppermute | solution.py:246
  22.1 4.9 %collective-permute-start.3 = (bf16[4,16,256]{2,1,0:T(8,128)(2,1)S(1)}, bf16[4,16,256]{2,1,0:T(8,128)(2,1)S(1)}, u32[]{:S(2)}, u32[]{:S(2)}) collective-permute-start(bf16[4,16,256]{2,1,0:T(8,128)(2,1)S(1)} %get-tuple-element.21.to_c), channel_id=1, source_target_pairs={{0,4},{4,0},{8,12},{12,8},{16,20},{20,16},{24,28},{28,24},{32,36},... | collective-permute-start | bytes 98312 | tf_op jit(solution)/shard_map/ppermute | solution.py:246
  42.6 16.3 %collective-permute-start.4 = (bf16[2,144,128]{2,1,0:T(8,128)(2,1)S(1)}, bf16[2,144,128]{2,1,0:T(8,128)(2,1)S(1)}, u32[]{:S(2)}, u32[]{:S(2)}) collective-permute-start(bf16[2,144,128]{2,1,0:T(8,128)(2,1)S(1)} %get-tuple-element.23), channel_id=1, source_target_pairs={{64,128},{128,64},{192,256},{256,192},{320,384},{384,320},{65,129}... | collective-permute-start | bytes 221192 | tf_op jit(solution)/shard_map/ppermute | solution.py:246
  54.5 4.4 %collective-permute-start.5 = (bf16[2,144,128]{2,1,0:T(8,128)(2,1)S(1)}, bf16[2,144,128]{2,1,0:T(8,128)(2,1)S(1)}, u32[]{:S(2)}, u32[]{:S(2)}) collective-permute-start(bf16[2,144,128]{2,1,0:T(8,128)(2,1)S(1)} %get-tuple-element.24), channel_id=1, source_target_pairs={{0,64},{64,0},{128,192},{192,128},{256,320},{320,256},{384,448},{4... | collective-permute-start | bytes 221192 | tf_op jit(solution)/shard_map/ppermute | solution.py:246

commit v8 on v7

--- a/solution.py
+++ b/solution.py
@@ -178,9 +178,7 @@
             jnp.where(row < 6, main[120:128], high),
             jnp.where(gy < last_gy, high, 0.0),
         ]
-        done = jnp.concatenate(parts, axis=0).astype(BF16)
-        for copy in range(4):
-            pooled[copy, pair] = done
+        pooled[pair] = jnp.concatenate(parts, axis=0).astype(BF16)
 
 
 def edges_kernel(group, to_a, to_b):
@@ -281,14 +279,14 @@
         2 * 10 * COLS * 768 * 768,
         5 << 20,
     )(from_b, from_a, to_a, to_b, early, b1, b2)
-    group = call(
+    pooled = call(
         strips_kernel,
-        sds((4, 2, HALF, 128), BF16),
+        sds((2, HALF, 128), BF16),
         [pltpu.VMEM((4, 4, 16, 256), BF16), pltpu.VMEM((32, 128), F32)],
         2 * 320 * 768 * 768,
         4 << 20,
     )(from_d, from_c, to_c, to_d, centre, b1, b2)
-    group = lax.all_to_all(group, "dev", split_axis=0, concat_axis=0, tiled=True)
+    group = lax.all_gather(pooled, "dev")
     edge = sds((2, HALF, 128), BF16)
     to_a, to_b = call(edges_kernel, [edge, edge], [], 0, 1 << 18)(group)
     from_b = swap(to_b, "gx", 1)

time: 60.9 us -> 63.5 us (1.043)
  the two profiles are of different devices: /device:TPU:5 before, /device:TPU:7 now
where the time goes in v8:
time: 63.5 us; the launch traced here: 62.7 us
  starting transfers between devices  31.4 us (49%)
  blocking collectives  15.9 us (25%)
  Pallas kernels  9.47 us (15%)
  local copies, waits for them, and re-layouts  4.15 us (7%)
  waiting for transfers between devices  1.64 us (3%)
    ppermute x4, starting transfers between devices, swap(): return lax.ppermute(cells, axis, pairs)  24.3 us
    all_gather x1, blocking collectives, body(): group = lax.all_gather(pooled, 'dev')  15.9 us
    ppermute x2, starting transfers between devices, swap_rows(): return lax.ppermute(cells, ('gx', 'gy', 'dev'), pairs)  7.12 us
    transpose x3, local copies, waits for them, and re-layouts, by_tap(): jnp.transpose(weight, (2, 3, 4, 1, 0))  3.1 us
    pallas_call x1, Pallas kernels, body(): call(centre_kernel, sds((2, 128, 128), F32), [pltpu.VMEM((8, COLS, 256),...  2.91 us
    pallas_call x1, Pallas kernels, body(): call(outer_kernel, sds((512, 128), BF16), [pltpu.VMEM((4, HALF, 128), BF1...  1.6 us
    pallas_call x1, Pallas kernels, body(): call(weights_kernel, [sds((768, 768), BF16), sds((768, 768), BF16), sds((...  1.46 us
    ppermute x2, waiting for transfers between devices, swap_rows(): return lax.ppermute(cells, ('gx', 'gy', 'dev'), pairs)  1.39 us
  transfers between devices with their start and end apart: 6, of which 2 were waited for; matrix products, arithmetic and copies ran while one was open for 5% of the time, Pallas kernels for 10%

profile of v8, /device:TPU:7, one launch (start us, length us, event | category | flops | bytes accessed | tf_op | source)
XLA Modules:
  0.0 62.7 jit_solution(11958085039285222185)
XLA Ops:
  0.0 1.0 %copy-done = bf16[16,16,4,256]{3,2,1,0:T(4,128)(2,1)S(1)} copy-done((bf16[16,16,4,256]{3,2,1,0:T(4,128)(2,1)S(1)}, bf16[16,16,4,256]{3,2,1,0:T(4,128)(2,1)}, u32[]{:S(2)}) %copy-start) | copy-done | bytes 524312
  1.0 0.7 %shard_map.55 = (bf16[2,256,256]{2,1,0:T(8,128)(2,1)S(1)}, bf16[2,256,256]{2,1,0:T(8,128)(2,1)S(1)}) custom-call(bf16[256,4,256]{2,1,0:T(4,128)(2,1)S(1)} %bitcast.16), custom_call_target="tpu_custom_call" | custom-call | bytes 1048576 | tf_op jit(solution)/shard_map/pallas_call | solution.py:255
  1.7 5.2 %collective-permute-start = (bf16[2,256,256]{2,1,0:T(8,128)(2,1)S(1)}, bf16[2,256,256]{2,1,0:T(8,128)(2,1)S(1)}, u32[]{:S(2)}, u32[]{:S(2)}) collective-permute-start(bf16[2,256,256]{2,1,0:T(8,128)(2,1)S(1)} %get-tuple-element.17.to_b), channel_id=1, source_target_pairs={{1,2},{2,1},{5,6},{6,5},{9,10},{10,9},{13,14},{14,13},{17,18},{18,... | collective-permute-start | bytes 786440 | tf_op jit(solution)/shard_map/ppermute | solution.py:237
  6.9 1.9 %collective-permute-start.1 = (bf16[2,256,256]{2,1,0:T(8,128)(2,1)S(1)}, bf16[2,256,256]{2,1,0:T(8,128)(2,1)S(1)}, u32[]{:S(2)}, u32[]{:S(2)}) collective-permute-start(bf16[2,256,256]{2,1,0:T(8,128)(2,1)S(1)} %get-tuple-element.18.to_a), channel_id=1, source_target_pairs={{0,1},{1,0},{4,5},{5,4},{8,9},{9,8},{12,13},{13,12},{16,17},{17,16... | collective-permute-start | bytes 786440 | tf_op jit(solution)/shard_map/ppermute | solution.py:237
  8.8 1.0 %copy.9 = bf16[3,3,3,16,16]{4,3,2,1,0:T(8,128)(2,1)S(1)} copy(bf16[3,3,3,16,16]{3,4,2,1,0:T(8,128)(2,1)} %bitcast.21) | data formatting | bytes 27648 | tf_op jit(solution)/shard_map/transpose | solution.py:248
  9.9 1.0 %copy.10 = bf16[3,3,3,16,16]{4,3,2,1,0:T(8,128)(2,1)S(1)} copy(bf16[3,3,3,16,16]{3,4,2,1,0:T(8,128)(2,1)} %bitcast.22) | data formatting | bytes 27648 | tf_op jit(solution)/shard_map/transpose | solution.py:248
  10.9 1.1 %copy.11 = bf16[3,3,3,32,32]{4,3,2,1,0:T(8,128)(2,1)S(1)} copy(bf16[3,3,3,32,32]{3,4,2,1,0:T(8,128)(2,1)} %bitcast.20) | data formatting | bytes 110592 | tf_op jit(solution)/shard_map/transpose | solution.py:248
  12.0 1.5 %shard_map.56 = (bf16[768,768]{1,0:T(8,128)(2,1)S(1)}, bf16[768,768]{1,0:T(8,128)(2,1)S(1)}, bf16[384,384]{1,0:T(8,128)(2,1)S(1)}, bf16[384,384]{1,0:T(8,128)(2,1)S(1)}) custom-call(bf16[432,16]{1,0:T(8,128)(2,1)S(1)} %bitcast.17, bf16[432,16]{1,0:T(8,128)(2,1)S(1)} %bitcast.18, bf16[432,32]{1,0:T(8,128)(2,1)S(1)} %bitcast.19, bf16[864,32]{1,0:T(8,128)(2,1)S(1)} %bitcast.15), custom_call_target="tpu_custom_call" | custom-call | bytes 4194304 | tf_op jit(solution)/shard_map/pallas_call | solution.py:261
  13.4 1.0 %shard_map.57.after.early = bf16[2,256,256]{2,1,0:T(8,128)(2,1)S(1)} custom-call(bf16[2,256,256]{2,1,0:T(8,128)(2,1)S(1)} %get-tuple-element.18.to_a, bf16[2,256,256]{2,1,0:T(8,128)(2,1)S(1)} %get-tuple-element.17.to_b, bf16[768,768]{1,0:T(8,128)(2,1)S(1)} %get-tuple-element.19.b1), custom_call_target="tpu_custom_call" | custom-call | flops 603979776 | bytes 2097152 | tf_op jit(solution)/shard_map/pallas_call | solution.py:269
  14.4 0.0 collective-permute-done.from_b
  14.4 1.4 %collective-permute-done.1.from_a = bf16[2,256,256]{2,1,0:T(8,128)(2,1)S(1)} collective-permute-done((bf16[2,256,256]{2,1,0:T(8,128)(2,1)S(1)}, bf16[2,256,256]{2,1,0:T(8,128)(2,1)S(1)}, u32[]{:S(2)}, u32[]{:S(2)}) %collective-permute-start.1) | collective-permute-done | bytes 262176 | tf_op jit(solution)/shard_map/ppermute | solution.py:237
  15.8 6.5 %collective-permute-start.2 = (bf16[4,16,256]{2,1,0:T(8,128)(2,1)S(1)}, bf16[4,16,256]{2,1,0:T(8,128)(2,1)S(1)}, u32[]{:S(2)}, u32[]{:S(2)}) collective-permute-start(bf16[4,16,256]{2,1,0:T(8,128)(2,1)S(1)} %get-tuple-element.20.to_d), channel_id=1, source_target_pairs={{4,8},{8,4},{12,16},{16,12},{20,24},{24,20},{28,32},{32,28},{36,40... | collective-permute-start | bytes 98312 | tf_op jit(solution)/shard_map/ppermute | solution.py:244
  22.4 1.9 %collective-permute-start.3 = (bf16[4,16,256]{2,1,0:T(8,128)(2,1)S(1)}, bf16[4,16,256]{2,1,0:T(8,128)(2,1)S(1)}, u32[]{:S(2)}, u32[]{:S(2)}) collective-permute-start(bf16[4,16,256]{2,1,0:T(8,128)(2,1)S(1)} %get-tuple-element.21.to_c), channel_id=1, source_target_pairs={{0,4},{4,0},{8,12},{12,8},{16,20},{20,16},{24,28},{28,24},{32,36},... | collective-permute-start | bytes 98312 | tf_op jit(solution)/shard_map/ppermute | solution.py:244
  24.3 2.9 %shard_map.59.centre = f32[2,128,128]{2,1,0:T(8,128)S(1)} custom-call(bf16[2,256,256]{2,1,0:T(8,128)(2,1)S(1)} %collective-permute-done.from_b, bf16[2,256,256]{2,1,0:T(8,128)(2,1)S(1)} %collective-permute-done.1.from_a, bf16[2,256,256]{2,1,0:T(8,128)(2,1)S(1)} %get-tuple-element.18.to_a, bf16[2,256,256]{2,1,0:T(8,128)(2,1)S(1)} %get-tuple-element.17.to_b, ...), custom_call_target="tpu_custom_call" | custom-call | flops 3019898880 | bytes 5242880 | tf_op jit(solution)/shard_map/pallas_call | solution.py:275
  27.2 0.0 collective-permute-done.2.from_d
  27.2 0.0 collective-permute-done.3.from_c
  27.2 0.8 %shard_map.60 = bf16[2,144,128]{2,1,0:T(8,128)(2,1)S(1)} custom-call(bf16[4,16,256]{2,1,0:T(8,128)(2,1)S(1)} %collective-permute-done.2.from_d, bf16[4,16,256]{2,1,0:T(8,128)(2,1)S(1)} %collective-permute-done.3.from_c, bf16[4,16,256]{2,1,0:T(8,128)(2,1)S(1)} %get-tuple-element.21.to_c, bf16[4,16,256]{2,1,0:T(8,128)(2,1)S(1)} %get-tuple-element.20.to_d, ...), custom_call_target="tpu_custom_call" | custom-call | flops 377487360 | bytes 4194304 | tf_op jit(solution)/shard_map/pallas_call | solution.py:282
  28.1 15.9 %all-gather = bf16[8,144,128]{2,1,0:T(8,128)(2,1)S(1)} all-gather(bf16[2,144,128]{2,1,0:T(8,128)(2,1)S(1)} %shard_map.60), channel_id=2, replica_groups=mesh['gx'=8,'gy'=16,'dev'=4] {'dev'}, dimensions={0}, use_global_device_ids=true | all-gather | bytes 368640 | tf_op jit(solution)/shard_map/all_gather | solution.py:289
  44.0 13.9 %collective-permute-start.4 = (bf16[2,144,128]{2,1,0:T(8,128)(2,1)S(1)}, bf16[2,144,128]{2,1,0:T(8,128)(2,1)S(1)}, u32[]{:S(2)}, u32[]{:S(2)}) collective-permute-start(bf16[2,144,128]{2,1,0:T(8,128)(2,1)S(1)} %get-tuple-element.23), channel_id=1, source_target_pairs={{64,128},{128,64},{192,256},{256,192},{320,384},{384,320},{65,129}... | collective-permute-start | bytes 221192 | tf_op jit(solution)/shard_map/ppermute | solution.py:244
  58.0 1.9 %collective-permute-start.5 = (bf16[2,144,128]{2,1,0:T(8,128)(2,1)S(1)}, bf16[2,144,128]{2,1,0:T(8,128)(2,1)S(1)}, u32[]{:S(2)}, u32[]{:S(2)}) collective-permute-start(bf16[2,144,128]{2,1,0:T(8,128)(2,1)S(1)} %get-tuple-element.24), channel_id=1, source_target_pairs={{0,64},{64,0},{128,192},{192,128},{256,320},{320,256},{384,448},{4... | collective-permute-start | bytes 221192 | tf_op jit(solution)/shard_map/ppermute | solution.py:244
  59.9 1.0 %shard_map.62 = (bf16[6,144,128]{2,1,0:T(8,128)(2,1)S(1)}, f32[4,64,128]{2,1,0:T(8,128)S(1)}) custom-call(bf16[4,2,144,128]{3,2,1,0:T(8,128)(2,1)S(1)} %bitcast.13, bf16[384,384]{1,0:T(8,128)(2,1)S(1)} %get-tuple-element.25.b3, bf16[384,384]{1,0:T(8,128)(2,1)S(1)} %get-tuple-element.26.b4), custom_call_target="tpu_custom_call" | custom-call | flops 424673280 | bytes 1048576 | tf_op jit(solution)/shard_map/pallas_call | solution.py:294
  60.9 0.0 collective-permute-done.4.from_b
  60.9 0.2 collective-permute-done.5.from_a
  61.1 1.6 %shard_map.63 = bf16[512,128]{1,0:T(8,128)(2,1)} custom-call(bf16[2,144,128]{2,1,0:T(8,128)(2,1)S(1)} %collective-permute-done.4.from_b, bf16[2,144,128]{2,1,0:T(8,128)(2,1)S(1)} %collective-permute-done.5.from_a, bf16[4,2,144,128]{3,2,1,0:T(8,128)(2,1)S(1)} %bitcast.14, bf16[6,144,128]{2,1,0:T(8,128)(2,1)S(1)} %get-tuple-element.27.inner, ...), custom_call_target="tpu_custom_call" | custom-call | flops 339738624 | bytes 1048576 | tf_op jit(solution)/shard_map/pallas_call | solution.py:297
  (5 shorter events, 0.0 us)
Async XLA Ops:
  0.0 1.0 %copy-start = (bf16[16,16,4,256]{3,2,1,0:T(4,128)(2,1)S(1)}, bf16[16,16,4,256]{3,2,1,0:T(4,128)(2,1)}, u32[]{:S(2)}) copy-start(bf16[16,16,4,256]{3,2,1,0:T(4,128)(2,1)} %param.5) | copy-start | bytes 1572868
  1.0 10.9 %copy-start.1 = (bf16[32,16,3,3,3]{0,1,4,3,2:T(8,128)(2,1)S(1)}, bf16[32,16,3,3,3]{0,1,4,3,2:T(8,128)(2,1)}, u32[]{:S(2)}) copy-start(bf16[32,16,3,3,3]{0,1,4,3,2:T(8,128)(2,1)} %param.8) | copy-start | bytes 82948
  1.7 12.7 %collective-permute-start = (bf16[2,256,256]{2,1,0:T(8,128)(2,1)S(1)}, bf16[2,256,256]{2,1,0:T(8,128)(2,1)S(1)}, u32[]{:S(2)}, u32[]{:S(2)}) collective-permute-start(bf16[2,256,256]{2,1,0:T(8,128)(2,1)S(1)} %get-tuple-element.17.to_b), channel_id=1, source_target_pairs={{1,2},{2,1},{5,6},{6,5},{9,10},{10,9},{13,14},{14,13},{17,18},{18,... | collective-permute-start | bytes 786440 | tf_op jit(solution)/shard_map/ppermute | solution.py:237
  6.9 8.9 %collective-permute-start.1 = (bf16[2,256,256]{2,1,0:T(8,128)(2,1)S(1)}, bf16[2,256,256]{2,1,0:T(8,128)(2,1)S(1)}, u32[]{:S(2)}, u32[]{:S(2)}) collective-permute-start(bf16[2,256,256]{2,1,0:T(8,128)(2,1)S(1)} %get-tuple-element.18.to_a), channel_id=1, source_target_pairs={{0,1},{1,0},{4,5},{5,4},{8,9},{9,8},{12,13},{13,12},{16,17},{17,16... | collective-permute-start | bytes 786440 | tf_op jit(solution)/shard_map/ppermute | solution.py:237
  15.8 11.4 %collective-permute-start.2 = (bf16[4,16,256]{2,1,0:T(8,128)(2,1)S(1)}, bf16[4,16,256]{2,1,0:T(8,128)(2,1)S(1)}, u32[]{:S(2)}, u32[]{:S(2)}) collective-permute-start(bf16[4,16,256]{2,1,0:T(8,128)(2,1)S(1)} %get-tuple-element.20.to_d), channel_id=1, source_target_pairs={{4,8},{8,4},{12,16},{16,12},{20,24},{24,20},{28,32},{32,28},{36,40... | collective-permute-start | bytes 98312 | tf_op jit(solution)/shard_map/ppermute | solution.py:244
  22.4 4.9 %collective-permute-start.3 = (bf16[4,16,256]{2,1,0:T(8,128)(2,1)S(1)}, bf16[4,16,256]{2,1,0:T(8,128)(2,1)S(1)}, u32[]{:S(2)}, u32[]{:S(2)}) collective-permute-start(bf16[4,16,256]{2,1,0:T(8,128)(2,1)S(1)} %get-tuple-element.21.to_c), channel_id=1, source_target_pairs={{0,4},{4,0},{8,12},{12,8},{16,20},{20,16},{24,28},{28,24},{32,36},... | collective-permute-start | bytes 98312 | tf_op jit(solution)/shard_map/ppermute | solution.py:244
  44.0 16.9 %collective-permute-start.4 = (bf16[2,144,128]{2,1,0:T(8,128)(2,1)S(1)}, bf16[2,144,128]{2,1,0:T(8,128)(2,1)S(1)}, u32[]{:S(2)}, u32[]{:S(2)}) collective-permute-start(bf16[2,144,128]{2,1,0:T(8,128)(2,1)S(1)} %get-tuple-element.23), channel_id=1, source_target_pairs={{64,128},{128,64},{192,256},{256,192},{320,384},{384,320},{65,129}... | collective-permute-start | bytes 221192 | tf_op jit(solution)/shard_map/ppermute | solution.py:244
  58.0 3.2 %collective-permute-start.5 = (bf16[2,144,128]{2,1,0:T(8,128)(2,1)S(1)}, bf16[2,144,128]{2,1,0:T(8,128)(2,1)S(1)}, u32[]{:S(2)}, u32[]{:S(2)}) collective-permute-start(bf16[2,144,128]{2,1,0:T(8,128)(2,1)S(1)} %get-tuple-element.24), channel_id=1, source_target_pairs={{0,64},{64,0},{128,192},{192,128},{256,320},{320,256},{384,448},{4... | collective-permute-start | bytes 221192 | tf_op jit(solution)/shard_map/ppermute | solution.py:244

commit v9 on v7

--- a/solution.py
+++ b/solution.py
@@ -189,41 +189,50 @@
     to_b[...] = group[3 * odd]
 
 
-def coarse_row(rows, b3, keep):
+def taps_of(triples, band_ref):
+    size = triples[0][0].shape[0]
+    total = taps([jnp.concatenate([triple[k] for triple in triples], axis=0) for k in range(3)], band_ref)
+    return [total[size * at : size * at + size] for at in range(len(triples))]
+
+
+def coarse_rows(triples, b3, keeps):
     gy, last_gy = lax.axis_index("gy"), lax.axis_size("gy") - 1
     col = lax.broadcasted_iota(jnp.int32, (HALF, 128), 0)
-    inside = ((col >= HALO // 2) | (gy > 0)) & ((col < HALF - HALO // 2) | (gy < last_gy)) & keep
-    return jnp.where(inside, taps(rows, b3), 0.0).astype(BF16)
-
-
-def feature_row(rows, b4):
-    features = taps(rows, b4)
-    return jnp.transpose(features[HALO // 2 : HALO // 2 + 128], (1, 0))[:64]
+    inside = ((col >= HALO // 2) | (gy > 0)) & ((col < HALF - HALO // 2) | (gy < last_gy))
+    rows = taps_of(triples, b3)
+    return [jnp.where(inside & keep, row, 0.0).astype(BF16) for row, keep in zip(rows, keeps)]
+
+
+def feature_rows(triples, b4):
+    rows = taps_of(triples, b4)
+    return [jnp.transpose(row[HALO // 2 : HALO // 2 + 128], (1, 0))[:64] for row in rows]
 
 
 def inner_kernel(group, b3, b4, level, turned):
     x = [group[part, r] for part in range(4) for r in range(2)]
-    for q in range(6):
-        level[q] = coarse_row([x[q], x[q + 1], x[q + 2]], b3, True)
+    for half in range(2):
+        rows = coarse_rows([x[q : q + 3] for q in range(3 * half, 3 * half + 3)], b3, [True] * 3)
+        for q in range(3):
+            level[3 * half + q] = rows[q]
+    rows = feature_rows([[level[q], level[q + 1], level[q + 2]] for q in range(4)], b4)
     for q in range(4):
-        turned[q] = feature_row([level[q], level[q + 1], level[q + 2]], b4)
-
-
-def outer_kernel(from_b, from_a, group, inner, turned, b3, b4, out, x, level, wide):
-    gx = lax.axis_index("gx")
+        turned[q] = rows[q]
+
+
+def outer_kernel(from_b, from_a, group, inner, turned, b3, b4, out, x, wide):
+    gx, last_gx = lax.axis_index("gx"), lax.axis_size("gx") - 1
     odd = gx % 2
     x[pl.ds(2 - 2 * odd, 2)] = from_a[...]
     x[pl.ds(2 * odd, 2)] = from_b[...]
     above = [x[0], x[1], group[0, 0], group[0, 1]]
     below = [group[3, 0], group[3, 1], x[2], x[3]]
-    for q in range(2):
-        level[q] = coarse_row(above[q : q + 3], b3, (gx > 0) | (q > 0))
-        level[2 + q] = coarse_row(below[q : q + 3], b3, (gx < lax.axis_size("gx") - 1) | (q < 1))
+    triples = [above[0:3], above[1:4], below[0:3], below[1:4]]
+    level = coarse_rows(triples, b3, [gx > 0, True, True, gx < last_gx])
     above = [level[0], level[1], inner[0], inner[1]]
     below = [inner[4], inner[5], level[2], level[3]]
-    for q in range(2):
-        wide[pl.ds(q, 64, stride=8), :] = feature_row(above[q : q + 3], b4)
-        wide[pl.ds(6 + q, 64, stride=8), :] = feature_row(below[q : q + 3], b4)
+    rows = feature_rows([above[0:3], above[1:4], below[0:3], below[1:4]], b4)
+    for row, at in zip(rows, (0, 1, 6, 7)):
+        wide[pl.ds(at, 64, stride=8), :] = row
     for q in range(4):
         wide[pl.ds(2 + q, 64, stride=8), :] = turned[q]
     out[...] = wide[...].astype(BF16)
@@ -299,7 +308,7 @@
     out = call(
         outer_kernel,
         sds((512, 128), BF16),
-        [pltpu.VMEM((4, HALF, 128), BF16), pltpu.VMEM((4, HALF, 128), BF16), pltpu.VMEM((512, 128), F32)],
+        [pltpu.VMEM((4, HALF, 128), BF16), pltpu.VMEM((512, 128), F32)],
         2 * 8 * HALF * 384 * 384,
         1 << 20,
     )(from_b, from_a, group, inner, turned, b3, b4)

time: 60.9 us -> 61 us (level)
  no operation moved by 1% of the time
where the time goes in v9:
time: 61 us; the launch traced here: 60.6 us
  starting transfers between devices  29.1 us (48%)
  blocking collectives  14.8 us (24%)
  Pallas kernels  9.51 us (16%)
  local copies, waits for them, and re-layouts  4.15 us (7%)
  waiting for transfers between devices  2.88 us (5%)
    ppermute x4, starting transfers between devices, swap(): return lax.ppermute(cells, axis, pairs)  22 us
    all_to_all x1, blocking collectives, body(): lax.all_to_all(group, 'dev', split_axis=0, concat_axis=0, tiled=True)  14.8 us
    ppermute x2, starting transfers between devices, swap_rows(): return lax.ppermute(cells, ('gx', 'gy', 'dev'), pairs)  7.12 us
    transpose x3, local copies, waits for them, and re-layouts, by_tap(): jnp.transpose(weight, (2, 3, 4, 1, 0))  3.1 us
    pallas_call x1, Pallas kernels, body(): call(centre_kernel, sds((2, 128, 128), F32), [pltpu.VMEM((8, COLS, 256),...  2.91 us
    pallas_call x1, Pallas kernels, body(): call(outer_kernel, sds((512, 128), BF16), [pltpu.VMEM((4, HALF, 128), BF1...  1.64 us
    ppermute x4, waiting for transfers between devices, swap(): return lax.ppermute(cells, axis, pairs)  1.49 us
    pallas_call x1, Pallas kernels, body(): call(weights_kernel, [sds((768, 768), BF16), sds((768, 768), BF16), sds((...  1.46 us
  transfers between devices with their start and end apart: 6, of which 2 were waited for; matrix products, arithmetic and copies ran while one was open for 5% of the time, Pallas kernels for 10%

profile of v9, /device:TPU:5, one launch (start us, length us, event | category | flops | bytes accessed | tf_op | source)
XLA Modules:
  0.0 60.6 jit_solution(16105942531459388313)
XLA Ops:
  0.0 1.0 %copy-done = bf16[16,16,4,256]{3,2,1,0:T(4,128)(2,1)S(1)} copy-done((bf16[16,16,4,256]{3,2,1,0:T(4,128)(2,1)S(1)}, bf16[16,16,4,256]{3,2,1,0:T(4,128)(2,1)}, u32[]{:S(2)}) %copy-start) | copy-done | bytes 524312
  1.0 0.7 %shard_map.55 = (bf16[2,256,256]{2,1,0:T(8,128)(2,1)S(1)}, bf16[2,256,256]{2,1,0:T(8,128)(2,1)S(1)}) custom-call(bf16[256,4,256]{2,1,0:T(4,128)(2,1)S(1)} %bitcast.12), custom_call_target="tpu_custom_call" | custom-call | bytes 1048576 | tf_op jit(solution)/shard_map/pallas_call | solution.py:266
  1.7 5.2 %collective-permute-start = (bf16[2,256,256]{2,1,0:T(8,128)(2,1)S(1)}, bf16[2,256,256]{2,1,0:T(8,128)(2,1)S(1)}, u32[]{:S(2)}, u32[]{:S(2)}) collective-permute-start(bf16[2,256,256]{2,1,0:T(8,128)(2,1)S(1)} %get-tuple-element.17.to_b), channel_id=1, source_target_pairs={{1,2},{2,1},{5,6},{6,5},{9,10},{10,9},{13,14},{14,13},{17,18},{18,... | collective-permute-start | bytes 786440 | tf_op jit(solution)/shard_map/ppermute | solution.py:248
  6.9 1.9 %collective-permute-start.1 = (bf16[2,256,256]{2,1,0:T(8,128)(2,1)S(1)}, bf16[2,256,256]{2,1,0:T(8,128)(2,1)S(1)}, u32[]{:S(2)}, u32[]{:S(2)}) collective-permute-start(bf16[2,256,256]{2,1,0:T(8,128)(2,1)S(1)} %get-tuple-element.18.to_a), channel_id=1, source_target_pairs={{0,1},{1,0},{4,5},{5,4},{8,9},{9,8},{12,13},{13,12},{16,17},{17,16... | collective-permute-start | bytes 786440 | tf_op jit(solution)/shard_map/ppermute | solution.py:248
  8.8 1.0 %copy.6 = bf16[3,3,3,16,16]{4,3,2,1,0:T(8,128)(2,1)S(1)} copy(bf16[3,3,3,16,16]{3,4,2,1,0:T(8,128)(2,1)} %bitcast.17) | data formatting | bytes 27648 | tf_op jit(solution)/shard_map/transpose | solution.py:259
  9.9 1.0 %copy.7 = bf16[3,3,3,16,16]{4,3,2,1,0:T(8,128)(2,1)S(1)} copy(bf16[3,3,3,16,16]{3,4,2,1,0:T(8,128)(2,1)} %bitcast.18) | data formatting | bytes 27648 | tf_op jit(solution)/shard_map/transpose | solution.py:259
  10.9 1.1 %copy.8 = bf16[3,3,3,32,32]{4,3,2,1,0:T(8,128)(2,1)S(1)} copy(bf16[3,3,3,32,32]{3,4,2,1,0:T(8,128)(2,1)} %bitcast.16) | data formatting | bytes 110592 | tf_op jit(solution)/shard_map/transpose | solution.py:259
  12.0 1.5 %shard_map.56 = (bf16[768,768]{1,0:T(8,128)(2,1)S(1)}, bf16[768,768]{1,0:T(8,128)(2,1)S(1)}, bf16[384,384]{1,0:T(8,128)(2,1)S(1)}, bf16[384,384]{1,0:T(8,128)(2,1)S(1)}) custom-call(bf16[432,16]{1,0:T(8,128)(2,1)S(1)} %bitcast.13, bf16[432,16]{1,0:T(8,128)(2,1)S(1)} %bitcast.14, bf16[432,32]{1,0:T(8,128)(2,1)S(1)} %bitcast.15, bf16[864,32]{1,0:T(8,128)(2,1)S(1)} %bitcast.11), custom_call_target="tpu_custom_call" | custom-call | bytes 4194304 | tf_op jit(solution)/shard_map/pallas_call | solution.py:272
  13.4 1.0 %shard_map.57.after.early = bf16[2,256,256]{2,1,0:T(8,128)(2,1)S(1)} custom-call(bf16[2,256,256]{2,1,0:T(8,128)(2,1)S(1)} %get-tuple-element.18.to_a, bf16[2,256,256]{2,1,0:T(8,128)(2,1)S(1)} %get-tuple-element.17.to_b, bf16[768,768]{1,0:T(8,128)(2,1)S(1)} %get-tuple-element.19.b1), custom_call_target="tpu_custom_call" | custom-call | flops 603979776 | bytes 2097152 | tf_op jit(solution)/shard_map/pallas_call | solution.py:280
  14.4 0.0 collective-permute-done.from_b
  14.4 1.4 %collective-permute-done.1.from_a = bf16[2,256,256]{2,1,0:T(8,128)(2,1)S(1)} collective-permute-done((bf16[2,256,256]{2,1,0:T(8,128)(2,1)S(1)}, bf16[2,256,256]{2,1,0:T(8,128)(2,1)S(1)}, u32[]{:S(2)}, u32[]{:S(2)}) %collective-permute-start.1) | collective-permute-done | bytes 262176 | tf_op jit(solution)/shard_map/ppermute | solution.py:248
  15.8 6.2 %collective-permute-start.2 = (bf16[4,16,256]{2,1,0:T(8,128)(2,1)S(1)}, bf16[4,16,256]{2,1,0:T(8,128)(2,1)S(1)}, u32[]{:S(2)}, u32[]{:S(2)}) collective-permute-start(bf16[4,16,256]{2,1,0:T(8,128)(2,1)S(1)} %get-tuple-element.20.to_d), channel_id=1, source_target_pairs={{4,8},{8,4},{12,16},{16,12},{20,24},{24,20},{28,32},{32,28},{36,40... | collective-permute-start | bytes 98312 | tf_op jit(solution)/shard_map/ppermute | solution.py:255
  22.1 1.9 %collective-permute-start.3 = (bf16[4,16,256]{2,1,0:T(8,128)(2,1)S(1)}, bf16[4,16,256]{2,1,0:T(8,128)(2,1)S(1)}, u32[]{:S(2)}, u32[]{:S(2)}) collective-permute-start(bf16[4,16,256]{2,1,0:T(8,128)(2,1)S(1)} %get-tuple-element.21.to_c), channel_id=1, source_target_pairs={{0,4},{4,0},{8,12},{12,8},{16,20},{20,16},{24,28},{28,24},{32,36},... | collective-permute-start | bytes 98312 | tf_op jit(solution)/shard_map/ppermute | solution.py:255
  24.0 2.9 %shard_map.59.centre = f32[2,128,128]{2,1,0:T(8,128)S(1)} custom-call(bf16[2,256,256]{2,1,0:T(8,128)(2,1)S(1)} %collective-permute-done.from_b, bf16[2,256,256]{2,1,0:T(8,128)(2,1)S(1)} %collective-permute-done.1.from_a, bf16[2,256,256]{2,1,0:T(8,128)(2,1)S(1)} %get-tuple-element.18.to_a, bf16[2,256,256]{2,1,0:T(8,128)(2,1)S(1)} %get-tuple-element.17.to_b, ...), custom_call_target="tpu_custom_call" | custom-call | flops 3019898880 | bytes 5242880 | tf_op jit(solution)/shard_map/pallas_call | solution.py:286
  26.9 0.0 collective-permute-done.2.from_d
  26.9 0.0 collective-permute-done.3.from_c
  26.9 0.8 %shard_map.60 = bf16[4,2,144,128]{3,2,1,0:T(8,128)(2,1)S(1)} custom-call(bf16[4,16,256]{2,1,0:T(8,128)(2,1)S(1)} %collective-permute-done.2.from_d, bf16[4,16,256]{2,1,0:T(8,128)(2,1)S(1)} %collective-permute-done.3.from_c, bf16[4,16,256]{2,1,0:T(8,128)(2,1)S(1)} %get-tuple-element.21.to_c, bf16[4,16,256]{2,1,0:T(8,128)(2,1)S(1)} %get-tuple-element.20.to_d, ...), custom_call_target="tpu_custom_call" | custom-call | flops 377487360 | bytes 4194304 | tf_op jit(solution)/shard_map/pallas_call | solution.py:293
  27.8 14.8 %all_to_all.5.group = bf16[4,2,144,128]{3,2,1,0:T(8,128)(2,1)S(1)} all-to-all(bf16[4,2,144,128]{3,2,1,0:T(8,128)(2,1)S(1)} %shard_map.60), channel_id=1, replica_groups=mesh['gx'=8,'gy'=16,'dev'=4] {'dev'}, dimensions={0} | all-to-all | bytes 589824 | tf_op jit(solution)/shard_map/all_to_all | solution.py:300
  42.6 11.9 %collective-permute-start.4 = (bf16[2,144,128]{2,1,0:T(8,128)(2,1)S(1)}, bf16[2,144,128]{2,1,0:T(8,128)(2,1)S(1)}, u32[]{:S(2)}, u32[]{:S(2)}) collective-permute-start(bf16[2,144,128]{2,1,0:T(8,128)(2,1)S(1)} %get-tuple-element.23), channel_id=1, source_target_pairs={{64,128},{128,64},{192,256},{256,192},{320,384},{384,320},{65,129}... | collective-permute-start | bytes 221192 | tf_op jit(solution)/shard_map/ppermute | solution.py:255
  54.5 1.9 %collective-permute-start.5 = (bf16[2,144,128]{2,1,0:T(8,128)(2,1)S(1)}, bf16[2,144,128]{2,1,0:T(8,128)(2,1)S(1)}, u32[]{:S(2)}, u32[]{:S(2)}) collective-permute-start(bf16[2,144,128]{2,1,0:T(8,128)(2,1)S(1)} %get-tuple-element.24), channel_id=1, source_target_pairs={{0,64},{64,0},{128,192},{192,128},{256,320},{320,256},{384,448},{4... | collective-permute-start | bytes 221192 | tf_op jit(solution)/shard_map/ppermute | solution.py:255
  56.5 1.0 %shard_map.62 = (bf16[6,144,128]{2,1,0:T(8,128)(2,1)S(1)}, f32[4,64,128]{2,1,0:T(8,128)S(1)}) custom-call(bf16[4,2,144,128]{3,2,1,0:T(8,128)(2,1)S(1)} %all_to_all.5.group, bf16[384,384]{1,0:T(8,128)(2,1)S(1)} %get-tuple-element.25.b3, bf16[384,384]{1,0:T(8,128)(2,1)S(1)} %get-tuple-element.26.b4), custom_call_target="tpu_custom_call" | custom-call | flops 424673280 | bytes 1048576 | tf_op jit(solution)/shard_map/pallas_call | solution.py:305
  57.5 1.5 %collective-permute-done.4.from_b = bf16[2,144,128]{2,1,0:T(8,128)(2,1)S(1)} collective-permute-done((bf16[2,144,128]{2,1,0:T(8,128)(2,1)S(1)}, bf16[2,144,128]{2,1,0:T(8,128)(2,1)S(1)}, u32[]{:S(2)}, u32[]{:S(2)}) %collective-permute-start.4) | collective-permute-done | bytes 73760 | tf_op jit(solution)/shard_map/ppermute | solution.py:255
  58.9 0.0 collective-permute-done.5.from_a
  58.9 1.6 %shard_map.63 = bf16[512,128]{1,0:T(8,128)(2,1)} custom-call(bf16[2,144,128]{2,1,0:T(8,128)(2,1)S(1)} %collective-permute-done.4.from_b, bf16[2,144,128]{2,1,0:T(8,128)(2,1)S(1)} %collective-permute-done.5.from_a, bf16[4,2,144,128]{3,2,1,0:T(8,128)(2,1)S(1)} %all_to_all.5.group, bf16[6,144,128]{2,1,0:T(8,128)(2,1)S(1)} %get-tuple-element.27.inner, ...), custom_call_target="tpu_custom_call" | custom-call | flops 339738624 | bytes 1048576 | tf_op jit(solution)/shard_map/pallas_call | solution.py:308
  (5 shorter events, 0.0 us)
Async XLA Ops:
  0.0 1.0 %copy-start = (bf16[16,16,4,256]{3,2,1,0:T(4,128)(2,1)S(1)}, bf16[16,16,4,256]{3,2,1,0:T(4,128)(2,1)}, u32[]{:S(2)}) copy-start(bf16[16,16,4,256]{3,2,1,0:T(4,128)(2,1)} %param.5) | copy-start | bytes 1572868
  1.0 10.9 %copy-start.1 = (bf16[32,16,3,3,3]{0,1,4,3,2:T(8,128)(2,1)S(1)}, bf16[32,16,3,3,3]{0,1,4,3,2:T(8,128)(2,1)}, u32[]{:S(2)}) copy-start(bf16[32,16,3,3,3]{0,1,4,3,2:T(8,128)(2,1)} %param.8) | copy-start | bytes 82948
  1.7 12.7 %collective-permute-start = (bf16[2,256,256]{2,1,0:T(8,128)(2,1)S(1)}, bf16[2,256,256]{2,1,0:T(8,128)(2,1)S(1)}, u32[]{:S(2)}, u32[]{:S(2)}) collective-permute-start(bf16[2,256,256]{2,1,0:T(8,128)(2,1)S(1)} %get-tuple-element.17.to_b), channel_id=1, source_target_pairs={{1,2},{2,1},{5,6},{6,5},{9,10},{10,9},{13,14},{14,13},{17,18},{18,... | collective-permute-start | bytes 786440 | tf_op jit(solution)/shard_map/ppermute | solution.py:248
  6.9 8.9 %collective-permute-start.1 = (bf16[2,256,256]{2,1,0:T(8,128)(2,1)S(1)}, bf16[2,256,256]{2,1,0:T(8,128)(2,1)S(1)}, u32[]{:S(2)}, u32[]{:S(2)}) collective-permute-start(bf16[2,256,256]{2,1,0:T(8,128)(2,1)S(1)} %get-tuple-element.18.to_a), channel_id=1, source_target_pairs={{0,1},{1,0},{4,5},{5,4},{8,9},{9,8},{12,13},{13,12},{16,17},{17,16... | collective-permute-start | bytes 786440 | tf_op jit(solution)/shard_map/ppermute | solution.py:248
  15.8 11.1 %collective-permute-start.2 = (bf16[4,16,256]{2,1,0:T(8,128)(2,1)S(1)}, bf16[4,16,256]{2,1,0:T(8,128)(2,1)S(1)}, u32[]{:S(2)}, u32[]{:S(2)}) collective-permute-start(bf16[4,16,256]{2,1,0:T(8,128)(2,1)S(1)} %get-tuple-element.20.to_d), channel_id=1, source_target_pairs={{4,8},{8,4},{12,16},{16,12},{20,24},{24,20},{28,32},{32,28},{36,40... | collective-permute-start | bytes 98312 | tf_op jit(solution)/shard_map/ppermute | solution.py:255
  22.1 4.9 %collective-permute-start.3 = (bf16[4,16,256]{2,1,0:T(8,128)(2,1)S(1)}, bf16[4,16,256]{2,1,0:T(8,128)(2,1)S(1)}, u32[]{:S(2)}, u32[]{:S(2)}) collective-permute-start(bf16[4,16,256]{2,1,0:T(8,128)(2,1)S(1)} %get-tuple-element.21.to_c), channel_id=1, source_target_pairs={{0,4},{4,0},{8,12},{12,8},{16,20},{20,16},{24,28},{28,24},{32,36},... | collective-permute-start | bytes 98312 | tf_op jit(solution)/shard_map/ppermute | solution.py:255
  42.6 16.3 %collective-permute-start.4 = (bf16[2,144,128]{2,1,0:T(8,128)(2,1)S(1)}, bf16[2,144,128]{2,1,0:T(8,128)(2,1)S(1)}, u32[]{:S(2)}, u32[]{:S(2)}) collective-permute-start(bf16[2,144,128]{2,1,0:T(8,128)(2,1)S(1)} %get-tuple-element.23), channel_id=1, source_target_pairs={{64,128},{128,64},{192,256},{256,192},{320,384},{384,320},{65,129}... | collective-permute-start | bytes 221192 | tf_op jit(solution)/shard_map/ppermute | solution.py:255
  54.5 4.4 %collective-permute-start.5 = (bf16[2,144,128]{2,1,0:T(8,128)(2,1)S(1)}, bf16[2,144,128]{2,1,0:T(8,128)(2,1)S(1)}, u32[]{:S(2)}, u32[]{:S(2)}) collective-permute-start(bf16[2,144,128]{2,1,0:T(8,128)(2,1)S(1)} %get-tuple-element.24), channel_id=1, source_target_pairs={{0,64},{64,0},{128,192},{192,128},{256,320},{320,256},{384,448},{4... | collective-permute-start | bytes 221192 | tf_op jit(solution)/shard_map/ppermute | solution.py:255
